TPU v7x, 32 devices: a whole 2x2x4 slice. The times are simulated.
32 devices in a mesh: dp: 4 (over y, x), fsdp: 8 (over z, core).
Axes of the slice: x: 2, y: 2, z: 4, core: 2. Of those that a mesh axis runs over, the one named last changes fastest.
Arguments:
- tokens: bfloat16 [5120, 2048], P(('dp', 'fsdp')), may hold values from -6 to 6
- cotangent: bfloat16 [5120, 2048], P(('dp', 'fsdp')), may hold values from -6 to 6
- lengths: int32 [4], P('dp'), may hold values from 320 to 1280, as said below
- norm_attn: bfloat16 [2048], P(('dp', 'fsdp')), may hold values from 0.5 to 1.5
- w_query: bfloat16 [2048, 2048], P(('dp', 'fsdp')), may hold values from -0.125 to 0.125
- w_key: bfloat16 [2048, 2048], P(('dp', 'fsdp')), may hold values from -0.125 to 0.125
- w_value: bfloat16 [2048, 2048], P(('dp', 'fsdp')), may hold values from -0.125 to 0.125
- w_output: bfloat16 [2048, 2048], P(('dp', 'fsdp')), may hold values from -2 to 2
- norm_mlp: bfloat16 [2048], P(('dp', 'fsdp')), may hold values from 0.5 to 1.5
- w_gate: bfloat16 [2048, 8192], P(('dp', 'fsdp')), may hold values from -0.125 to 0.125
- w_up: bfloat16 [2048, 8192], P(('dp', 'fsdp')), may hold values from -0.125 to 0.125
- w_down: bfloat16 [8192, 2048], P(('dp', 'fsdp')), may hold values from -0.0625 to 0.0625
Outputs:
- output: bfloat16 [5120, 2048], P(('dp', 'fsdp'))
- grad_tokens: bfloat16 [5120, 2048], P(('dp', 'fsdp'))
- grad_norm_attn: float32 [2048], P(('dp', 'fsdp'))
- grad_w_query: float32 [2048, 2048], P(('dp', 'fsdp'))
- grad_w_key: float32 [2048, 2048], P(('dp', 'fsdp'))
- grad_w_value: float32 [2048, 2048], P(('dp', 'fsdp'))
- grad_w_output: float32 [2048, 2048], P(('dp', 'fsdp'))
- grad_norm_mlp: float32 [2048], P(('dp', 'fsdp'))
- grad_w_gate: float32 [2048, 8192], P(('dp', 'fsdp'))
- grad_w_up: float32 [2048, 8192], P(('dp', 'fsdp'))
- grad_w_down: float32 [8192, 2048], P(('dp', 'fsdp'))
Inputs may be any that keep to these rules, and one draw needn't show every extreme that they name: `lengths`: one sequence, drawn from the seed, has all 1280 positions live.
All inputs are finite; a program needn't handle non-finite values.
Results may differ from a plain program's by a relative error of at most 0.017.
Values may be sent and summed in bfloat16 or wider, within the bound.
A program may use at most 512 MiB of HBM per device.

v0:
```python
import math

import jax
import jax.numpy as jnp
from jax import lax
from jax.sharding import PartitionSpec as P

HEADS = 32
HEAD_DIM = 64


EPSILON = 1e-05
THETA = 130000.0


def rotary(values, positions):
    half = HEAD_DIM // 2
    inverse = THETA ** (-jnp.arange(half, dtype=jnp.float32) * 2.0 / HEAD_DIM)
    angles = positions[:, None] * inverse[None, :]
    cosine = jnp.cos(angles)[:, None, :]
    sine = jnp.sin(angles)[:, None, :]
    shaped = values.reshape(values.shape[0], HEADS, HEAD_DIM)
    first_half = shaped[..., :half]
    second_half = shaped[..., half:]
    turned = jnp.concatenate(
        [first_half * cosine - second_half * sine, second_half * cosine + first_half * sine], -1
    )
    return turned.reshape(values.shape)


def norm_scale(values):
    return values * lax.rsqrt(jnp.mean(values * values, -1, keepdims=True) + EPSILON)


def split_heads(values, block):
    return values.reshape(values.shape[0], HEADS // block, block, HEAD_DIM).transpose(1, 2, 0, 3)


def join_heads(values):
    groups, block, count, width = values.shape
    return values.transpose(2, 0, 1, 3).reshape(count, groups * block * width)


def rows_inner(left, right):
    return lax.dot_general(
        left, right, (((0,), (0,)), ((), ())), preferred_element_type=jnp.float32
    )


def cols_inner(left, right):
    return lax.dot_general(
        left, right, (((1,), (1,)), ((), ())), preferred_element_type=jnp.float32
    )


def masked_scores(query_part, key_part, allowed):
    scores = (
        jnp.einsum("hqd,hkd->hqk", query_part, key_part, preferred_element_type=jnp.float32) * 0.125
    )
    return jnp.where(allowed[None], scores, -1000000000.0)


def attend_local(queries_b, keys_all, values_all, allowed):
    block = math.gcd(4, HEADS)

    def head_block(parts):
        query_part, key_part, value_part = parts
        scores = masked_scores(query_part, key_part, allowed)
        row_max = jnp.max(scores, -1, keepdims=True)
        log_total = row_max + jnp.log(jnp.sum(jnp.exp(scores - row_max), -1, keepdims=True))
        weights = jnp.exp(scores - log_total).astype(jnp.bfloat16)
        result = jnp.einsum("hqk,hkd->hqd", weights, value_part, preferred_element_type=jnp.float32)
        return (result, log_total[..., 0])

    results, totals = lax.map(
        head_block,
        (
            split_heads(queries_b, block),
            split_heads(keys_all, block),
            split_heads(values_all, block),
        ),
    )
    return (join_heads(results), totals)


def attend_back(queries_b, keys_all, values_all, grad_b, totals, allowed):
    block = math.gcd(4, HEADS)

    def head_block(parts):
        query_part, key_part, value_part, grad_part, total_part = parts
        scores = masked_scores(query_part, key_part, allowed)
        weights = jnp.exp(scores - total_part[..., None])
        weights_b = weights.astype(jnp.bfloat16)
        grad_weights = jnp.einsum(
            "hqd,hkd->hqk", grad_part, value_part, preferred_element_type=jnp.float32
        )
        grad_scores = (
            weights * (grad_weights - jnp.sum(weights * grad_weights, -1, keepdims=True))
        ).astype(jnp.bfloat16)
        grad_query = 0.125 * jnp.einsum(
            "hqk,hkd->hqd", grad_scores, key_part, preferred_element_type=jnp.float32
        )
        grad_key = 0.125 * jnp.einsum(
            "hqk,hqd->hkd", grad_scores, query_part, preferred_element_type=jnp.float32
        )
        grad_value = jnp.einsum(
            "hqk,hqd->hkd", weights_b, grad_part, preferred_element_type=jnp.float32
        )
        return (grad_query, grad_key, grad_value)

    grad_query, grad_key, grad_value = lax.map(
        head_block,
        (
            split_heads(queries_b, block),
            split_heads(keys_all, block),
            split_heads(values_all, block),
            split_heads(grad_b, block),
            totals,
        ),
    )
    return (join_heads(grad_query), join_heads(grad_key), join_heads(grad_value))


def forward_pass(
    tokens, lengths, norm_attn, w_query, w_key, w_value, w_output, norm_mlp, w_gate, w_up, w_down
):
    count_rows = tokens.shape[0]
    query_places = lax.axis_index("fsdp") * count_rows + jnp.arange(count_rows, dtype=jnp.int32)
    positions = query_places.astype(jnp.float32)
    tokens_f = tokens.astype(jnp.float32)
    scaled_one = norm_scale(tokens_f)
    gain_piece = lax.all_gather(norm_attn, ("dp", "fsdp"), axis=0, tiled=True)
    query_piece = lax.all_gather(w_query, ("dp", "fsdp"), axis=0, tiled=True)
    key_piece = lax.all_gather(w_key, ("dp", "fsdp"), axis=0, tiled=True)
    value_piece = lax.all_gather(w_value, ("dp", "fsdp"), axis=0, tiled=True)
    normed_cols = (scaled_one * gain_piece.astype(jnp.float32)).astype(jnp.bfloat16)
    query_lin = jnp.dot(normed_cols, query_piece, preferred_element_type=jnp.float32)
    key_lin = jnp.dot(normed_cols, key_piece, preferred_element_type=jnp.float32)
    value_lin = jnp.dot(normed_cols, value_piece, preferred_element_type=jnp.float32)
    normed_one = normed_cols
    queries_b = rotary(query_lin, positions).astype(jnp.bfloat16)
    keys_b = rotary(key_lin, positions).astype(jnp.bfloat16)
    values_b = value_lin.astype(jnp.bfloat16)
    keys_all, values_all = (
        lax.all_gather(keys_b, "fsdp", axis=0, tiled=True),
        lax.all_gather(values_b, "fsdp", axis=0, tiled=True),
    )
    key_places = jnp.arange(keys_all.shape[0], dtype=jnp.int32)
    allowed = (key_places[None, :] <= query_places[:, None]) & (key_places[None, :] < lengths[0])
    attended, totals = attend_local(queries_b, keys_all, values_all, allowed)
    attended_b = attended.astype(jnp.bfloat16)
    branch = jnp.dot(
        attended_b,
        lax.all_gather(w_output, ("dp", "fsdp"), axis=0, tiled=True),
        preferred_element_type=jnp.float32,
    )
    hidden = tokens_f + branch
    scaled_two = norm_scale(hidden)
    gain_piece = lax.all_gather(norm_mlp, ("dp", "fsdp"), axis=0, tiled=True)
    gate_piece = lax.all_gather(w_gate, ("dp", "fsdp"), axis=0, tiled=True)
    up_piece = lax.all_gather(w_up, ("dp", "fsdp"), axis=0, tiled=True)
    normed_cols = (scaled_two * gain_piece.astype(jnp.float32)).astype(jnp.bfloat16)
    gate = jnp.dot(normed_cols, gate_piece, preferred_element_type=jnp.float32)
    up_part = jnp.dot(normed_cols, up_piece, preferred_element_type=jnp.float32)
    mixed_b = (jax.nn.silu(gate) * up_part).astype(jnp.bfloat16)
    down = jnp.dot(
        mixed_b,
        lax.all_gather(w_down, ("dp", "fsdp"), axis=0, tiled=True),
        preferred_element_type=jnp.float32,
    )
    output = (hidden + down).astype(jnp.bfloat16)
    return {
        "output": output,
        "places": query_places,
        "positions": positions,
        "tokens_f": tokens_f,
        "scaled_one": scaled_one,
        "normed_one": normed_one,
        "queries_b": queries_b,
        "keys_all": keys_all,
        "values_all": values_all,
        "allowed": allowed,
        "totals": totals,
        "attended_b": attended_b,
        "hidden": hidden,
        "scaled_two": scaled_two,
        "normed_two": normed_cols,
        "gate": gate,
        "up_part": up_part,
        "mixed_b": mixed_b,
    }


def body(
    tokens,
    cotangent,
    lengths,
    norm_attn,
    w_query,
    w_key,
    w_value,
    w_output,
    norm_mlp,
    w_gate,
    w_up,
    w_down,
):
    weights = (norm_attn, w_query, w_key, w_value, w_output, norm_mlp, w_gate, w_up, w_down)
    saved = forward_pass(tokens, lengths, *weights)
    output = saved["output"]
    again = lax.optimization_barrier((tokens, output))[0]
    saved = forward_pass(again, lengths, *weights)
    count_rows = tokens.shape[0]
    width = tokens.shape[1]
    live = (saved["places"] < lengths[0]).astype(jnp.float32)[:, None]
    grad_out = cotangent.astype(jnp.float32) * live
    grad_out_b = grad_out.astype(jnp.bfloat16)
    mixed_b = saved["mixed_b"]
    grad_mixed = cols_inner(grad_out_b, lax.all_gather(w_down, ("dp", "fsdp"), axis=0, tiled=True))
    grad_w_down = lax.psum_scatter(
        rows_inner(mixed_b, grad_out_b), ("dp", "fsdp"), scatter_dimension=0, tiled=True
    )
    _, silu_pull = jax.vjp(
        lambda first_in, second_in: jax.nn.silu(first_in) * second_in,
        saved["gate"],
        saved["up_part"],
    )
    grad_gate, grad_up = silu_pull(grad_mixed)
    grad_gate_b = grad_gate.astype(jnp.bfloat16)
    grad_up_b = grad_up.astype(jnp.bfloat16)
    zero_rows = jnp.zeros((count_rows, width), jnp.float32)
    gain_piece = lax.all_gather(norm_mlp, ("dp", "fsdp"), axis=0, tiled=True)
    gate_piece = lax.all_gather(w_gate, ("dp", "fsdp"), axis=0, tiled=True)
    up_piece = lax.all_gather(w_up, ("dp", "fsdp"), axis=0, tiled=True)
    columns = cols_inner(grad_gate_b, gate_piece) + cols_inner(grad_up_b, up_piece)
    grad_normed_two = columns
    grad_scaled_two = columns * gain_piece.astype(jnp.float32)
    normed_two = saved["normed_two"]
    grad_norm_mlp, grad_w_gate, grad_w_up = (
        lax.psum_scatter(
            jnp.sum(grad_normed_two * saved["scaled_two"], 0),
            ("dp", "fsdp"),
            scatter_dimension=0,
            tiled=True,
        ),
        lax.psum_scatter(
            rows_inner(normed_two, grad_gate_b), ("dp", "fsdp"), scatter_dimension=0, tiled=True
        ),
        lax.psum_scatter(
            rows_inner(normed_two, grad_up_b), ("dp", "fsdp"), scatter_dimension=0, tiled=True
        ),
    )
    _, norm_pull_two = jax.vjp(norm_scale, saved["hidden"])
    grad_hidden = grad_out + norm_pull_two(grad_scaled_two)[0]
    grad_hidden_b = grad_hidden.astype(jnp.bfloat16)
    grad_attended_b = cols_inner(
        grad_hidden_b, lax.all_gather(w_output, ("dp", "fsdp"), axis=0, tiled=True)
    ).astype(jnp.bfloat16)
    grad_query, grad_key_all, grad_value_all = attend_back(
        saved["queries_b"],
        saved["keys_all"],
        saved["values_all"],
        grad_attended_b,
        saved["totals"],
        saved["allowed"],
    )
    grad_key, grad_value = (
        lax.psum_scatter(
            grad_key_all.astype(jnp.bfloat16), "fsdp", scatter_dimension=0, tiled=True
        ).astype(jnp.float32),
        lax.psum_scatter(
            grad_value_all.astype(jnp.bfloat16), "fsdp", scatter_dimension=0, tiled=True
        ).astype(jnp.float32),
    )
    positions = saved["positions"]
    _, rope_pull = jax.vjp(lambda values: rotary(values, positions), zero_rows)
    grad_query_b = rope_pull(grad_query)[0].astype(jnp.bfloat16)
    grad_key_b = rope_pull(grad_key)[0].astype(jnp.bfloat16)
    grad_value_b = grad_value.astype(jnp.bfloat16)
    gain_piece = lax.all_gather(norm_attn, ("dp", "fsdp"), axis=0, tiled=True)
    query_piece = lax.all_gather(w_query, ("dp", "fsdp"), axis=0, tiled=True)
    key_piece = lax.all_gather(w_key, ("dp", "fsdp"), axis=0, tiled=True)
    value_piece = lax.all_gather(w_value, ("dp", "fsdp"), axis=0, tiled=True)
    columns = (
        cols_inner(grad_query_b, query_piece)
        + cols_inner(grad_key_b, key_piece)
        + cols_inner(grad_value_b, value_piece)
    )
    grad_scaled_one = columns * gain_piece.astype(jnp.float32)
    normed_one = saved["normed_one"]
    grad_norm_attn, grad_w_query, grad_w_key, grad_w_value, grad_w_output = (
        lax.psum_scatter(
            jnp.sum(columns * saved["scaled_one"], 0),
            ("dp", "fsdp"),
            scatter_dimension=0,
            tiled=True,
        ),
        lax.psum_scatter(
            rows_inner(normed_one, grad_query_b), ("dp", "fsdp"), scatter_dimension=0, tiled=True
        ),
        lax.psum_scatter(
            rows_inner(normed_one, grad_key_b), ("dp", "fsdp"), scatter_dimension=0, tiled=True
        ),
        lax.psum_scatter(
            rows_inner(normed_one, grad_value_b), ("dp", "fsdp"), scatter_dimension=0, tiled=True
        ),
        lax.psum_scatter(
            rows_inner(saved["attended_b"], grad_hidden_b),
            ("dp", "fsdp"),
            scatter_dimension=0,
            tiled=True,
        ),
    )
    _, norm_pull_one = jax.vjp(norm_scale, saved["tokens_f"])
    grad_tokens = (grad_hidden + norm_pull_one(grad_scaled_one)[0]).astype(jnp.bfloat16)
    return (
        output,
        grad_tokens,
        grad_norm_attn,
        grad_w_query,
        grad_w_key,
        grad_w_value,
        grad_w_output,
        grad_norm_mlp,
        grad_w_gate,
        grad_w_up,
        grad_w_down,
    )


def solution(mesh):
    placed = (
        P(("dp", "fsdp"), None),
        P(("dp", "fsdp"), None),
        P("dp"),
        P(("dp", "fsdp")),
        P(("dp", "fsdp"), None),
        P(("dp", "fsdp"), None),
        P(("dp", "fsdp"), None),
        P(("dp", "fsdp"), None),
        P(("dp", "fsdp")),
        P(("dp", "fsdp"), None),
        P(("dp", "fsdp"), None),
        P(("dp", "fsdp"), None),
    )
    return jax.shard_map(
        body,
        mesh=mesh,
        in_specs=placed,
        out_specs=(
            P(("dp", "fsdp"), None),
            P(("dp", "fsdp"), None),
            P(("dp", "fsdp")),
            P(("dp", "fsdp"), None),
            P(("dp", "fsdp"), None),
            P(("dp", "fsdp"), None),
            P(("dp", "fsdp"), None),
            P(("dp", "fsdp")),
            P(("dp", "fsdp"), None),
            P(("dp", "fsdp"), None),
            P(("dp", "fsdp"), None),
        ),
        check_vma=False,
    )
```

profile of v0, /device:TPU:0, one launch (start us, length us, event | category | flops | bytes accessed | tf_op | source)
XLA Modules:
  0.0 4454.6 jit_solution(17785644732839322267)
XLA Ops:
  11.2 42.6 all-reduce.9
  55.5 35.9 all-gather.14.cloned.1.call-done
  91.4 6.2 fusion.107
  99.9 70.5 %all-gather.12.cloned.1.call-done = bf16[2048,2048]{1,0:T(8,128)(2,1)} async-done(((bf16[64,2048]{1,0:T(8,128)(2,1)}), bf16[2048,2048]{1,0:T(8,128)(2,1)}) %all-gather.12.cloned.1.call-update) | async-done | bytes 8388624 | tf_op jit(solution)/shard_map/all_gather | solution.py:133
  170.4 6.0 fusion.109
  176.4 3.2 reshape.242
  179.6 5.5 subtract_convert_fusion.2
  187.8 61.7 %all-gather.18.cloned.1.call-done = bf16[2048,2048]{1,0:T(8,128)(2,1)} async-done(((bf16[64,2048]{1,0:T(8,128)(2,1)}), bf16[2048,2048]{1,0:T(8,128)(2,1)}) %all-gather.18.cloned.1.call-update) | async-done | bytes 8388624 | tf_op jit(solution)/shard_map/all_gather | solution.py:135
  249.4 5.8 convolution_convert_fusion.2
  264.0 42.1 all-gather.16.cloned.1.call-done
  306.1 7.9 copy.52
  314.0 49.0 %all-gather.20.cloned.1.call-done = bf16[1280,2048]{1,0:T(8,128)(2,1)} async-done(((bf16[160,2048]{1,0:T(8,128)(2,1)}), bf16[1280,2048]{1,0:T(8,128)(2,1)}) %all-gather.20.cloned.1.call-update) | async-done | bytes 5242896 | tf_op jit(solution)/shard_map/all_gather | solution.py:146
  363.1 7.9 copy.53
  370.9 38.4 while.42
  409.4 33.1 all-gather.22.cloned.1.call-done
  442.4 5.0 multiply_reduce_fusion.4
  447.5 191.4 %all-gather.24.cloned.1.call-done = bf16[2048,8192]{1,0:T(8,128)(2,1)} async-done(((bf16[64,8192]{1,0:T(8,128)(2,1)}), bf16[2048,8192]{1,0:T(8,128)(2,1)}) %all-gather.24.cloned.1.call-update) | async-done | bytes 33554448 | tf_op jit(solution)/shard_map/all_gather | solution.py:160
  638.8 16.5 fusion.88
  655.4 179.5 %all-gather.28.cloned.1.call-done = bf16[8192,2048]{1,0:T(8,128)(2,1)} async-done(((bf16[256,2048]{1,0:T(8,128)(2,1)}), bf16[8192,2048]{1,0:T(8,128)(2,1)}) %all-gather.28.cloned.1.call-update) | async-done | bytes 33554448 | tf_op jit(solution)/shard_map/all_gather | solution.py:168
  834.8 196.0 %all-gather.26.cloned.1.call-done = bf16[2048,8192]{1,0:T(8,128)(2,1)} async-done(((bf16[64,8192]{1,0:T(8,128)(2,1)}), bf16[2048,8192]{1,0:T(8,128)(2,1)}) %all-gather.26.cloned.1.call-update) | async-done | bytes 33554448 | tf_op jit(solution)/shard_map/all_gather | solution.py:161
  1030.8 27.3 fusion.73
  1058.9 6.0 fusion.118
  1067.1 6.0 fusion.120
  1073.1 3.2 reshape.246
  1076.4 5.5 subtract_convert_fusion
  1084.5 5.9 convolution_convert_fusion.1
  1095.4 43.4 all-gather.30.cloned.1.call-done
  1138.8 8.0 copy.55
  1146.8 48.5 %all-gather.32.cloned.1.call-done = bf16[1280,2048]{1,0:T(8,128)(2,1)} async-done(((bf16[160,2048]{1,0:T(8,128)(2,1)}), bf16[1280,2048]{1,0:T(8,128)(2,1)}) %all-gather.32.cloned.1.call-update) | async-done | bytes 5242896 | tf_op jit(solution)/shard_map/all_gather | solution.py:146
  1195.3 7.9 copy.56
  1203.2 37.8 while.43
  1242.0 5.0 multiply_reduce_fusion.3
  1247.3 16.3 fusion.126
  1263.6 15.8 fusion.125
  1279.4 21.4 multiply_convert_fusion.2
  1300.8 17.6 fusion.127
  1318.4 18.9 multiply_reduce_fusion.1
  1339.5 6.8 convolution_convert_fusion
  1347.6 94.7 %while.44 = (s32[]{:T(128)}, f32[8,4,160,64]{2,3,1,0:T(8,128)}, bf16[8,4,1280,64]{2,3,1,0:T(8,128)(2,1)}, bf16[8,4,1280,64]{2,3,1,0:T(8,128)(2,1)}, bf16[8,4,160...) while((s32[]{:T(128)}, f32[8,4,160,64]{2,3,1,0:T(8,128)}, ...), condition=%wide.region_15.16_spmd.clone.clone, body=%wide.region_13.15_spmd.clone.sunk.clone | while | flops 532438400 | bytes 30379512 | solution.py:111
  1442.3 7.9 copy.59
  1450.3 8.1 copy.60
  1458.5 8.2 fusion.95
  1466.7 3.6 copy.58
  1470.4 38.7 reduce-scatter.12.cloned.1.call-done
  1509.1 3.2 reshape.254
  1512.3 4.5 multiply_add_fusion.1
  1520.4 8.3 fusion.115
  1531.1 8.2 fusion.113
  1539.6 30.1 reduce-scatter.28.cloned.1.call-done
  1569.7 9.5 fusion.111
  1580.3 25.7 fusion.129
  1606.0 25.7 fusion.130
  1632.9 28.2 fusion.70
  1661.1 6.5 fusion.128
  1667.7 6.5 convolution_add_fusion.3
  1674.3 3.2 fusion.77
  1677.5 40.3 all-reduce.8
  1720.2 38.3 reduce-scatter.20.cloned.1.call-done
  1758.5 187.1 %reduce-scatter.14.cloned.1.call-done = f32[64,2048]{1,0:T(8,128)} async-done(((f32[2048,2048]{1,0:T(8,128)}), f32[64,2048]{1,0:T(8,128)}) %reduce-scatter.14.cloned.1.call-update) | async-done | bytes 524304 | tf_op jit(solution)/shard_map/reduce_scatter | solution.py:298
  1945.6 187.1 %reduce-scatter.16.cloned.1.call-done = f32[64,2048]{1,0:T(8,128)} async-done(((f32[2048,2048]{1,0:T(8,128)}), f32[64,2048]{1,0:T(8,128)}) %reduce-scatter.16.cloned.1.call-update) | async-done | bytes 524304 | tf_op jit(solution)/shard_map/reduce_scatter | solution.py:301
  2132.7 187.1 %reduce-scatter.18.cloned.1.call-done = f32[64,2048]{1,0:T(8,128)} async-done(((f32[2048,2048]{1,0:T(8,128)}), f32[64,2048]{1,0:T(8,128)}) %reduce-scatter.18.cloned.1.call-update) | async-done | bytes 524304 | tf_op jit(solution)/shard_map/reduce_scatter | solution.py:304
  2319.8 709.9 %reduce-scatter.22.cloned.1.call-done = f32[64,8192]{1,0:T(8,128)} async-done(((f32[2048,8192]{1,0:T(8,128)}), f32[64,8192]{1,0:T(8,128)}) %reduce-scatter.22.cloned.1.call-update) | async-done | bytes 2097168 | tf_op jit(solution)/shard_map/reduce_scatter | solution.py:246
  3029.7 708.9 %reduce-scatter.24.cloned.1.call-done = f32[64,8192]{1,0:T(8,128)} async-done(((f32[2048,8192]{1,0:T(8,128)}), f32[64,8192]{1,0:T(8,128)}) %reduce-scatter.24.cloned.1.call-update) | async-done | bytes 2097168 | tf_op jit(solution)/shard_map/reduce_scatter | solution.py:249
  3738.6 708.7 %reduce-scatter.26.cloned.1.call-done = f32[256,2048]{1,0:T(8,128)} async-done(((f32[8192,2048]{1,0:T(8,128)}), f32[256,2048]{1,0:T(8,128)}) %reduce-scatter.26.cloned.1.call-update) | async-done | bytes 2097168 | tf_op jit(solution)/shard_map/reduce_scatter | solution.py:220
  (291 shorter events, 214.5 us)
Async XLA Ops:
  7.2 84.2 %all-gather.14.cloned.1.call-start = ((), (), s32[]{:S(2)}) async-start(), calls=%async_computation.10 | async-start | bytes 8650752 | tf_op jit(solution)/shard_map/all_gather | solution.py:134
  7.9 162.5 %all-gather.12.cloned.1.call-start = ((), (), s32[]{:S(2)}) async-start(), calls=%async_computation.9 | async-start | bytes 8650752 | tf_op jit(solution)/shard_map/all_gather | solution.py:133
  8.7 240.7 %all-gather.18.cloned.1.call-start = ((), (), s32[]{:S(2)}) async-start(), calls=%async_computation.12 | async-start | bytes 8650752 | tf_op jit(solution)/shard_map/all_gather | solution.py:135
  9.4 296.8 %all-gather.16.cloned.1.call-start = ((), (), s32[]{:S(2)}) async-start(), calls=%async_computation.11 | async-start | bytes 5898240 | tf_op jit(solution)/shard_map/all_gather | solution.py:145
  53.8 1030.7 %copy-start.20 = (f32[2048]{0:T(1024)}, f32[2048]{0:T(1024)S(1)}, u32[]{:S(2)}) copy-start(f32[2048]{0:T(1024)S(1)} %convert_element_type.161) | copy-start | bytes 24580
  55.5 1020.9 %copy-start.16 = (f32[160,32]{1,0:T(8,128)}, f32[160,32]{1,0:T(8,128)S(1)}, u32[]{:S(2)}) copy-start(f32[160,32]{1,0:T(8,128)S(1)} %get-tuple-element.297) | copy-start | bytes 61444
  55.5 1020.9 %copy-start.18 = (f32[160,32]{1,0:T(8,128)}, f32[160,32]{1,0:T(8,128)S(1)}, u32[]{:S(2)}) copy-start(f32[160,32]{1,0:T(8,128)S(1)} %get-tuple-element.298) | copy-start | bytes 61444
  97.6 72.8 %copy-start = (bf16[160,2048]{1,0:T(8,128)(2,1)S(1)}, bf16[160,2048]{1,0:T(8,128)(2,1)}, u32[]{:S(2)}) copy-start(bf16[160,2048]{1,0:T(8,128)(2,1)} %param.18) | copy-start | bytes 1966084
  187.7 175.4 %all-gather.20.cloned.1.call-start = ((), (), s32[]{:S(2)}) async-start(), calls=%async_computation.13 | async-start | bytes 5898240 | tf_op jit(solution)/shard_map/all_gather | solution.py:146
  255.2 187.2 %all-gather.22.cloned.1.call-start = ((), (), s32[]{:S(2)}) async-start(), calls=%async_computation.14 | async-start | bytes 8650752 | tf_op jit(solution)/shard_map/all_gather | solution.py:154
  255.8 383.0 %all-gather.24.cloned.1.call-start = ((), (), s32[]{:S(2)}) async-start(), calls=%async_computation.15 | async-start | bytes 34603008 | tf_op jit(solution)/shard_map/all_gather | solution.py:160
  256.5 578.3 %all-gather.28.cloned.1.call-start = ((), (), s32[]{:S(2)}) async-start(), calls=%async_computation.17 | async-start | bytes 34603008 | tf_op jit(solution)/shard_map/all_gather | solution.py:168
  257.3 773.5 %all-gather.26.cloned.1.call-start = ((), (), s32[]{:S(2)}) async-start(), calls=%async_computation.16 | async-start | bytes 34603008 | tf_op jit(solution)/shard_map/all_gather | solution.py:161
  258.0 880.8 %all-gather.30.cloned.1.call-start = ((), (), s32[]{:S(2)}) async-start(), calls=%async_computation.18 | async-start | bytes 5898240 | tf_op jit(solution)/shard_map/all_gather | solution.py:145
  258.4 3.2 copy-start.2
  314.0 56.9 %copy-start.4 = (bf16[8,4,160,64]{2,3,1,0:T(8,128)(2,1)S(1)}, bf16[8,4,160,64]{2,3,1,0:T(8,128)(2,1)}, u32[]{:S(2)}) copy-start(bf16[8,4,160,64]{2,3,1,0:T(8,128)(2,1)} %copy-done.2) | copy-start | bytes 1966084
  1058.3 0.6 copy-start.27
  1058.9 25.6 copy-start.22
  1084.4 6.2 copy-start.11
  1084.5 6.2 copy-start.12
  1084.5 110.8 %all-gather.32.cloned.1.call-start = ((), (), s32[]{:S(2)}) async-start(), calls=%async_computation.19 | async-start | bytes 5898240 | tf_op jit(solution)/shard_map/all_gather | solution.py:146
  1090.5 418.6 %reduce-scatter.12.cloned.1.call-start = ((), (), s32[]{:S(2)}) async-start(), calls=%async_computation.20 | async-start | bytes 5898240 | tf_op jit(solution)/shard_map/reduce_scatter | solution.py:268
  1090.6 246.8 %copy-start.25 = (f32[160]{0:T(256)}, f32[160]{0:T(256)S(1)}, u32[]{:S(2)}) copy-start(f32[160]{0:T(256)S(1)} %compare_convert_fusion) | copy-start | bytes 1924
  1146.8 56.4 %copy-start.3 = (bf16[8,4,160,64]{2,3,1,0:T(8,128)(2,1)S(1)}, bf16[8,4,160,64]{2,3,1,0:T(8,128)(2,1)}, u32[]{:S(2)}) copy-start(bf16[8,4,160,64]{2,3,1,0:T(8,128)(2,1)} %copy-done.2) | copy-start | bytes 1966084
  1241.0 1.0 copy-start.10
  1247.0 71.4 %copy-start.7 = (f32[160,2048]{1,0:T(8,128)}, f32[160,2048]{1,0:T(8,128)S(1)}, u32[]{:S(2)}) copy-start(f32[160,2048]{1,0:T(8,128)S(1)} %get-tuple-element.302) | copy-start | bytes 3932164
  1247.2 16.3 copy-start.8
  1263.6 15.8 copy-start.13
  1339.5 119.0 %copy-start.5 = (f32[160,2048]{1,0:T(8,128)}, f32[160,2048]{1,0:T(8,128)S(1)}, u32[]{:S(2)}) copy-start(f32[160,2048]{1,0:T(8,128)S(1)} %fusion.81) | copy-start | bytes 3932164
  1450.2 119.5 %reduce-scatter.28.cloned.1.call-start = ((), (), s32[]{:S(2)}) async-start(), calls=%async_computation.28 | async-start | bytes 5898240
  1458.4 300.1 %reduce-scatter.20.cloned.1.call-start = ((), (), s32[]{:S(2)}) async-start(), calls=%async_computation.24 | async-start | bytes 17301504 | tf_op jit(solution)/shard_map/reduce_scatter | solution.py:307
  1466.7 478.9 %reduce-scatter.14.cloned.1.call-start = ((), (), s32[]{:S(2)}) async-start(), calls=%async_computation.21 | async-start | bytes 17301504 | tf_op jit(solution)/shard_map/reduce_scatter | solution.py:298
  1470.3 42.0 copy-start.17
  1470.4 42.0 copy-start.19
  1516.9 3.5 copy-start.1
  1516.9 3.5 copy-start.21
  1516.9 3.5 copy-start.23
  1528.7 604.0 %reduce-scatter.16.cloned.1.call-start = ((), (), s32[]{:S(2)}) async-start(), calls=%async_computation.22 | async-start | bytes 17301504 | tf_op jit(solution)/shard_map/reduce_scatter | solution.py:301
  1539.3 780.5 %reduce-scatter.18.cloned.1.call-start = ((), (), s32[]{:S(2)}) async-start(), calls=%async_computation.23 | async-start | bytes 17301504 | tf_op jit(solution)/shard_map/reduce_scatter | solution.py:304
  1579.2 1.1 copy-start.9
  1579.2 1450.5 %reduce-scatter.22.cloned.1.call-start = ((), (), s32[]{:S(2)}) async-start(), calls=%async_computation.25 | async-start | bytes 69206016 | tf_op jit(solution)/shard_map/reduce_scatter | solution.py:246
  1606.0 2132.6 %reduce-scatter.24.cloned.1.call-start = ((), (), s32[]{:S(2)}) async-start(), calls=%async_computation.26 | async-start | bytes 69206016 | tf_op jit(solution)/shard_map/reduce_scatter | solution.py:249
  1631.8 1.1 copy-start.14
  1631.8 1.1 copy-start.26
  1631.8 2815.5 %reduce-scatter.26.cloned.1.call-start = ((), (), s32[]{:S(2)}) async-start(), calls=%async_computation.27 | async-start | bytes 69206016 | tf_op jit(solution)/shard_map/reduce_scatter | solution.py:220
  1661.1 13.1 slice-start
  1667.6 6.6 slice-start.1
  1667.6 6.6 copy-start.15
  1674.2 3.3 copy-start.24
  1674.3 44.7 %copy-start.28 = (f32[160]{0:T(256)S(1)}, f32[160]{0:T(256)}, u32[]{:S(2)}) copy-start(f32[160]{0:T(256)} %copy-done.27) | copy-start | bytes 1924
  1674.3 44.7 %copy-start.6 = (f32[160,2048]{1,0:T(8,128)S(1)}, f32[160,2048]{1,0:T(8,128)}, u32[]{:S(2)}) copy-start(f32[160,2048]{1,0:T(8,128)} %copy-done.5) | copy-start | bytes 3932164
Sparse Core Ops, SparseCore 0:
  11.0 80.3 all-gather.13
  94.4 75.9 all-gather.11
  173.4 75.9 all-gather.17
  251.5 54.6 all-gather.15
  308.2 54.8 all-gather.19
  365.9 76.4 all-gather.21
  445.4 193.3 all-gather.23
  641.8 192.9 all-gather.27
  837.8 192.9 all-gather.25
  1084.6 54.2 all-gather.29
  1140.5 54.8 all-gather.31
  1450.4 58.6 reduce-scatter.11
  1511.4 58.2 reduce-scatter.27
  1572.4 186.0 reduce-scatter.19
  1761.2 184.3 reduce-scatter.13
  1948.3 184.3 reduce-scatter.15
  2135.4 184.3 reduce-scatter.17
  2322.6 707.0 reduce-scatter.21
  3032.6 705.9 reduce-scatter.23
  3741.3 705.8 reduce-scatter.25
where the time goes:
time: 4470 us; the launch traced here: 4450 us
  waiting for transfers between devices  3750 us (84%)
  matrix products  468 us (10%)
  local copies, waits for them, and re-layouts  85.4 us (2%)
  blocking collectives  82.9 us (2%)
  other arithmetic  47.9 us (1%)
    reduce_scatter x1, waiting for transfers between devices, body(): lax.psum_scatter(rows_inner(normed_two, grad_gate_b), ('dp', 'fsdp'), sca...  710 us
    reduce_scatter x1, waiting for transfers between devices, body(): lax.psum_scatter(rows_inner(normed_two, grad_up_b), ('dp', 'fsdp'), scatt...  709 us
    reduce_scatter x1, waiting for transfers between devices, body(): lax.psum_scatter(rows_inner(mixed_b, grad_out_b), ('dp', 'fsdp'), scatter...  709 us
    all_gather x1, waiting for transfers between devices, forward_pass(): up_piece = lax.all_gather(w_up, ('dp', 'fsdp'), axis=0, tiled=True)  196 us
    all_gather x1, waiting for transfers between devices, forward_pass(): gate_piece = lax.all_gather(w_gate, ('dp', 'fsdp'), axis=0, tiled=True)  191 us
    reduce_scatter x1, waiting for transfers between devices, body(): lax.psum_scatter(rows_inner(normed_one, grad_key_b), ('dp', 'fsdp'), scat...  187 us
    reduce_scatter x1, waiting for transfers between devices, body(): lax.psum_scatter(rows_inner(normed_one, grad_query_b), ('dp', 'fsdp'), sc...  187 us
    reduce_scatter x1, waiting for transfers between devices, body(): lax.psum_scatter(rows_inner(normed_one, grad_value_b), ('dp', 'fsdp'), sc...  187 us
  transfers between devices with their start and end apart: 20, of which 20 were waited for; matrix products, arithmetic and copies ran while one was open for 7% of the time, Pallas kernels for 0%

commit v1 on v0

v1 whole, which is shorter than its diff:
```python
import jax
import jax.numpy as jnp
from jax import lax
from jax.sharding import PartitionSpec as P

HEADS = 32
HEAD_DIM = 64


EPSILON = 1e-05
THETA = 130000.0
BF16 = jnp.bfloat16
F32 = jnp.float32


def rotary_tables(count):
    half = HEAD_DIM // 2
    inverse = THETA ** (-jnp.arange(half, dtype=F32) * 2.0 / HEAD_DIM)
    angles = jnp.arange(count, dtype=jnp.int32).astype(F32)[:, None] * inverse[None, :]
    return jnp.cos(angles)[:, None, :], jnp.sin(angles)[:, None, :]


def rotary(values, tables, sign):
    cosine, sine = tables
    sine = sine * sign
    half = HEAD_DIM // 2
    shaped = values.reshape(values.shape[0], -1, HEAD_DIM)
    first, second = shaped[..., :half], shaped[..., half:]
    turned = jnp.concatenate(
        [first * cosine - second * sine, second * cosine + first * sine], -1
    )
    return turned.reshape(values.shape)


def dot(left, right):
    return jnp.dot(left, right, preferred_element_type=F32)


def rows_inner(left, right):
    return lax.dot_general(left, right, (((0,), (0,)), ((), ())), preferred_element_type=F32)


def cols_inner(left, right):
    return lax.dot_general(left, right, (((1,), (1,)), ((), ())), preferred_element_type=F32)


def inverse_rms(values):
    return lax.rsqrt(jnp.mean(values * values, -1, keepdims=True) + EPSILON)


def norm_back(grad_scaled, scaled, scale):
    return scale * (grad_scaled - scaled * jnp.mean(grad_scaled * scaled, -1, keepdims=True))


def by_heads(values):
    return values.reshape(values.shape[0], -1, HEAD_DIM).transpose(1, 0, 2)


def by_rows(values):
    return values.transpose(1, 0, 2).reshape(values.shape[1], -1)


def attend(queries, keys, values, allowed):
    scores = (
        jnp.einsum("hqd,hkd->hqk", by_heads(queries), by_heads(keys), preferred_element_type=F32)
        * 0.125
    )
    scores = jnp.where(allowed[None], scores, -1000000000.0)
    row_max = jnp.max(scores, -1, keepdims=True)
    log_total = row_max + jnp.log(jnp.sum(jnp.exp(scores - row_max), -1, keepdims=True))
    weights = jnp.exp(scores - log_total).astype(BF16)
    result = jnp.einsum("hqk,hkd->hqd", weights, by_heads(values), preferred_element_type=F32)
    return by_rows(result), log_total


def attend_back(queries, keys, values, grad, log_total, allowed):
    queries, keys, values, grad = (by_heads(v) for v in (queries, keys, values, grad))
    scores = jnp.einsum("hqd,hkd->hqk", queries, keys, preferred_element_type=F32) * 0.125
    scores = jnp.where(allowed[None], scores, -1000000000.0)
    weights = jnp.exp(scores - log_total)
    grad_weights = jnp.einsum("hqd,hkd->hqk", grad, values, preferred_element_type=F32)
    grad_scores = (
        weights * (grad_weights - jnp.sum(weights * grad_weights, -1, keepdims=True))
    ).astype(BF16)
    grad_q = 0.125 * jnp.einsum("hqk,hkd->hqd", grad_scores, keys, preferred_element_type=F32)
    grad_k = 0.125 * jnp.einsum("hqk,hqd->hkd", grad_scores, queries, preferred_element_type=F32)
    grad_v = jnp.einsum("hqk,hqd->hkd", weights.astype(BF16), grad, preferred_element_type=F32)
    return by_rows(grad_q), by_rows(grad_k), by_rows(grad_v)


def build(groups, ranks):
    def gather_rows(value):
        return lax.all_gather(value, "fsdp", axis=0, tiled=True)

    def scatter_rows(value):
        return lax.psum_scatter(
            value.astype(BF16), "fsdp", scatter_dimension=0, tiled=True
        ).astype(F32)

    def exchange(value):
        return lax.all_to_all(value, "fsdp", 0, 0, tiled=True)

    def body(
        tokens, cotangent, lengths, norm_attn, w_query, w_key, w_value, w_output, norm_mlp, w_gate, w_up, w_down
    ):
        rows, width = tokens.shape
        depth = w_query.shape[0]
        count = rows * ranks
        rank_heads = HEADS // ranks
        hidden_part = w_down.shape[0]
        out_rows = w_output.shape[0]
        split = max(1, HEAD_DIM // out_rows)
        rank = lax.axis_index("fsdp")

        def heads_out(weight):
            shaped = weight.reshape(depth, split, rank_heads, ranks // split, HEAD_DIM)
            return shaped.transpose(3, 1, 0, 2, 4).reshape(ranks, depth, rank_heads * HEAD_DIM)

        def heads_in(pieces):
            shaped = pieces.reshape(ranks // split, split, depth, rank_heads, HEAD_DIM)
            return shaped.transpose(2, 1, 3, 0, 4).reshape(depth, HEADS * HEAD_DIM)

        def units_out(weight):
            shaped = weight.reshape(depth, groups, ranks, hidden_part)
            return shaped.transpose(2, 0, 1, 3).reshape(ranks, depth, groups * hidden_part)

        def units_in(pieces):
            shaped = pieces.reshape(ranks, depth, groups, hidden_part)
            return shaped.transpose(1, 2, 0, 3).reshape(depth, groups * ranks * hidden_part)

        span = [[base * split + i for i in range(split)] for base in range(ranks // split)]

        def gather_output(weight):
            if split > 1:
                weight = lax.all_gather(weight, "fsdp", axis=0, tiled=True, axis_index_groups=span)
            whole = lax.all_gather(weight, "dp", axis=0, tiled=True)
            if split > 1:
                whole = whole.reshape(split, -1, width)[lax.rem(rank, split)]
            return whole

        def scatter_output(grad):
            grad = grad.astype(BF16)
            if split > 1:
                place = lax.rem(rank, split)
                grad = jnp.where(
                    (jnp.arange(split) == place)[:, None, None], grad[None], jnp.zeros((), BF16)
                ).reshape(-1, width)
            grad = lax.psum_scatter(grad, "dp", scatter_dimension=0, tiled=True)
            if split > 1:
                grad = lax.psum_scatter(
                    grad, "fsdp", scatter_dimension=0, tiled=True, axis_index_groups=span
                )
            return grad.astype(F32)

        head_cols = rank_heads * HEAD_DIM
        unit_cols = groups * hidden_part
        qkv_out = jnp.concatenate([heads_out(w) for w in (w_query, w_key, w_value)], -1)
        gate_up_out = jnp.concatenate([units_out(w) for w in (w_gate, w_up)], -1)
        x_all = gather_rows(tokens)
        qkv = lax.all_gather(exchange(qkv_out), "dp", axis=0, tiled=True).reshape(width, -1)
        gains = lax.all_gather(jnp.stack([norm_attn, norm_mlp], -1), ("dp", "fsdp"), axis=0, tiled=True)
        gain_one, gain_two = gains[:, 0].astype(F32), gains[:, 1].astype(F32)
        out_w = gather_output(w_output)
        gate_up = lax.all_gather(exchange(gate_up_out), "dp", axis=0, tiled=True).reshape(width, -1)
        down_w = lax.all_gather(w_down, "dp", axis=0, tiled=True)

        tokens_f = tokens.astype(F32)
        x_f = x_all.astype(F32)
        normed_one = (x_f * inverse_rms(x_f) * gain_one).astype(BF16)
        qkv_lin = dot(normed_one, qkv)
        tables = rotary_tables(count)
        queries = rotary(qkv_lin[:, :head_cols], tables, 1.0).astype(BF16)
        keys = rotary(qkv_lin[:, head_cols : 2 * head_cols], tables, 1.0).astype(BF16)
        values = qkv_lin[:, 2 * head_cols :].astype(BF16)
        places = jnp.arange(count, dtype=jnp.int32)
        allowed = (places[None, :] <= places[:, None]) & (places[None, :] < lengths[0])
        attended, log_total = attend(queries, keys, values, allowed)
        attended = attended.astype(BF16)
        hidden = tokens_f + scatter_rows(dot(attended, out_w))
        scale_two = inverse_rms(hidden)
        scaled_two = hidden * scale_two
        normed_two = gather_rows((scaled_two * gain_two).astype(BF16))
        gate_up_lin = dot(normed_two, gate_up)
        gate, up = gate_up_lin[:, :unit_cols], gate_up_lin[:, unit_cols:]
        sigmoid = 1.0 / (1.0 + jnp.exp(-gate))
        silu = gate * sigmoid
        mixed = (silu * up).astype(BF16)
        output = (hidden + scatter_rows(dot(mixed, down_w))).astype(BF16)

        live = places[:, None] < lengths[0]
        grad_out_all = jnp.where(live, gather_rows(cotangent), jnp.zeros((), BF16))
        own_places = rank * rows + jnp.arange(rows, dtype=jnp.int32)
        grad_out = cotangent.astype(F32) * (own_places < lengths[0]).astype(F32)[:, None]
        grad_mixed = cols_inner(grad_out_all, down_w)
        grad_w_down = lax.psum_scatter(
            rows_inner(mixed, grad_out_all).astype(BF16), "dp", scatter_dimension=0, tiled=True
        ).astype(F32)
        grad_gate = grad_mixed * up * (sigmoid * (1.0 + gate * (1.0 - sigmoid)))
        grad_up = grad_mixed * silu
        grad_gate_up = jnp.concatenate([grad_gate.astype(BF16), grad_up.astype(BF16)], -1)
        grad_normed_two = scatter_rows(cols_inner(grad_gate_up, gate_up))
        sum_two = jnp.sum(grad_normed_two * scaled_two, 0)
        grad_hidden = grad_out + norm_back(grad_normed_two * gain_two, scaled_two, scale_two)
        grad_hidden_all = gather_rows(grad_hidden.astype(BF16))
        grad_gate_up_w = exchange(
            lax.psum_scatter(
                rows_inner(normed_two, grad_gate_up).astype(BF16), "dp", scatter_dimension=0, tiled=True
            ).reshape(ranks, depth, 2 * unit_cols)
        )
        grad_w_gate = units_in(grad_gate_up_w[..., :unit_cols]).astype(F32)
        grad_w_up = units_in(grad_gate_up_w[..., unit_cols:]).astype(F32)
        grad_w_output = scatter_output(rows_inner(attended, grad_hidden_all))
        grad_attended = cols_inner(grad_hidden_all, out_w).astype(BF16)
        grad_q, grad_k, grad_v = attend_back(queries, keys, values, grad_attended, log_total, allowed)
        grad_qkv = jnp.concatenate(
            [
                rotary(grad_q, tables, -1.0).astype(BF16),
                rotary(grad_k, tables, -1.0).astype(BF16),
                grad_v.astype(BF16),
            ],
            -1,
        )
        grad_normed_one = scatter_rows(cols_inner(grad_qkv, qkv))
        scale_one = inverse_rms(tokens_f)
        scaled_one = tokens_f * scale_one
        sum_one = jnp.sum(grad_normed_one * scaled_one, 0)
        grad_tokens = (
            grad_hidden + norm_back(grad_normed_one * gain_one, scaled_one, scale_one)
        ).astype(BF16)
        grad_qkv_w = exchange(
            lax.psum_scatter(
                rows_inner(normed_one, grad_qkv).astype(BF16), "dp", scatter_dimension=0, tiled=True
            ).reshape(ranks, depth, 3 * head_cols)
        )
        grad_w_query, grad_w_key, grad_w_value = (
            heads_in(grad_qkv_w[..., i * head_cols : (i + 1) * head_cols]).astype(F32) for i in range(3)
        )
        sums = lax.psum_scatter(
            jnp.stack([sum_one, sum_two], -1), ("dp", "fsdp"), scatter_dimension=0, tiled=True
        )
        return (
            output,
            grad_tokens,
            sums[:, 0],
            grad_w_query,
            grad_w_key,
            grad_w_value,
            grad_w_output,
            sums[:, 1],
            grad_w_gate,
            grad_w_up,
            grad_w_down,
        )

    return body


def solution(mesh):
    both = P(("dp", "fsdp"))
    rows = P(("dp", "fsdp"), None)
    return jax.shard_map(
        build(mesh.shape["dp"], mesh.shape["fsdp"]),
        mesh=mesh,
        in_specs=(rows, rows, P("dp"), both, rows, rows, rows, rows, both, rows, rows, rows),
        out_specs=(rows, rows, both, rows, rows, rows, rows, both, rows, rows, rows),
        check_vma=False,
    )
```

time: 4470 us -> 1180 us (0.26)
  waiting for transfers between devices: 3750 us -> 622 us
  matrix products: 468 us -> 194 us
  blocking collectives: 82.9 us -> 226 us
    reduce_scatter x8, waiting for transfers between devices: 2770 us -> 188 us  [the longest x4 163 us: scatter_rows(): lax.psum_scatter(value.astype(BF16), 'fsdp', scatter_dimension=0, tiled=T...]
    all_gather x11 -> x8, waiting for transfers between devices: 951 us -> 299 us  [the longest x4 154 us: gather_rows(): return lax.all_gather(value, 'fsdp', axis=0, tiled=True)]
    all_to_all x0 -> x3, blocking collectives: none -> 186 us  [exchange(): return lax.all_to_all(value, 'fsdp', 0, 0, tiled=True)]
    dot_general x84 -> x10, matrix products: 273 us -> 111 us  [the longest x4 40.8 us: dot(): return jnp.dot(left, right, preferred_element_type=F32)]
    unnamed x21 -> x18, waiting for transfers between devices: 35 us -> 135 us
    unnamed x2 -> x0, blocking collectives: 82.9 us -> none
    dot_general x7 -> x4, matrix products: 114 us -> 39.3 us  [rows_inner(): lax.dot_general(left, right, (((0,), (0,)), ((), ())), preferred_element_...]
  transfers between devices with their start and end apart: 20 -> 18, of which waited for: 20 -> 13; matrix products, arithmetic and copies ran while one was open for 7% -> 22% of each run, Pallas kernels for 0% -> 0%
where the time goes in v1:
time: 1180 us
  waiting for transfers between devices  622 us (53%)
  blocking collectives  226 us (19%)
  matrix products  194 us (16%)
  other arithmetic  68.7 us (6%)
  local copies, waits for them, and re-layouts  46.3 us (4%)
  between operations  15.5 us (1%)
    all_to_all x3, blocking collectives, exchange(): return lax.all_to_all(value, 'fsdp', 0, 0, tiled=True)  186 us
    reduce_scatter x4, waiting for transfers between devices, scatter_rows(): lax.psum_scatter(value.astype(BF16), 'fsdp', scatter_dimension=0, tiled=T...  163 us
    all_gather x4, waiting for transfers between devices, gather_rows(): return lax.all_gather(value, 'fsdp', axis=0, tiled=True)  154 us
    unnamed x18, waiting for transfers between devices  135 us
    all_gather x1, waiting for transfers between devices, body(): lax.all_gather(exchange(gate_up_out), 'dp', axis=0, tiled=True)  90.2 us
    dot_general x4, matrix products, cols_inner(): lax.dot_general(left, right, (((1,), (1,)), ((), ())), preferred_element_...  43.4 us
    dot_general x4, matrix products, dot(): return jnp.dot(left, right, preferred_element_type=F32)  40.8 us
    all_gather x1, blocking collectives, body(): lax.all_gather(jnp.stack([norm_attn, norm_mlp], -1), ('dp', 'fsdp'), axis...  40 us
  transfers between devices with their start and end apart: 18, of which 13 were waited for; matrix products, arithmetic and copies ran while one was open for 22% of the time, Pallas kernels for 0%

profile of v1, /device:TPU:0, one launch (start us, length us, event | category | flops | bytes accessed | tf_op | source)
XLA Modules:
  0.0 1177.5 jit_solution(18107789999146092967)
XLA Ops:
  12.3 47.1 %all_to_all.20 = bf16[8,64,768]{2,1,0:T(8,128)(2,1)} all-to-all(bf16[8,64,768]{2,1,0:T(8,128)(2,1)S(1)} %pad_maximum_fusion.7), channel_id=1, replica_groups=mesh['dp'=4,'fsdp'=8] {'fsdp'}, dimensions={0} | all-to-all | bytes 1572864 | tf_op jit(solution)/shard_map/all_to_all | solution.py:101
  60.9 40.0 %all-gather = bf16[32,64,2]{1,2,0:T(2,128)(2,1)S(1)} all-gather(bf16[1,64,2]{1,2,0:T(2,128)(2,1)S(1)} %maximum_bitcast_fusion.6), channel_id=1, replica_groups=mesh['dp'=4,'fsdp'=8] {'dp','fsdp'}, dimensions={0}, use_global_device_ids=true | all-gather | bytes 8448 | tf_op jit(solution)/shard_map/all_gather | solution.py:161
  101.0 2.6 fusion.5
  104.9 3.6 fusion.2
  108.6 19.6 %all-gather.12.cloned.1.call-done = bf16[32,64,768]{2,1,0:T(8,128)(2,1)} async-done(((bf16[8,64,768]{2,1,0:T(8,128)(2,1)}), bf16[32,64,768]{2,1,0:T(8,128)(2,1)}) %all-gather.12.cloned.1.call-update) | async-done | bytes 3145744 | tf_op jit(solution)/shard_map/all_gather | solution.py:160
  128.1 8.0 fusion.27
  138.2 11.2 fusion.52
  149.5 10.6 exponential_reduce_fusion
  160.1 11.2 fusion.13
  171.3 5.4 convolution_convert_fusion.4
  178.6 1.5 reshape.312
  180.2 1.5 copy.78
  182.1 1.5 reshape.314
  183.6 1.7 pad_maximum_fusion.3
  185.4 85.9 %all_to_all.21 = bf16[8,64,2048]{2,1,0:T(8,128)(2,1)} all-to-all(bf16[8,64,2048]{2,1,0:T(8,128)(2,1)S(1)} %pad_maximum_fusion.3), channel_id=1, replica_groups=mesh['dp'=4,'fsdp'=8] {'fsdp'}, dimensions={0} | all-to-all | bytes 4194304 | tf_op jit(solution)/shard_map/all_to_all | solution.py:101
  271.4 2.3 reduce-scatter.12.cloned.1.call-done
  275.1 2.2 multiply_convert_fusion.4
  278.8 90.2 %all-gather.18.cloned.1.call-done = bf16[32,64,2048]{2,1,0:T(8,128)(2,1)} async-done(((bf16[8,64,2048]{2,1,0:T(8,128)(2,1)}), bf16[32,64,2048]{2,1,0:T(8,128)(2,1)}) %all-gather.18.cloned.1.call-update) | async-done | bytes 8388624 | tf_op jit(solution)/shard_map/all_gather | solution.py:164
  369.0 58.1 %all-gather.16.cloned.1.call-done = bf16[1280,2048]{1,0:T(8,128)(2,1)} async-done(((bf16[160,2048]{1,0:T(8,128)(2,1)}), bf16[1280,2048]{1,0:T(8,128)(2,1)}) %all-gather.16.cloned.1.call-update) | async-done | bytes 5242896 | tf_op jit(solution)/shard_map/all_gather | solution.py:93
  427.2 17.5 %fusion.53 = f32[1280,2048]{1,0:T(8,128)} fusion(bf16[1280,2048]{1,0:T(8,128)(2,1)} %all-gather.16.cloned.1.call-done, bf16[2048,2048]{1,0:T(8,128)(2,1)} %bitcast.176), kind=kOutput, calls=%fused_computation.125 | convolution fusion | flops 10737418240 | bytes 24117248 | tf_op jit(solution)/shard_map/dot_general | solution.py:36
  444.6 35.9 %all-gather.20.cloned.1.call-done = bf16[1024,2048]{1,0:T(8,128)(2,1)} async-done(((bf16[256,2048]{1,0:T(8,128)(2,1)}), bf16[1024,2048]{1,0:T(8,128)(2,1)}) %all-gather.20.cloned.1.call-update) | async-done | bytes 4194320 | tf_op jit(solution)/shard_map/all_gather | solution.py:165
  480.5 57.7 %all-gather.22.cloned.1.call-done = bf16[1280,2048]{1,0:T(8,128)(2,1)} async-done(((bf16[160,2048]{1,0:T(8,128)(2,1)}), bf16[1280,2048]{1,0:T(8,128)(2,1)}) %all-gather.22.cloned.1.call-update) | async-done | bytes 5242896 | tf_op jit(solution)/shard_map/all_gather | solution.py:93
  538.2 14.9 %multiply_convert_fusion.2 = (bf16[1280,1024]{1,0:T(8,128)(2,1)S(1)}, bf16[1280,1024]{1,0:T(8,128)(2,1)S(1)}, bf16[1280,1024]{1,0:T(8,128)(2,1)}) fusion(f32[1280,2048]{1,0:T(8,128)} %fusion.53, bf16[1024,2048]{1,0:T(8,128)(2,1)} %all-gather.20.cloned.1.call-done, bf16[1280,2048]{1,0:T(8,128)(2,1)} %all-gather.22.cloned.1.call-done, ...), kind=kOutput, calls=%fused_computation.21 | convolution fusion | flops 5390991360 | bytes 27788544 | tf_op jit(solution)/shard_map/dot_general | solution.py:44
  553.2 1.5 copy-done.35
  555.6 15.2 %convolution_convert_fusion.2 = bf16[1280,2048]{1,0:T(8,128)(2,1)} fusion(bf16[2048,2048]{1,0:T(8,128)(2,1)} %bitcast.177, bf16[1280,1024]{1,0:T(8,128)(2,1)S(1)} %get-tuple-element.17, bf16[1280,1024]{1,0:T(8,128)(2,1)S(1)} %get-tuple-element.16), kind=kOutput, calls=%fused_computation.14 | convolution fusion | flops 10750525440 | bytes 18874368 | tf_op jit(solution)/shard_map/dot_general | solution.py:44
  570.8 58.8 %reduce-scatter.16.cloned.1.call-done = bf16[160,2048]{1,0:T(8,128)(2,1)} async-done(((bf16[1280,2048]{1,0:T(8,128)(2,1)}), bf16[160,2048]{1,0:T(8,128)(2,1)}) %reduce-scatter.16.cloned.1.call-update) | async-done | bytes 655376 | tf_op jit(solution)/shard_map/reduce_scatter | solution.py:96
  629.6 1.8 fusion.35
  631.5 2.5 fusion.49
  634.1 16.7 %convolution_convert_fusion = bf16[2048,2048]{1,0:T(8,128)(2,1)} fusion(bf16[1280,2048]{1,0:T(8,128)(2,1)} %all-gather.16.cloned.1.call-done, bf16[1280,1024]{1,0:T(8,128)(2,1)} %copy-done.36, bf16[1280,1024]{1,0:T(8,128)(2,1)} %copy-done.35), kind=kOutput, calls=%fused_computation.12 | convolution fusion | flops 10752098304 | bytes 18874368 | tf_op jit(solution)/shard_map/dot_general | solution.py:40
  650.9 37.7 %all-gather.24.cloned.1.call-done = bf16[1280,2048]{1,0:T(8,128)(2,1)} async-done(((bf16[160,2048]{1,0:T(8,128)(2,1)}), bf16[1280,2048]{1,0:T(8,128)(2,1)}) %all-gather.24.cloned.1.call-update) | async-done | bytes 5242896 | tf_op jit(solution)/shard_map/all_gather | solution.py:93
  688.6 4.3 convolution_convert_fusion.8
  692.9 17.9 %multiply_reduce_fusion = (f32[4,1280]{1,0:T(4,128)S(1)}, f32[4,1280,1280]{1,2,0:T(8,128)}) fusion(f32[4,1280,1280]{1,2,0:T(8,128)} %get-tuple-element.48, f32[4,1280]{1,0:T(4,128)S(1)} %log_add_fusion, bf16[4,1280,64]{1,2,0:T(8,128)(2,1)S(1)} %bitcast.134, bf16[4,1280,64]{1,2,0:T(8,128)(2,1)S(1)} %bitcast.131), kind=kOutput, calls=%fused_computation.3 | convolution fusion | flops 858516480 | bytes 53780480 | tf_op jit(solution)/shard_map/hqd,hkd->hqk/dot_general | solution.py:81
  710.8 23.8 %multiply_convert_fusion = bf16[4,1280,1280]{1,2,0:T(8,128)(2,1)} fusion(f32[4,1280,1280]{1,2,0:T(8,128)} %get-tuple-element.50, f32[4,1280,1280]{1,2,0:T(8,128)} %get-tuple-element.48, f32[4,1280]{1,0:T(4,128)S(1)} %get-tuple-element.49, f32[4,1280]{1,0:T(4,128)S(1)} %log_add_fusion), kind=kLoop, calls=%fused_computation.2 | loop fusion | flops 26214400 | bytes 65576960 | tf_op jit(solution)/shard_map/convert_element_type | solution.py:84
  734.7 8.3 fusion.12
  743.0 10.0 fusion.11
  753.0 2.2 subtract_convert_fusion.1
  755.3 12.0 %fusion.16 = bf16[4,1280,64]{1,2,0:T(8,128)(2,1)S(1)} fusion(bf16[4,1280,64]{1,2,0:T(8,128)(2,1)S(1)} %bitcast.135, f32[4,1280,1280]{1,2,0:T(8,128)} %get-tuple-element.48, f32[4,1280]{1,0:T(4,128)S(1)} %log_add_fusion), kind=kOutput, calls=%fused_computation.35 | convolution fusion | flops 852295680 | bytes 27545600 | tf_op jit(solution)/shard_map/hqk,hqd->hkd/dot_general | solution.py:87
  767.4 6.3 convolution_convert_fusion.6
  773.8 10.8 convolution_convert_fusion.5
  785.6 5.6 convolution_convert_fusion.7
  791.3 9.0 convolution_convert_fusion.1
  800.3 10.0 convolution_convert_fusion.3
  810.3 52.8 %all_to_all.22 = bf16[8,64,2048]{2,1,0:T(8,128)(2,1)S(1)} all-to-all(bf16[8,64,2048]{2,1,0:T(8,128)(2,1)} %bitcast.149), channel_id=1, replica_groups=mesh['dp'=4,'fsdp'=8] {'fsdp'}, dimensions={0} | all-to-all | bytes 4194304 | tf_op jit(solution)/shard_map/all_to_all | solution.py:101
  863.2 4.2 all-to-all-start.2
  867.5 12.5 %reduce-scatter.26.cloned.1.call-done = bf16[256,2048]{1,0:T(8,128)(2,1)} async-done(((bf16[1024,2048]{1,0:T(8,128)(2,1)}), bf16[256,2048]{1,0:T(8,128)(2,1)}) %reduce-scatter.26.cloned.1.call-update) | async-done | bytes 1048592 | tf_op jit(solution)/shard_map/reduce_scatter | solution.py:195
  879.9 2.8 convert_element_type.301
  882.7 2.5 slice_convert_fusion.1
  885.2 2.4 reshape.330
  888.8 2.5 copy.80
  891.3 2.0 reshape.329
  893.3 2.9 copy.66
  896.2 2.5 copy.79
  898.7 11.8 reduce-scatter.22.cloned.1.call-done
  910.4 1.8 convert_element_type.290
  912.2 2.3 slice_convert_fusion.3
  916.7 1.5 reshape.327
  920.0 2.4 reshape.326
  922.4 3.0 copy.91
  925.4 2.4 reshape.321
  927.7 44.9 %reduce-scatter.18.cloned.1.call-done = bf16[160,2048]{1,0:T(8,128)(2,1)} async-done(((bf16[1280,2048]{1,0:T(8,128)(2,1)}), bf16[160,2048]{1,0:T(8,128)(2,1)}) %reduce-scatter.18.cloned.1.call-update) | async-done | bytes 655376 | tf_op jit(solution)/shard_map/reduce_scatter | solution.py:96
  972.7 1.7 fusion.37
  975.8 57.4 %reduce-scatter.14.cloned.1.call-done = bf16[160,2048]{1,0:T(8,128)(2,1)} async-done(((bf16[1280,2048]{1,0:T(8,128)(2,1)}), bf16[160,2048]{1,0:T(8,128)(2,1)}) %reduce-scatter.14.cloned.1.call-update) | async-done | bytes 655376 | tf_op jit(solution)/shard_map/reduce_scatter | solution.py:96
  1033.2 3.2 fusion.31
  1036.5 132.2 %reduce-scatter.28.cloned.1.call-done = f32[64,2]{1,0:T(8,128)} async-done(((f32[2048,2]{1,0:T(8,128)}), f32[64,2]{1,0:T(8,128)}) %reduce-scatter.28.cloned.1.call-update) | async-done | bytes 528
  (161 shorter events, 25.7 us)
Async XLA Ops:
  7.2 2.8 copy-start.27
  7.2 3.9 copy-start.28
  7.2 97.7 %all-gather.10.cloned.1.call-start = ((), (), s32[]{:S(2)}) async-start(), calls=%async_computation.13 | async-start | bytes 5898240 | tf_op jit(solution)/shard_map/all_gather | solution.py:93
  7.9 120.2 %all-gather.12.cloned.1.call-start = ((), (), s32[]{:S(2)}) async-start(), calls=%async_computation.14 | async-start | bytes 3932160 | tf_op jit(solution)/shard_map/all_gather | solution.py:160
  11.6 49.2 %copy-start.33 = (bf16[64]{0:T(256)(128)(2,1)S(1)}, bf16[64]{0:T(256)(128)(2,1)}, u32[]{:S(2)}) copy-start(bf16[64]{0:T(256)(128)(2,1)} %param.20) | copy-start | bytes 388
  11.6 49.2 %copy-start.34 = (bf16[64]{0:T(256)(128)(2,1)S(1)}, bf16[64]{0:T(256)(128)(2,1)}, u32[]{:S(2)}) copy-start(bf16[64]{0:T(256)(128)(2,1)} %param.15) | copy-start | bytes 388
  59.3 112.0 %all-gather.14.cloned.1.call-start = ((), (), s32[]{:S(2)}) async-start(), calls=%async_computation.15 | async-start | bytes 1310720 | tf_op jit(solution)/shard_map/all_gather | solution.py:136
  60.1 213.6 %reduce-scatter.12.cloned.1.call-start = ((), (), s32[]{:S(2)}) async-start(), calls=%async_computation.16 | async-start | bytes 5898240 | tf_op jit(solution)/shard_map/reduce_scatter | solution.py:96
  101.0 27.2 %copy-start.29 = (f32[2048,1]{0,1:T(1,128)}, f32[2048,1]{0,1:T(1,128)S(1)}, u32[]{:S(2)}) copy-start(f32[2048,1]{0,1:T(1,128)S(1)} %get-tuple-element.46) | copy-start | bytes 24580
  104.9 31.5 %copy-start.10 = (f32[1280,32]{0,1:T(8,128)}, f32[1280,32]{0,1:T(8,128)S(1)}, u32[]{:S(2)}) copy-start(f32[1280,32]{0,1:T(8,128)S(1)} %get-tuple-element.44) | copy-start | bytes 491524
  108.6 27.6 %copy-start.31 = (f32[1280]{0:T(1024)}, f32[1280]{0:T(1024)S(1)}, u32[]{:S(2)}) copy-start(f32[1280]{0:T(1024)S(1)} %add_rsqrt_fusion) | copy-start | bytes 15364
  136.4 1.8 copy-start.9
  136.8 12.6 %copy-start.14 = (bf16[1280,4,32]{0,2,1:T(8,128)(2,1)}, bf16[1280,4,32]{0,2,1:T(8,128)(2,1)S(1)}, u32[]{:S(2)}) copy-start(bf16[1280,4,32]{0,2,1:T(8,128)(2,1)S(1)} %get-tuple-element.27) | copy-start | bytes 983044
  136.8 12.6 %copy-start.16 = (bf16[1280,4,32]{0,2,1:T(8,128)(2,1)}, bf16[1280,4,32]{0,2,1:T(8,128)(2,1)S(1)}, u32[]{:S(2)}) copy-start(bf16[1280,4,32]{0,2,1:T(8,128)(2,1)S(1)} %get-tuple-element.28) | copy-start | bytes 983044
  136.8 12.6 %copy-start.18 = (bf16[1280,4,32]{0,2,1:T(8,128)(2,1)}, bf16[1280,4,32]{0,2,1:T(8,128)(2,1)S(1)}, u32[]{:S(2)}) copy-start(bf16[1280,4,32]{0,2,1:T(8,128)(2,1)S(1)} %get-tuple-element.38) | copy-start | bytes 983044
  136.9 12.6 %copy-start.20 = (bf16[1280,4,32]{0,2,1:T(8,128)(2,1)}, bf16[1280,4,32]{0,2,1:T(8,128)(2,1)S(1)}, u32[]{:S(2)}) copy-start(bf16[1280,4,32]{0,2,1:T(8,128)(2,1)S(1)} %get-tuple-element.39) | copy-start | bytes 983044
  171.3 5.4 copy-start.6
  176.7 1.2 copy-start.22
  176.7 192.3 %all-gather.18.cloned.1.call-start = ((), (), s32[]{:S(2)}) async-start(), calls=%async_computation.18 | async-start | bytes 10485760 | tf_op jit(solution)/shard_map/all_gather | solution.py:164
  185.4 88.3 %copy-start = (bf16[160,2048]{1,0:T(8,128)(2,1)S(1)}, bf16[160,2048]{1,0:T(8,128)(2,1)}, u32[]{:S(2)}) copy-start(bf16[160,2048]{1,0:T(8,128)(2,1)} %param.12) | copy-start | bytes 1966084
  271.3 155.9 %all-gather.16.cloned.1.call-start = ((), (), s32[]{:S(2)}) async-start(), calls=%async_computation.17 | async-start | bytes 5898240 | tf_op jit(solution)/shard_map/all_gather | solution.py:93
  277.3 203.3 %all-gather.20.cloned.1.call-start = ((), (), s32[]{:S(2)}) async-start(), calls=%async_computation.19 | async-start | bytes 5242880 | tf_op jit(solution)/shard_map/all_gather | solution.py:165
  278.0 260.2 %all-gather.22.cloned.1.call-start = ((), (), s32[]{:S(2)}) async-start(), calls=%async_computation.21 | async-start | bytes 5898240 | tf_op jit(solution)/shard_map/all_gather | solution.py:93
  278.8 350.9 %reduce-scatter.16.cloned.1.call-start = ((), (), s32[]{:S(2)}) async-start(), calls=%async_computation.22 | async-start | bytes 5898240 | tf_op jit(solution)/shard_map/reduce_scatter | solution.py:96
  553.2 1.5 copy-start.35
  553.2 2.4 copy-start.36
  570.7 58.9 %copy-start.1 = (bf16[160,2048]{1,0:T(8,128)(2,1)S(1)}, bf16[160,2048]{1,0:T(8,128)(2,1)}, u32[]{:S(2)}) copy-start(bf16[160,2048]{1,0:T(8,128)(2,1)} %reduce-scatter.12.cloned.1.call-done) | copy-start | bytes 1966084
  570.7 60.7 %copy-start.3 = (bf16[160,2048]{1,0:T(8,128)(2,1)S(1)}, bf16[160,2048]{1,0:T(8,128)(2,1)}, u32[]{:S(2)}) copy-start(bf16[160,2048]{1,0:T(8,128)(2,1)} %param.13) | copy-start | bytes 1966084
  570.8 117.8 %all-gather.24.cloned.1.call-start = ((), (), s32[]{:S(2)}) async-start(), calls=%async_computation.23 | async-start | bytes 5898240 | tf_op jit(solution)/shard_map/all_gather | solution.py:93
  634.0 176.3 %reduce-scatter.24.cloned.1.call-start = ((), (), s32[]{:S(2)}) async-start(), calls=%async_computation.27 | async-start | bytes 10485760 | tf_op jit(solution)/shard_map/reduce_scatter | solution.py:206
  650.8 212.4 %reduce-scatter.20.cloned.1.call-start = ((), (), s32[]{:S(2)}) async-start(), calls=%async_computation.25 | async-start | bytes 3932160 | tf_op jit(solution)/shard_map/reduce_scatter | solution.py:231
  710.8 23.8 %copy-start.19 = (bf16[1280,4,32]{0,2,1:T(8,128)(2,1)S(1)}, bf16[1280,4,32]{0,2,1:T(8,128)(2,1)}, u32[]{:S(2)}) copy-start(bf16[1280,4,32]{0,2,1:T(8,128)(2,1)} %copy-done.18) | copy-start | bytes 983044
  710.8 23.8 %copy-start.21 = (bf16[1280,4,32]{0,2,1:T(8,128)(2,1)S(1)}, bf16[1280,4,32]{0,2,1:T(8,128)(2,1)}, u32[]{:S(2)}) copy-start(bf16[1280,4,32]{0,2,1:T(8,128)(2,1)} %copy-done.20) | copy-start | bytes 983044
  734.7 8.3 copy-start.15
  734.7 8.3 copy-start.17
  743.0 10.0 copy-start.11
  743.0 10.0 copy-start.23
  753.0 14.4 %slice-start = ((s8[5242880]{0:T(1024)(128)(4,1)}), s8[4194304]{0:T(1024)(128)(4,1)S(1)}, s32[]{:S(2)}) async-start(s8[5242880]{0:T(1024)(128)(4,1)} %bitcast.140), calls=%async_computation.30 | async-start | bytes 8388608
  755.2 12.1 %copy-start.24 = (bf16[1280,4,64]{0,2,1:T(8,128)(2,1)}, bf16[1280,4,64]{0,2,1:T(8,128)(2,1)S(1)}, u32[]{:S(2)}) copy-start(bf16[1280,4,64]{0,2,1:T(8,128)(2,1)S(1)} %get-tuple-element.51) | copy-start | bytes 1966084
  755.2 12.1 %copy-start.26 = (bf16[1280,4,64]{0,2,1:T(8,128)(2,1)}, bf16[1280,4,64]{0,2,1:T(8,128)(2,1)S(1)}, u32[]{:S(2)}) copy-start(bf16[1280,4,64]{0,2,1:T(8,128)(2,1)S(1)} %get-tuple-element.52) | copy-start | bytes 1966084
  755.3 12.1 %slice-start.1 = ((s8[5242880]{0:T(1024)(128)(4,1)}), s8[1048576]{0:T(1024)(128)(4,1)S(1)}, s32[]{:S(2)}) async-start(s8[5242880]{0:T(1024)(128)(4,1)} %bitcast.140), calls=%async_computation.31 | async-start | bytes 2097152
  755.3 12.1 %copy-start.30 = (f32[2048,1]{0,1:T(1,128)S(1)}, f32[2048,1]{0,1:T(1,128)}, u32[]{:S(2)}) copy-start(f32[2048,1]{0,1:T(1,128)} %copy-done.29) | copy-start | bytes 24580
  755.3 12.1 %copy-start.32 = (f32[1280]{0:T(1024)S(1)}, f32[1280]{0:T(1024)}, u32[]{:S(2)}) copy-start(f32[1280]{0:T(1024)} %copy-done.31) | copy-start | bytes 15364
  767.3 6.4 copy-start.12
  773.7 106.2 %reduce-scatter.26.cloned.1.call-start = ((), (), s32[]{:S(2)}) async-start(), calls=%async_computation.28 | async-start | bytes 5242880 | tf_op jit(solution)/shard_map/reduce_scatter | solution.py:195
  784.5 1.1 copy-start.7
  784.6 6.7 copy-start.13
  784.6 6.7 copy-start.25
  784.6 125.9 %reduce-scatter.22.cloned.1.call-start = ((), (), s32[]{:S(2)}) async-start(), calls=%async_computation.26 | async-start | bytes 1310720 | tf_op jit(solution)/shard_map/reduce_scatter | solution.py:148
  791.2 181.4 %reduce-scatter.18.cloned.1.call-start = ((), (), s32[]{:S(2)}) async-start(), calls=%async_computation.24 | async-start | bytes 5898240 | tf_op jit(solution)/shard_map/reduce_scatter | solution.py:96
  800.3 232.9 %reduce-scatter.14.cloned.1.call-start = ((), (), s32[]{:S(2)}) async-start(), calls=%async_computation.20 | async-start | bytes 5898240 | tf_op jit(solution)/shard_map/reduce_scatter | solution.py:96
  863.2 49.0 %all-to-all-start.2 = ((bf16[8,64,768]{2,1,0:T(8,128)(2,1)}), bf16[8,64,768]{2,1,0:T(8,128)(2,1)}, u32[]{:S(2)}, u32[]{:S(2)}) async-start(bf16[8,64,768]{2,1,0:T(8,128)(2,1)} %bitcast.159), calls=%async_computation.7 | async-start | bytes 1572864 | tf_op jit(solution)/shard_map/all_to_all | solution.py:101
  867.4 301.3 %reduce-scatter.28.cloned.1.call-start = ((), (), s32[]{:S(2)}) async-start(), calls=%async_computation.29 | async-start | bytes 1081344
  888.8 2.5 copy-start.2
  922.4 110.8 %copy-start.4 = (bf16[160,2048]{1,0:T(8,128)(2,1)S(1)}, bf16[160,2048]{1,0:T(8,128)(2,1)}, u32[]{:S(2)}) copy-start(bf16[160,2048]{1,0:T(8,128)(2,1)} %param.13) | copy-start | bytes 1966084
  922.4 110.8 %copy-start.5 = (bf16[160,2048]{1,0:T(8,128)(2,1)S(1)}, bf16[160,2048]{1,0:T(8,128)(2,1)}, u32[]{:S(2)}) copy-start(bf16[160,2048]{1,0:T(8,128)(2,1)} %reduce-scatter.16.cloned.1.call-done) | copy-start | bytes 1966084
  972.7 60.6 %copy-start.8 = (bf16[160,2048]{1,0:T(8,128)(2,1)S(1)}, bf16[160,2048]{1,0:T(8,128)(2,1)}, u32[]{:S(2)}) copy-start(bf16[160,2048]{1,0:T(8,128)(2,1)} %reduce-scatter.18.cloned.1.call-done) | copy-start | bytes 1966084
Sparse Core Ops, SparseCore 0:
  9.7 73.5 all-gather.9
  85.1 42.9 all-gather.11
  130.0 26.6 all-gather.13
  176.9 96.7 reduce-scatter.11
  275.4 93.6 all-gather.17
  371.1 56.0 all-gather.15
  429.0 51.4 all-gather.19
  482.2 56.0 all-gather.21
  570.9 58.6 reduce-scatter.15
  634.1 54.3 all-gather.23
  691.6 85.1 reduce-scatter.23
  780.0 43.9 reduce-scatter.19
  827.2 52.6 reduce-scatter.25
  882.7 27.7 reduce-scatter.21
  912.7 59.9 reduce-scatter.17
  974.9 58.2 reduce-scatter.13
  1035.4 133.2 reduce-scatter.27

commit v2 on v1

v2 whole, which is shorter than its diff:
```python
import functools

import jax
import jax.numpy as jnp
from jax import lax
from jax.experimental import pallas as pl
from jax.experimental.pallas import tpu as pltpu
from jax.sharding import PartitionSpec as P

HEADS = 32
HEAD_DIM = 64


EPSILON = 1e-05
THETA = 130000.0
BF16 = jnp.bfloat16
F32 = jnp.float32


def dot(left, right):
    return jnp.dot(left, right, preferred_element_type=F32)


def rows_inner(left, right):
    return lax.dot_general(left, right, (((0,), (0,)), ((), ())), preferred_element_type=F32)


def cols_inner(left, right):
    return lax.dot_general(left, right, (((1,), (1,)), ((), ())), preferred_element_type=F32)


def inverse_rms(values):
    return lax.rsqrt(jnp.mean(values * values, -1, keepdims=True) + EPSILON)


def norm_back(grad_scaled, scaled, scale):
    return scale * (grad_scaled - scaled * jnp.mean(grad_scaled * scaled, -1, keepdims=True))


BLOCK = 256
SCALE = 0.125


def turn_halves(values, cosine, sine):
    width = values.shape[1]
    half = HEAD_DIM // 2
    lane = lax.broadcasted_iota(jnp.int32, values.shape, 1)
    ahead = pltpu.roll(values, width - half, 1)
    behind = pltpu.roll(values, half, 1)
    return values * cosine + jnp.where(lane % HEAD_DIM < half, ahead, behind) * sine


def wide_tables(count, width):
    half = HEAD_DIM // 2
    inverse = THETA ** (-jnp.arange(half, dtype=F32) * 2.0 / HEAD_DIM)
    angles = jnp.arange(count, dtype=jnp.int32).astype(F32)[:, None] * inverse[None, :]
    cosine, sine = jnp.cos(angles), jnp.sin(angles)
    repeats = width // HEAD_DIM
    return (
        jnp.tile(jnp.concatenate([cosine, cosine], -1), (1, repeats)),
        jnp.tile(jnp.concatenate([-sine, sine], -1), (1, repeats)),
    )


def head_rows(values, head):
    row = lax.broadcasted_iota(jnp.int32, values.shape, 0)
    return jnp.where((row >= head * HEAD_DIM) & (row < (head + 1) * HEAD_DIM), values, 0.0)


def future(shape):
    return lax.broadcasted_iota(jnp.int32, shape, 0) > lax.broadcasted_iota(jnp.int32, shape, 1)


def attend_block(i, rank_heads, queries, keys, values_t, bias, attended, log_totals):
    queries_t = queries.T
    masked = [(head_rows(queries_t, h) * SCALE).astype(BF16) for h in range(rank_heads)]

    def chunk(j, carry, last):
        part = pl.ds(pl.multiple_of(j * BLOCK, BLOCK), BLOCK)
        key_part, bias_part = keys[part, :], bias[part, :]
        after = []
        for h in range(rank_heads):
            top, total, out = carry[h]
            scores = dot(key_part, masked[h]) + bias_part
            if last:
                scores = jnp.where(future(scores.shape), -1000000000.0, scores)
            new_top = jnp.maximum(top, jnp.max(scores, 0, keepdims=True))
            keep = jnp.exp(top - new_top)
            weights = jnp.exp(scores - new_top)
            total = total * keep + jnp.sum(weights, 0, keepdims=True)
            out = out * keep + dot(
                values_t[j, h * HEAD_DIM : (h + 1) * HEAD_DIM, :], weights.astype(BF16)
            )
            after.append((new_top, total, out))
        return tuple(after)

    carry = tuple(
        (
            jnp.full((1, BLOCK), -3.0e38, F32),
            jnp.zeros((1, BLOCK), F32),
            jnp.zeros((HEAD_DIM, BLOCK), F32),
        )
        for _ in range(rank_heads)
    )
    carry = lax.fori_loop(0, i, lambda j, c: chunk(j, c, False), carry)
    carry = chunk(i, carry, True)
    outs = []
    for h, (top, total, out) in enumerate(carry):
        log_totals[i, h : h + 1, :] = top + jnp.log(total)
        outs.append(out * (1.0 / total))
    attended[pl.ds(pl.multiple_of(i * BLOCK, BLOCK), BLOCK), :] = (
        jnp.concatenate(outs, 0).T.astype(BF16)
    )


def project_block(i, x, gain, qkv, cosine, sine, normed, queries, keys, values, values_t):
    cols = queries.shape[1]
    start = i * BLOCK

    def rows_of(part):
        rows = x[part, :].astype(F32)
        normed[part, :] = (rows * inverse_rms(rows) * gain[...]).astype(BF16)

    pl.loop(0, BLOCK // 16)(
        lambda t: rows_of(pl.ds(pl.multiple_of(start + t * 16, 16), 16))
    )
    block = pl.ds(pl.multiple_of(start, BLOCK), BLOCK)
    rows = normed[block, :]
    cos, sin = cosine[block, :], sine[block, :]
    rounded = turn_halves(dot(rows, qkv[:, :cols]), cos, sin).astype(BF16)
    queries[block, :] = rounded
    keys[block, :] = turn_halves(dot(rows, qkv[:, cols : 2 * cols]), cos, sin).astype(BF16)
    value = dot(rows, qkv[:, 2 * cols :])
    values[block, :] = value.astype(BF16)
    values_t[i] = value.T.astype(BF16)
    return rounded.astype(F32)


def matmul_block(i, left, right, out, step=512):
    block = pl.ds(pl.multiple_of(i * BLOCK, BLOCK), BLOCK)
    rows = left[block, :]

    @pl.loop(0, right.shape[1] // step)
    def _(c):
        part = pl.ds(pl.multiple_of(c * step, step), step)
        out[block, part] = dot(rows, right[:, part]).astype(out.dtype)


def lanes_of(values, head):
    lane = lax.broadcasted_iota(jnp.int32, values.shape, 1)
    return jnp.where((lane >= head * HEAD_DIM) & (lane < (head + 1) * HEAD_DIM), values, 0.0)


def attend_back_block(
    i, rank_heads, queries, keys, keys_t, values, attended, grad, bias, log_totals, grad_keys, grad_values
):
    block = pl.ds(pl.multiple_of(i * BLOCK, BLOCK), BLOCK)
    query = queries[block, :].astype(F32) * SCALE
    query_t, grad_t = query.T, grad.T
    product = attended[block, :].astype(F32).T * grad_t
    masked_q = [head_rows(query_t, h).astype(BF16) for h in range(rank_heads)]
    masked_g = [head_rows(grad_t, h).astype(BF16) for h in range(rank_heads)]
    stacked_q = jnp.concatenate([lanes_of(query, h).astype(BF16) for h in range(rank_heads)], 0)
    stacked_g = jnp.concatenate([lanes_of(grad, h).astype(BF16) for h in range(rank_heads)], 0)
    deltas = [
        jnp.sum(product[h * HEAD_DIM : (h + 1) * HEAD_DIM], 0, keepdims=True)
        for h in range(rank_heads)
    ]
    totals = [log_totals[i, h : h + 1, :] for h in range(rank_heads)]

    def chunk(j, carry, last):
        part = pl.ds(pl.multiple_of(j * BLOCK, BLOCK), BLOCK)
        key_part, value_part, bias_part = keys[part, :], values[part, :], bias[part, :]
        after, weights_all, grads_all = [], [], []
        for h in range(rank_heads):
            scores = dot(key_part, masked_q[h]) + bias_part
            if last:
                scores = jnp.where(future(scores.shape), -1000000000.0, scores)
            weights = jnp.exp(scores - totals[h])
            grad_scores = weights * (dot(value_part, masked_g[h]) - deltas[h])
            weights_all.append(weights.astype(BF16))
            grads_all.append(grad_scores.astype(BF16))
            after.append(
                carry[h] + dot(keys_t[j, h * HEAD_DIM : (h + 1) * HEAD_DIM, :], grads_all[-1])
            )
        grad_values[part, :] += dot(jnp.concatenate(weights_all, 1), stacked_g)
        grad_keys[part, :] += dot(jnp.concatenate(grads_all, 1), stacked_q)
        return tuple(after)

    carry = tuple(jnp.zeros((HEAD_DIM, BLOCK), F32) for _ in range(rank_heads))
    carry = lax.fori_loop(0, i, lambda j, c: chunk(j, c, False), carry)
    carry = chunk(i, carry, True)
    return jnp.concatenate(carry, 0).T * SCALE


def attend_back_rows(
    i, rank_heads, grad_hidden, out_w, queries, keys, keys_t, values, attended, bias, log_totals,
    cosine, sine, grad_keys, grad_values, grad_qkv,
):
    block = pl.ds(pl.multiple_of(i * BLOCK, BLOCK), BLOCK)
    cols = queries.shape[1]
    grad = cols_inner(grad_hidden[block, :], out_w[...]).astype(BF16).astype(F32)
    grad_q = attend_back_block(
        i, rank_heads, queries, keys, keys_t, values, attended, grad, bias, log_totals, grad_keys, grad_values
    )
    grad_qkv[block, :cols] = turn_halves(grad_q, cosine[block, :], -sine[block, :]).astype(BF16)


def finish_back_rows(i, qkv, cosine, sine, grad_keys, grad_values, grad_qkv, parts):
    block = pl.ds(pl.multiple_of(i * BLOCK, BLOCK), BLOCK)
    cols = grad_keys.shape[1]
    grad_qkv[block, cols : 2 * cols] = turn_halves(
        grad_keys[block, :], cosine[block, :], -sine[block, :]
    ).astype(BF16)
    grad_qkv[block, 2 * cols :] = grad_values[block, :].astype(BF16)
    rows = grad_qkv[block, :]
    step = 512

    @pl.loop(0, qkv.shape[0] // step)
    def _(c):
        part = pl.ds(pl.multiple_of(c * step, step), step)
        parts[block, part] = cols_inner(rows, qkv[part, :]).astype(BF16)

MESH = pl.DeviceIdType.MESH


def when(cond, action):
    if cond is None:
        action()
    else:
        pl.when(cond)(action)


class Links:
    def __init__(self, groups, ranks, sends, recvs):
        self.groups, self.ranks, self.chips = groups, ranks, ranks // 2
        self.bits = groups.bit_length() - 1
        self.sends, self.recvs = sends, recvs
        self.used_sends = self.used_recvs = 0
        self.d, self.f = lax.axis_index("dp"), lax.axis_index("fsdp")
        self.z, self.c = lax.div(self.f, 2), lax.rem(self.f, 2)
        self.sibling = (self.d, self.z * 2 + 1 - self.c)
        self.pending = []

    def bit(self, b):
        return lax.rem(lax.div(self.d, 1 << b), 2)

    def partner(self, b):
        return (self.d + (1 - 2 * self.bit(b)) * (1 << b), self.f)

    def beside(self, way):
        return (self.d, self.f + 2 * way)

    def barrier(self):
        gate = pltpu.get_barrier_semaphore()
        for k in range(1, self.ranks):
            other = lax.rem(self.f + k, self.ranks)
            pl.semaphore_signal(gate, inc=1, device_id=(self.d, other), device_id_type=MESH)
        for k in range(1, self.groups):
            other = lax.rem(self.d + k, self.groups)
            pl.semaphore_signal(gate, inc=1, device_id=(other, self.f), device_id_type=MESH)
        pl.semaphore_wait(gate, self.ranks + self.groups - 2)

    def take(self, sends, recvs):
        first = (self.used_sends, self.used_recvs)
        self.used_sends += sends
        self.used_recvs += recvs
        return first

    def copy(self, source, target, send, recv, device):
        return pltpu.make_async_remote_copy(
            src_ref=source,
            dst_ref=target,
            send_sem=self.sends.at[send],
            recv_sem=self.recvs.at[recv],
            device_id=device,
            device_id_type=MESH,
        )

    def send(self, cond, source, target, send, recv, device, later=True):
        when(cond, lambda: self.copy(source, target, send, recv, device).start())
        gone = lambda: when(
            cond, lambda: self.copy(source, target, send, recv, device).wait_send()
        )
        if later:
            self.pending.append(gone)
        return gone

    def arrived(self, cond, target, recv):
        when(cond, lambda: self.copy(target, target, 0, recv, self.sibling).wait_recv())

    def move(self, source, target):
        send, _ = self.take(1, 0)
        make = lambda: pltpu.make_async_copy(source, target, self.sends.at[send])
        make().start()
        return lambda: make().wait()

    def finish(self):
        for wait in self.pending:
            wait()
        self.pending = []


class LineGather:
    def __init__(self, links, view):
        self.links, self.view = links, view
        chips = links.chips
        self.sends, self.recvs = links.take(3 * chips, 3 * chips)

    def start(self, source):
        k, chips = self.links, self.links.chips
        target = self.view(k.f)
        for side, way in enumerate((1, -1)):
            valid = (k.z + way >= 0) & (k.z + way < chips)
            k.send(
                valid, source, target, self.sends + side * chips, self.recvs + side * chips + 1, k.beside(way)
            )
        k.send(
            None, source, target, self.sends + 2 * chips + k.z, self.recvs + 2 * chips + k.z, k.sibling
        )

    def step(self, reach):
        k, chips = self.links, self.links.chips
        for side, way in enumerate((1, -1)):
            origin = k.z - way * reach
            here = (origin >= 0) & (origin < chips)
            block = self.view(origin * 2 + k.c)
            k.arrived(here, block, self.recvs + side * chips + reach)
            if reach + 1 < chips:
                onward = here & (k.z + way >= 0) & (k.z + way < chips)
                k.send(
                    onward,
                    block,
                    block,
                    self.sends + side * chips + reach,
                    self.recvs + side * chips + reach + 1,
                    k.beside(way),
                )
            k.send(
                here,
                block,
                block,
                self.sends + 2 * chips + origin,
                self.recvs + 2 * chips + origin,
                k.sibling,
            )

    def finish(self):
        k, chips = self.links, self.links.chips
        for chip in range(chips):
            k.arrived(None, self.view(chip * 2 + 1 - k.c), self.recvs + 2 * chips + chip)


def add_rows(target, *sources, step=16):
    rows = target.shape[0]

    @pl.loop(0, rows // step)
    def _(i):
        part = pl.ds(pl.multiple_of(i * step, step), step)
        total = sources[0][part].astype(F32)
        for source in sources[1:]:
            total = total + source[part].astype(F32)
        target[part] = total.astype(target.dtype)


class LineScatter:
    def __init__(self, links, parts, mine, held, landed):
        self.links, self.parts, self.mine = links, parts, mine
        self.held, self.landed = held, landed
        chips = links.chips
        self.sends, self.recvs = links.take(2 * chips, 3 * chips)
        self.gone = [lambda: None] * 2

    def start(self):
        k, chips = self.links, self.links.chips
        for chip in range(chips):
            k.send(
                None,
                self.parts(chip * 2 + 1 - k.c),
                self.held(chip),
                self.sends + chip,
                self.recvs + chip,
                k.sibling,
            )
        self.own = [k.move(self.parts(chip * 2 + k.c), self.mine(chip)) for chip in range(chips)]

    def pair(self):
        k = self.links
        for chip in range(k.chips):
            self.own[chip]()
            k.arrived(None, self.held(chip), self.recvs + chip)
            add_rows(self.held(chip), self.held(chip), self.mine(chip))

    def step(self, i):
        k, chips = self.links, self.links.chips
        for side, way in enumerate((1, -1)):
            chip = k.z + way * (chips - 1 - i)
            before = (chip >= 0) & (chip < chips)
            inner = before & (k.z > 0 if way > 0 else k.z < chips - 1)
            mine = self.recvs + (1 + side) * chips + chip

            def add():
                k.arrived(None, self.landed(side, chip), mine)
                add_rows(self.held(chip), self.held(chip), self.landed(side, chip))

            pl.when(inner)(add)
            self.gone[side]()
            self.gone[side] = k.send(
                before,
                self.held(chip),
                self.landed(side, chip),
                self.sends + chips + chip,
                mine,
                k.beside(way),
                later=False,
            )

    def last(self):
        k, chips = self.links, self.links.chips
        for side, inner in enumerate((k.z > 0, k.z < chips - 1)):

            def add():
                k.arrived(None, self.landed(side, k.z), self.recvs + (1 + side) * chips + k.z)
                add_rows(self.held(k.z), self.held(k.z), self.landed(side, k.z))

            pl.when(inner)(add)
        for gone in self.gone:
            gone()


class Exchange:
    def __init__(self, links):
        self.links = links
        self.sends, self.recvs = links.take(links.ranks, links.ranks)

    def start(self, source, target):
        k = self.links
        self.own = k.move(source(k.f), target(k.f))
        for i in range(1, k.ranks):
            other = lax.rem(k.f + i, k.ranks)
            k.send(
                None, source(other), target(k.f), self.sends + other, self.recvs + k.f, (k.d, other)
            )

    def finish(self, target, own=True):
        k = self.links
        if own:
            self.own()
        for i in range(1, k.ranks):
            other = lax.rem(k.f + i, k.ranks)
            k.arrived(None, target(other), self.recvs + other)

    def start_piece(self, rank, source, target):
        k = self.links
        k.send(
            k.f != rank, source, target(k.f), self.sends + rank, self.recvs + k.f, (k.d, rank)
        )
        here = lambda: pltpu.make_async_copy(source, target(k.f), k.sends.at[self.sends + rank])
        pl.when(k.f == rank)(lambda: here().start())
        k.pending.append(lambda: pl.when(k.f == rank)(lambda: here().wait()))


def spread_bits(base, bits):
    places = [base]
    for b, own in bits:
        places = places + [place + (1 - 2 * own) * (1 << b) for place in places]
    return places


class GroupGather:
    def __init__(self, links, view):
        self.links, self.view = links, view
        count = links.groups - 1
        self.sends, self.recvs = links.take(2 * count, 2 * count)

    def order(self, half):
        bits = list(range(self.links.bits))
        return bits if half == 0 else bits[::-1]

    def base(self, half, stage):
        return half * (self.links.groups - 1) + (1 << stage) - 1

    def start(self, half, stage, source=None):
        k = self.links
        order = self.order(half)
        blocks = spread_bits(k.d, [(b, k.bit(b)) for b in order[:stage]])
        for i, block in enumerate(blocks):
            at = self.base(half, stage) + i
            target = self.view(block, half)
            k.send(
                None,
                target if source is None else source(half),
                target,
                self.sends + at,
                self.recvs + at,
                k.partner(order[stage]),
            )

    def wait(self, half, stage):
        k = self.links
        order = self.order(half)
        far = k.partner(order[stage])[0]
        blocks = spread_bits(far, [(b, k.bit(b)) for b in order[:stage]])
        for i, block in enumerate(blocks):
            k.arrived(None, self.view(block, half), self.recvs + self.base(half, stage) + i)


class GroupScatter:
    def __init__(self, links, view, landed, high):
        self.links, self.view, self.landed = links, view, landed
        bits = list(range(links.bits))
        self.order = bits[::-1] if high else bits
        count = links.groups - 1
        self.sends, self.recvs = links.take(count, count)

    def base(self, stage):
        return sum(self.links.groups >> (s + 1) for s in range(stage))

    def sources(self, stage, flip):
        k = self.links
        b = self.order[stage]
        value = 1 - k.bit(b) if flip else k.bit(b)
        if stage > 0:
            count = k.groups >> (stage + 1)
            return [self.landed(self.base(stage - 1) + value + 2 * i) for i in range(count)]
        places = [value * (1 << b)]
        for b in self.order[1:]:
            places = places + [place + (1 << b) for place in places]
        return [self.view(place) for place in places]

    def start(self, stage):
        k = self.links
        for i, source in enumerate(self.sources(stage, True)):
            at = self.base(stage) + i
            k.send(
                None,
                source,
                self.landed(at),
                self.sends + at,
                self.recvs + at,
                k.partner(self.order[stage]),
            )

    def wait(self, stage, target=None):
        k = self.links
        for i, source in enumerate(self.sources(stage, False)):
            at = self.base(stage) + i
            k.arrived(None, self.landed(at), self.recvs + at)
            add_rows(self.landed(at) if target is None else target, source, self.landed(at))
        return self.landed(self.base(stage))


def row_loop(rows, action, step=16, first=0):
    @pl.loop(0, rows // step)
    def _(i):
        action(pl.ds(pl.multiple_of(first + i * step, step), step))


def halved(ref, count):
    return lambda group, half: ref.at[group, pl.ds(half * count, count)]


def first_kernel(
    groups, ranks, tokens, qkv_out, gains, out_w, down_w,
    x_all, qkv, gains_all, out_all, down_all, sends, recvs,
):
    k = Links(groups, ranks, sends, recvs)
    x_line = LineGather(k, lambda rank: x_all.at[rank])
    gains_ex, qkv_ex = Exchange(k), Exchange(k)
    out_half, down_half = out_w.shape[0] // 2, down_w.shape[0] // 2
    early = [
        (GroupGather(k, halved(out_all, out_half)), lambda h: out_w.at[pl.ds(h * out_half, out_half)]),
        (GroupGather(k, halved(down_all, down_half)), lambda h: down_w.at[pl.ds(h * down_half, down_half)]),
    ]
    late = [GroupGather(k, halved(qkv, ranks // 2)), GroupGather(k, halved(gains_all, ranks // 2))]
    k.barrier()
    gains_in = lambda rank: gains_all.at[k.d, rank]
    qkv_in = lambda rank: qkv.at[k.d, rank]
    gains_ex.start(lambda rank: gains, gains_in)
    qkv_ex.start(lambda rank: qkv_out.at[rank], qkv_in)
    for gather, source in early:
        for half in range(2):
            gather.start(half, 0, source)
    own = [
        k.move(tokens, x_all.at[k.f]),
        k.move(out_w, out_all.at[k.d]),
        k.move(down_w, down_all.at[k.d]),
    ]
    x_line.start(tokens)
    gains_ex.finish(gains_in)
    qkv_ex.finish(qkv_in)
    for gather in late:
        for half in range(2):
            gather.start(half, 0)
    for wait in own:
        wait()
    early = [gather for gather, _ in early]
    x_line.step(1)
    for gather in early:
        for half in range(2):
            gather.wait(half, 0)
            gather.start(half, 1)
    for reach in range(2, k.chips):
        x_line.step(reach)
        if reach == 2:
            for gather in late:
                for half in range(2):
                    gather.wait(half, 0)
                    gather.start(half, 1)
    for stage in range(1, k.bits):
        for gather in late + early:
            for half in range(2):
                gather.wait(half, stage)
                if stage + 1 < k.bits:
                    gather.start(half, stage + 1)
    x_line.finish()
    k.finish()


def spaced(events, blocks):
    count = len(events)
    return [events[b * count // blocks : (b + 1) * count // blocks] for b in range(blocks)]


def attend_kernel(
    groups, ranks, rank_heads, x_all, cotangent, gate_up_out, qkv, gain, out_w, cosine, sine, bias,
    parts, normed, queries, keys, values, attended, log_totals, cotangent_all, gate_up,
    values_t, sends, recvs,
):
    k = Links(groups, ranks, sends, recvs)
    depth = gate_up_out.shape[1]
    pieces = depth // 16
    exchanges = [Exchange(k) for _ in range(pieces)]
    gathers = [
        GroupGather(
            k,
            lambda group, half, q=q: gate_up.at[
                group, pl.ds(half * (ranks // 2), ranks // 2), pl.ds(q * 16, 16)
            ],
        )
        for q in range(pieces)
    ]
    line = LineGather(k, lambda rank: cotangent_all.at[rank])
    k.barrier()
    own = k.move(cotangent, cotangent_all.at[k.f])

    def send_out(q):
        part = pl.ds(q * 16, 16)
        exchanges[q].start(
            lambda rank: gate_up_out.at[rank, part], lambda rank: gate_up.at[k.d, rank, part]
        )

    def came_in(q):
        exchanges[q].finish(lambda rank: gate_up.at[k.d, rank, pl.ds(q * 16, 16)])
        for half in range(2):
            gathers[q].start(half, 0)

    def onward(q, stage):
        for half in range(2):
            gathers[q].wait(half, stage)
            if stage + 1 < k.bits:
                gathers[q].start(half, stage + 1)

    events = []
    for q in range(pieces):
        events.append([lambda q=q: came_in(q)])
        if q + 2 < pieces:
            events[-1].append(lambda q=q: send_out(q + 2))
        if q > 0:
            events[-1].append(lambda q=q: onward(q - 1, 0))
        if q == pieces - 2 or pieces == 1:
            events[-1].append(lambda: line.start(cotangent))
    events.append([lambda: line.step(1), lambda: onward(pieces - 1, 0)])
    for q in range(min(2, pieces)):
        send_out(q)
    blocks = values_t.shape[0]
    plan = spaced(events, blocks)
    for i in range(blocks):
        query = project_block(
            i, x_all, gain, qkv, cosine, sine, normed, queries, keys, values, values_t
        )
        attend_block(i, rank_heads, query, keys, values_t, bias, attended, log_totals)
        matmul_block(i, attended, out_w, parts)
        for event in plan[i]:
            for action in event:
                action()
    for reach in range(2, k.chips):
        line.step(reach)
    for stage in range(1, k.bits):
        for q in range(pieces):
            onward(q, stage)
    own()
    line.finish()
    k.finish()


def sub_lines(k, subs, rows, parts, mine, held, landed, gathered):
    scatters, gathers = [], []
    for sub in range(subs):
        part = pl.ds(sub * rows, rows)
        scatters.append(
            LineScatter(
                k,
                lambda rank, part=part: parts.at[rank, part],
                lambda chip, part=part: mine.at[chip, part],
                lambda chip, part=part: held.at[chip, part],
                lambda side, chip, part=part: landed.at[side, chip, part],
            )
        )
        gathers.append(LineGather(k, lambda rank, part=part: gathered.at[rank, part]))
    return scatters, gathers


def hidden_kernel(groups, ranks, subs, parts, tokens, gain, hidden, normed_all, mine, held, landed, normed, sends, recvs):
    k = Links(groups, ranks, sends, recvs)
    rows = tokens.shape[0] // subs
    scatters, gathers = sub_lines(k, subs, rows, parts, mine, held, landed, normed_all)
    k.barrier()
    for scatter in scatters:
        scatter.start()
    own = []
    for turn in range(subs + 1):
        if turn < subs:
            scatters[turn].pair()
        for i in range(k.chips - 1):
            if turn < subs:
                scatters[turn].step(i)
            if turn > 0:
                gathers[turn - 1].step(i + 1)
        if turn < subs:
            scatters[turn].last()

            def rows_of(part):
                total = tokens[part].astype(F32) + held[k.z, part].astype(F32)
                hidden[part] = total
                scaled = total * inverse_rms(total)
                normed[part] = (scaled * gain[...]).astype(BF16)

            row_loop(rows, rows_of, first=turn * rows)
            piece = pl.ds(turn * rows, rows)
            gathers[turn].start(normed.at[piece])
            own.append(k.move(normed.at[piece], normed_all.at[k.f, piece]))
    for gather in gathers:
        gather.finish()
    for wait in own:
        wait()
    k.finish()


def middle_kernel(
    groups, ranks, subs, parts, hidden, grad_out, gain, grad_gate_up,
    grad_all, grad_hidden, sums, gate_up_sum,
    mine, held, landed, rounded, gate_up_landed, sends, recvs,
):
    k = Links(groups, ranks, sends, recvs)
    rows = hidden.shape[0] // subs
    scatters, gathers = sub_lines(k, subs, rows, parts, mine, held, landed, grad_all)
    gate_up_sums = [
        GroupScatter(
            k,
            lambda group, n=n: grad_gate_up.at[group, n],
            lambda i, n=n: gate_up_landed.at[n, i],
            n % 2 == 1,
        )
        for n in range(ranks)
    ]
    k.barrier()
    for scatter in scatters:
        scatter.start()
    for sums_of in gate_up_sums:
        sums_of.start(0)
    sums[...] = jnp.zeros_like(sums)

    def rows_of(part):
        total = hidden[part]
        scale = inverse_rms(total)
        scaled = total * scale
        grad = held[k.z, part].astype(F32)
        sums[...] += jnp.sum(grad * scaled, 0, keepdims=True)
        grad_total = grad_out[part].astype(F32) + norm_back(grad * gain[...], scaled, scale)
        grad_hidden[part] = grad_total
        rounded[part] = grad_total.astype(BF16)

    own = []
    for turn in range(subs + 1):
        if turn < subs:
            scatters[turn].pair()
        for i in range(k.chips - 1):
            if turn < subs:
                scatters[turn].step(i)
            if turn > 0:
                gathers[turn - 1].step(i + 1)
        if turn < subs:
            scatters[turn].last()
            row_loop(rows, rows_of, first=turn * rows)
            piece = pl.ds(turn * rows, rows)
            gathers[turn].start(rounded.at[piece])
            own.append(k.move(rounded.at[piece], grad_all.at[k.f, piece]))
        if turn == subs - 1:
            for sums_of in gate_up_sums:
                sums_of.wait(0)
                sums_of.start(1)
    for stage in range(1, k.bits):
        for n, sums_of in enumerate(gate_up_sums):
            if stage + 1 < k.bits:
                sums_of.wait(stage)
                sums_of.start(stage + 1)
            else:
                sums_of.wait(stage, gate_up_sum.at[n])
    for gather in gathers:
        gather.finish()
    for wait in own:
        wait()
    k.finish()


def attend_back_kernel(
    groups, ranks, rank_heads, grad_hidden, out_w, queries, keys, values, attended, bias, log_totals,
    cosine, sine, qkv, normed, gate_up_sum, grad_down,
    parts, grad_qkv_w, grad_out_w, gate_up_grad, down_grad,
    grad_qkv, keys_t, grad_keys, grad_values, down_landed, sends, recvs,
):
    k = Links(groups, ranks, sends, recvs)
    pieces = down_landed.shape[0]
    down_rows = down_grad.shape[0] // pieces
    down_sums = [
        GroupScatter(
            k,
            lambda group, n=n: grad_down.at[group, pl.ds(n * down_rows, down_rows)],
            lambda i, n=n: down_landed.at[n, i],
            n % 2 == 1,
        )
        for n in range(pieces)
    ]
    exchange = Exchange(k)
    gate_up_in = lambda rank: gate_up_grad.at[rank]
    k.barrier()
    exchange.start(lambda rank: gate_up_sum.at[rank], gate_up_in)
    for sums_of in down_sums:
        sums_of.start(0)
    blocks = keys_t.shape[0]
    grad_keys[...] = jnp.zeros_like(grad_keys)
    grad_values[...] = jnp.zeros_like(grad_values)

    @pl.loop(0, blocks)
    def _(i):
        block = pl.ds(pl.multiple_of(i * BLOCK, BLOCK), BLOCK)
        keys_t[i] = keys[block, :].astype(F32).T.astype(BF16)

    @pl.loop(0, blocks)
    def _(i):
        attend_back_rows(
            i, rank_heads, grad_hidden, out_w, queries, keys, keys_t, values, attended, bias, log_totals,
            cosine, sine, grad_keys, grad_values, grad_qkv,
        )

    for stage in range(k.bits - 1):
        for sums_of in down_sums:
            sums_of.wait(stage)
            sums_of.start(stage + 1)

    @pl.loop(0, blocks)
    def _(i):
        finish_back_rows(i, qkv, cosine, sine, grad_keys, grad_values, grad_qkv, parts)

    @pl.loop(0, normed.shape[1] // BLOCK)
    def _(t):
        part = pl.ds(pl.multiple_of(t * BLOCK, BLOCK), BLOCK)
        grad_qkv_w[part, :] = rows_inner(normed[:, part], grad_qkv[...]).astype(BF16)
        grad_out_w[:, part] = rows_inner(attended[...], grad_hidden[:, part]).astype(BF16)

    for n, sums_of in enumerate(down_sums):
        sums_of.wait(k.bits - 1, down_grad.at[pl.ds(n * down_rows, down_rows)])
    exchange.finish(gate_up_in)
    k.finish()


def last_kernel(
    groups, ranks, slice_width, parts, tokens, grad_hidden, gain, sums_two, grad_qkv, grad_out_w,
    grad_tokens, qkv_grad, out_grad, gain_grads,
    mine, held, landed, sums, qkv_landed, out_landed, tiles, tiles_landed, tiles_sum, group_tiles, sends, recvs,
):
    k = Links(groups, ranks, sends, recvs)
    rows = tokens.shape[0]
    scatter = LineScatter(
        k, lambda rank: parts.at[rank], lambda chip: mine.at[chip], lambda chip: held.at[chip], lambda side, chip: landed.at[side, chip]
    )
    qkv_sums = [
        GroupScatter(
            k,
            lambda group, n=n: grad_qkv.at[group, n],
            lambda i, n=n: qkv_landed.at[n, i],
            n % 2 == 1,
        )
        for n in range(ranks)
    ]
    pieces = out_landed.shape[0]
    piece_rows = out_grad.shape[0] // pieces
    out_sums = [
        GroupScatter(
            k,
            lambda group, n=n: grad_out_w.at[group, pl.ds(n * piece_rows, piece_rows)],
            lambda i, n=n: out_landed.at[n, i],
            n % 2 == 1,
        )
        for n in range(pieces)
    ]
    exchange, tile_exchange = Exchange(k), Exchange(k)
    tile_sends, tile_recvs = k.take(groups, groups)
    qkv_in = lambda rank: qkv_grad.at[rank]
    k.barrier()
    scatter.start()
    for sums_of in qkv_sums:
        sums_of.start(0)
    for sums_of in out_sums:
        sums_of.start(0)
    scatter.pair()
    for i in range(k.chips - 1):
        scatter.step(i)
        if i == 0:
            for sums_of in qkv_sums:
                sums_of.wait(0)
                sums_of.start(1)
    for stage in range(1, k.bits - 1):
        for sums_of in qkv_sums:
            sums_of.wait(stage)
            sums_of.start(stage + 1)
    for n, sums_of in enumerate(qkv_sums):
        exchange.start_piece(n, sums_of.wait(k.bits - 1), qkv_in)
    scatter.last()
    sums[...] = jnp.zeros_like(sums)

    def rows_of(part):
        total = tokens[part].astype(F32)
        scale = inverse_rms(total)
        scaled = total * scale
        grad = held[k.z, part].astype(F32)
        sums[...] += jnp.sum(grad * scaled, 0, keepdims=True)
        grad_tokens[part] = (
            grad_hidden[part] + norm_back(grad * gain[...], scaled, scale)
        ).astype(BF16)

    row_loop(rows, rows_of)
    tiles[...] = jnp.zeros_like(tiles)
    for rank in range(ranks):
        for group in range(groups):
            at = (group * ranks + rank) * slice_width // 128 * 128
            tiles[rank, group, 0:1] = sums[:, at : at + 128]
            tiles[rank, group, 1:2] = sums_two[:, at : at + 128]
    tile_in = lambda rank: tiles_landed.at[rank]
    tile_exchange.start(lambda rank: tiles.at[rank], tile_in)
    for stage in range(k.bits - 1):
        for sums_of in out_sums:
            sums_of.wait(stage)
            sums_of.start(stage + 1)
    for n, sums_of in enumerate(out_sums):
        sums_of.wait(k.bits - 1, out_grad.at[pl.ds(n * piece_rows, piece_rows)])
    tile_exchange.finish(tile_in)
    total = tiles_landed[0]
    for rank in range(1, ranks):
        total = total + tiles_landed[rank]
    tiles_sum[...] = total
    for i in range(1, groups):
        other = lax.rem(k.d + i, groups)
        k.send(
            None,
            tiles_sum.at[other],
            group_tiles.at[k.d],
            tile_sends + other,
            tile_recvs + k.d,
            (other, k.f),
        )
    group_tiles[k.d] = tiles_sum[k.d]
    for i in range(1, groups):
        other = lax.rem(k.d + i, groups)
        k.arrived(None, group_tiles.at[other], tile_recvs + other)
    total = group_tiles[0]
    for group in range(1, groups):
        total = total + group_tiles[group]
    gain_grads[...] = total
    exchange.finish(qkv_in, own=False)
    k.finish()


VMEM = pl.BlockSpec(memory_space=pltpu.VMEM)
ANY = pl.BlockSpec(memory_space=pl.ANY)


def call(kernel, identity, ins, outs, scratch, semaphores, args):
    return pl.pallas_call(
        kernel,
        out_shape=[jax.ShapeDtypeStruct(shape, kind) for shape, kind, _ in outs],
        in_specs=ins,
        out_specs=[place for _, _, place in outs],
        scratch_shapes=[pltpu.VMEM(shape, kind) for shape, kind in scratch]
        + [pltpu.SemaphoreType.DMA((semaphores,))] * 2,
        compiler_params=pltpu.CompilerParams(
            collective_id=identity, has_side_effects=True, vmem_limit_bytes=60 * 1024 * 1024
        ),
    )(*args)


def build(groups, ranks):
    def body(
        tokens, cotangent, lengths, norm_attn, w_query, w_key, w_value, w_output, norm_mlp, w_gate, w_up, w_down
    ):
        rows, width = tokens.shape
        depth = w_query.shape[0]
        count = rows * ranks
        rank_heads = HEADS // ranks
        hidden_part = w_down.shape[0]
        out_rows = w_output.shape[0]
        split = max(1, HEAD_DIM // out_rows)
        rank = lax.axis_index("fsdp")

        def heads_out(weight):
            shaped = weight.reshape(depth, split, rank_heads, ranks // split, HEAD_DIM)
            return shaped.transpose(3, 1, 0, 2, 4).reshape(ranks, depth, rank_heads * HEAD_DIM)

        def heads_in(pieces):
            shaped = pieces.reshape(ranks // split, split, depth, rank_heads, HEAD_DIM)
            return shaped.transpose(2, 1, 3, 0, 4).reshape(depth, HEADS * HEAD_DIM)

        def units_out(weight):
            shaped = weight.reshape(depth, groups, ranks, hidden_part)
            return shaped.transpose(2, 0, 1, 3).reshape(ranks, depth, groups * hidden_part)

        def units_in(pieces):
            shaped = pieces.reshape(ranks, depth, groups, hidden_part)
            return shaped.transpose(1, 2, 0, 3).reshape(depth, groups * ranks * hidden_part)

        span = [[base * split + i for i in range(split)] for base in range(ranks // split)]

        def widen(weight):
            if split > 1:
                weight = lax.all_gather(weight, "fsdp", axis=0, tiled=True, axis_index_groups=span)
            return weight

        def narrow(whole):
            if split > 1:
                whole = whole.reshape(split, -1, width)[lax.rem(rank, split)]
            return whole

        def place_output(grad):
            if split > 1:
                place = lax.rem(rank, split)
                grad = jnp.where(
                    (jnp.arange(split) == place)[:, None, None], grad[None], jnp.zeros((), BF16)
                )
            return grad.reshape(groups, -1, width)

        head_cols = rank_heads * HEAD_DIM
        unit_cols = groups * hidden_part
        chips = ranks // 2
        slice_width = norm_attn.shape[0]
        qkv_out = jnp.concatenate([heads_out(w) for w in (w_query, w_key, w_value)], -1)
        gate_up_out = jnp.concatenate([units_out(w) for w in (w_gate, w_up)], -1)
        gains = jnp.pad(
            jnp.stack([norm_attn, norm_mlp]), ((0, 14), (0, 128 - slice_width))
        )
        out_own = widen(w_output)
        x_all, qkv, gains_all, out_w, down_w = call(
            functools.partial(first_kernel, groups, ranks),
            1,
            [VMEM] * 5,
            [
                ((ranks, rows, width), BF16, ANY),
                ((groups,) + qkv_out.shape, BF16, ANY),
                ((groups, ranks, 16, 128), BF16, ANY),
                ((groups,) + out_own.shape, BF16, ANY),
                ((groups,) + w_down.shape, BF16, ANY),
            ],
            [],
            160,
            (tokens, qkv_out, gains, out_own, w_down),
        )
        qkv = qkv.reshape(width, -1)
        gain_one, gain_two = (
            gains_all[:, :, i, :slice_width].astype(F32).reshape(1, width) for i in range(2)
        )
        out_w = narrow(out_w.reshape(-1, width))
        down_w = down_w.reshape(-1, width)

        places = jnp.arange(count, dtype=jnp.int32)
        bias = jnp.where(places < lengths[0], 0.0, -1000000000.0).astype(F32)[:, None]
        cosine, sine = wide_tables(count, head_cols)
        blocks = count // BLOCK
        heads_shape = ((count, head_cols), BF16, VMEM)
        parts, normed_one, queries, keys, values, attended, log_totals, cotangent_all, gate_up = call(
            functools.partial(attend_kernel, groups, ranks, rank_heads),
            5,
            [VMEM] * 9,
            [((count, width), BF16, VMEM)] * 2
            + [heads_shape] * 4
            + [
                ((blocks, rank_heads, BLOCK), F32, VMEM),
                ((ranks, rows, width), BF16, ANY),
                ((groups,) + gate_up_out.shape, BF16, ANY),
            ],
            [((blocks, head_cols, BLOCK), BF16)],
            192,
            (
                x_all.reshape(count, width),
                cotangent,
                gate_up_out,
                qkv,
                gain_one,
                out_w,
                cosine,
                sine,
                bias,
            ),
        )
        gate_up = gate_up.reshape(width, -1)
        line_scratch = [((chips, rows, width), BF16)] * 2 + [((2, chips, rows, width), BF16)]
        hidden, normed_two = call(
            functools.partial(hidden_kernel, groups, ranks, 2),
            2,
            [ANY] + [VMEM] * 2,
            [((rows, width), F32, VMEM), ((ranks, rows, width), BF16, ANY)],
            line_scratch + [((rows, width), BF16)],
            160,
            (parts.reshape(ranks, rows, width), tokens, gain_two),
        )
        normed_two = normed_two.reshape(count, width)
        gate_up_lin = dot(normed_two, gate_up)
        gate, up = gate_up_lin[:, :unit_cols], gate_up_lin[:, unit_cols:]
        sigmoid = 1.0 / (1.0 + jnp.exp(-gate))
        silu = gate * sigmoid
        mixed = (silu * up).astype(BF16)
        down_sum = lax.psum_scatter(
            dot(mixed, down_w).astype(BF16), "fsdp", scatter_dimension=0, tiled=True
        )
        output = (hidden + down_sum.astype(F32)).astype(BF16)

        live = places[:, None] < lengths[0]
        grad_out_all = jnp.where(
            live, cotangent_all.reshape(count, width), jnp.zeros((), BF16)
        )
        own_places = rank * rows + jnp.arange(rows, dtype=jnp.int32)
        grad_out = jnp.where(own_places[:, None] < lengths[0], cotangent, jnp.zeros((), BF16))
        grad_mixed = cols_inner(grad_out_all, down_w)
        grad_down = rows_inner(mixed, grad_out_all).astype(BF16).reshape(groups, hidden_part, width)
        grad_gate = grad_mixed * up * (sigmoid * (1.0 + gate * (1.0 - sigmoid)))
        grad_up = grad_mixed * silu
        grad_gate_up = jnp.concatenate([grad_gate.astype(BF16), grad_up.astype(BF16)], -1)
        parts = cols_inner(grad_gate_up, gate_up).astype(BF16).reshape(ranks, rows, width)
        grad_gate_up_w = rows_inner(normed_two, grad_gate_up).astype(BF16)
        grad_hidden_all, grad_hidden, sums_two, gate_up_sum = call(
            functools.partial(middle_kernel, groups, ranks, 2),
            3,
            [ANY] + [VMEM] * 4,
            [
                ((ranks, rows, width), BF16, ANY),
                ((rows, width), F32, VMEM),
                ((1, width), F32, VMEM),
                ((ranks, depth, 2 * unit_cols), BF16, VMEM),
            ],
            line_scratch
            + [
                ((rows, width), BF16),
                ((ranks, groups - 1, depth, 2 * unit_cols), BF16),
            ],
            160,
            (
                parts,
                hidden,
                grad_out,
                gain_two,
                grad_gate_up_w.reshape(groups, ranks, depth, 2 * unit_cols),
            ),
        )
        pieces = 4
        parts, grad_qkv_w, grad_out_w, grad_gate_up_w, grad_w_down = call(
            functools.partial(attend_back_kernel, groups, ranks, rank_heads),
            6,
            [VMEM] * 14,
            [
                ((count, width), BF16, VMEM),
                ((width, 3 * head_cols), BF16, VMEM),
                ((head_cols, width), BF16, VMEM),
                ((ranks, depth, 2 * unit_cols), BF16, ANY),
                ((hidden_part, width), F32, VMEM),
            ],
            [
                ((count, 3 * head_cols), BF16),
                ((blocks, head_cols, BLOCK), BF16),
                ((count, head_cols), F32),
                ((count, head_cols), F32),
                ((pieces, groups - 1, hidden_part // pieces, width), BF16),
            ],
            160,
            (
                grad_hidden_all.reshape(count, width),
                out_w,
                queries,
                keys,
                values,
                attended,
                bias,
                log_totals,
                cosine,
                sine,
                qkv,
                normed_one,
                gate_up_sum,
                grad_down,
            ),
        )
        grad_out_w = place_output(grad_out_w)
        grad_w_gate = units_in(grad_gate_up_w[..., :unit_cols]).astype(F32)
        grad_w_up = units_in(grad_gate_up_w[..., unit_cols:]).astype(F32)
        parts = parts.reshape(ranks, rows, width)
        pieces = 2
        out_rows = grad_out_w.shape[1]
        tile = (8, 128)
        grad_tokens, grad_qkv_w, grad_w_output, sums = call(
            functools.partial(last_kernel, groups, ranks, slice_width),
            4,
            [ANY] + [VMEM] * 6,
            [
                ((rows, width), BF16, VMEM),
                ((ranks, depth, 3 * head_cols), BF16, ANY),
                ((out_rows, width), F32, VMEM),
                (tile, F32, VMEM),
            ],
            line_scratch
            + [
                ((1, width), F32),
                ((ranks, groups - 1, depth, 3 * head_cols), BF16),
                ((pieces, groups - 1, out_rows // pieces, width), BF16),
                ((ranks, groups) + tile, F32),
                ((ranks, groups) + tile, F32),
                ((groups,) + tile, F32),
                ((groups,) + tile, F32),
            ],
            160,
            (
                parts,
                tokens,
                grad_hidden,
                gain_one,
                sums_two,
                grad_qkv_w.reshape(groups, ranks, depth, 3 * head_cols),
                grad_out_w,
            ),
        )
        if split > 1:
            grad_w_output = lax.psum_scatter(
                grad_w_output, "fsdp", scatter_dimension=0, tiled=True, axis_index_groups=span
            )
        grad_w_query, grad_w_key, grad_w_value = (
            heads_in(grad_qkv_w[..., i * head_cols : (i + 1) * head_cols]).astype(F32) for i in range(3)
        )
        place = (lax.axis_index("dp") * ranks + rank) * slice_width % 128
        sums = lax.dynamic_slice_in_dim(sums, place, slice_width, 1)
        return (
            output,
            grad_tokens,
            sums[0],
            grad_w_query,
            grad_w_key,
            grad_w_value,
            grad_w_output,
            sums[1],
            grad_w_gate,
            grad_w_up,
            grad_w_down,
        )

    return body


def solution(mesh):
    both = P(("dp", "fsdp"))
    rows = P(("dp", "fsdp"), None)
    return jax.shard_map(
        build(mesh.shape["dp"], mesh.shape["fsdp"]),
        mesh=mesh,
        in_specs=(rows, rows, P("dp"), both, rows, rows, rows, rows, both, rows, rows, rows),
        out_specs=(rows, rows, both, rows, rows, rows, rows, both, rows, rows, rows),
        check_vma=False,
    )
```

time: 1180 us -> 715 us (0.61)
  waiting for transfers between devices: 622 us -> 0.02 us
  Pallas kernels: 0 us -> 553 us
  blocking collectives: 226 us -> 0 us
  matrix products: 194 us -> 77.4 us
  other arithmetic: 68.7 us -> 18.4 us
    pallas_call x0 -> x6, Pallas kernels: none -> 553 us  [call(): pl.pallas_call(kernel, out_shape=[jax.ShapeDtypeStruct(shape, kind) for s...]
    all_gather x8 -> x0, waiting for transfers between devices: 299 us -> none  [the longest x4 154 us: gather_rows(): return lax.all_gather(value, 'fsdp', axis=0, tiled=True)]
    reduce_scatter x8 -> x1, waiting for transfers between devices: 188 us -> 0.01 us  [body(): lax.psum_scatter(dot(mixed, down_w).astype(BF16), 'fsdp', scatter_dimensi...]
    all_to_all x3 -> x0, blocking collectives: 186 us -> none  [exchange(): return lax.all_to_all(value, 'fsdp', 0, 0, tiled=True)]
    unnamed x18 -> x1, waiting for transfers between devices: 135 us -> 0.02 us
    dot_general x6 -> x0, matrix products: 70.6 us -> none  [the longest x1 17.9 us: attend_back(): jnp.einsum('hqd,hkd->hqk', grad, values, preferred_element_type=F32)]
    all_gather x1 -> x0, blocking collectives: 40 us -> none  [body(): lax.all_gather(jnp.stack([norm_attn, norm_mlp], -1), ('dp', 'fsdp'), axis...]
    convert_element_type x9 -> x3, other arithmetic: 36.3 us -> 3.09 us  [the longest x1 2.07 us: body(): output = (hidden + down_sum.astype(F32)).astype(BF16)]
  transfers between devices with their start and end apart: 18 -> 1, of which waited for: 13 -> 0; matrix products, arithmetic and copies ran while one was open for 22% -> 10% of each run, Pallas kernels for 0% -> 36%
where the time goes in v2:
time: 715 us; the launch traced here: 711 us
  Pallas kernels  553 us (77%)
  matrix products  77.4 us (11%)
  local copies, waits for them, and re-layouts  47.2 us (7%)
  other arithmetic  18.4 us (3%)
  between operations  15.6 us (2%)
    pallas_call x6, Pallas kernels, call(): pl.pallas_call(kernel, out_shape=[jax.ShapeDtypeStruct(shape, kind) for s...  553 us
    dot_general x2, matrix products, cols_inner(): lax.dot_general(left, right, (((1,), (1,)), ((), ())), preferred_element_...  27.7 us
    dot_general x2, matrix products, dot(): return jnp.dot(left, right, preferred_element_type=F32)  24.9 us
    dot_general x2, matrix products, rows_inner(): lax.dot_general(left, right, (((0,), (0,)), ((), ())), preferred_element_...  24.9 us
  transfers between devices with their start and end apart: 1, of which 0 were waited for; matrix products, arithmetic and copies ran while one was open for 10% of the time, Pallas kernels for 36%

profile of v2, /device:TPU:0, one launch (start us, length us, event | category | flops | bytes accessed | tf_op | source)
XLA Modules:
  0.0 711.3 jit_solution(15511662455012188230)
XLA Ops:
  7.3 1.6 reshape.201
  8.8 0.2 copy.63
  9.0 1.0 reshape.202
  10.1 1.5 reshape.199
  11.8 1.0 reshape.200
  12.8 0.5 reshape.197
  13.6 1.0 reshape.198
  14.6 0.3 copy.53
  14.9 0.4 copy.61
  15.3 1.0 reshape.207
  16.3 0.3 copy.52
  16.6 0.4 copy.62
  17.0 0.8 reshape.205
  17.8 0.6 fusion.8.gains
  18.4 2.0 pad_maximum_fusion.4.qkv_out
  20.4 87.0 %shard_map.203 = (bf16[8,160,2048]{2,1,0:T(8,128)(2,1)}, bf16[4,8,64,768]{3,2,1,0:T(8,128)(2,1)}, bf16[4,8,16,128]{3,2,1,0:T(8,128)(2,1)}, bf16[4,64,2048]{2,1,0:T(8,128)(2,1)}, bf16[4,256,2048]{2,1,0:T(8,128)(2,1)}) custom-call(bf16[160,2048]{1,0:T(8,128)(2,1)} %tokens.5, bf16[8,64,768]{2,1,0:T(8,128)(2,1)} %pad_maximum_fusion.4.qkv_out, ...), custom_call_target="tpu_custom_call" | custom-call | tf_op jit(solution)/shard_map/pallas_call | solution.py:990
  107.3 1.0 convert_reduce_fusion
  108.3 0.7 reshape.222.gain
  109.0 0.7 fusion.2
  109.7 0.8 pad_maximum_fusion.5
  110.5 1.5 copy.40.cosine
  112.0 1.1 tile.20
  113.1 1.5 copy.41.sine
  115.2 0.9 fusion.1.bias
  116.1 0.7 reshape.223.gain
  116.8 1.5 pad_maximum_fusion.3.gate_up_out
  118.3 116.6 %shard_map.204 = (bf16[1280,2048]{1,0:T(8,128)(2,1)}, bf16[1280,2048]{1,0:T(8,128)(2,1)}, bf16[1280,256]{1,0:T(8,128)(2,1)}, bf16[1280,256]{1,0:T(8,128)(2,1)}, ...) custom-call(bf16[1280,2048]{1,0:T(8,128)(2,1)} %bitcast.99, ...), custom_call_target="tpu_custom_call" | custom-call | tf_op jit(solution)/shard_map/pallas_call | solution.py:990
  234.9 93.8 %shard_map.205 = (f32[160,2048]{1,0:T(8,128)}, bf16[8,160,2048]{2,1,0:T(8,128)(2,1)}) custom-call(bf16[8,160,2048]{2,1,0:T(8,128)(2,1)} %bitcast.102, bf16[160,2048]{1,0:T(8,128)(2,1)} %tokens.5, f32[1,2048]{1,0:T(1,128)} %reshape.223.gain), custom_call_target="tpu_custom_call" | custom-call | tf_op jit(solution)/shard_map/pallas_call | solution.py:990
  328.7 17.5 %fusion.11 = f32[1280,2048]{1,0:T(8,128)} fusion(bf16[1280,2048]{1,0:T(8,128)(2,1)} %bitcast.130, bf16[2048,2048]{1,0:T(8,128)(2,1)} %bitcast.128), kind=kOutput, calls=%fused_computation.53 | convolution fusion | flops 10737418240 | bytes 24117248 | tf_op jit(solution)/shard_map/dot_general | solution.py:21
  346.3 0.4 broadcast_select_fusion
  346.7 1.7 copy-done.10
  348.5 12.3 %multiply_convert_fusion.1 = (bf16[1280,1024]{1,0:T(8,128)(2,1)}, bf16[1280,1024]{1,0:T(8,128)(2,1)}, bf16[1280,1024]{1,0:T(8,128)(2,1)S(1)}) fusion(f32[1280,2048]{1,0:T(8,128)} %fusion.11, bf16[1280,2048]{1,0:T(8,128)(2,1)S(1)} %bitcast.105, bf16[1024,2048]{1,0:T(8,128)(2,1)S(1)} %bitcast.132), kind=kOutput, calls=%fused_computation.6 | convolution fusion | flops 5388369920 | bytes 27787264 | tf_op jit(solution)/shard_map/dot_general | solution.py:29
  360.8 7.3 %convolution_convert_fusion.2 = bf16[1280,2048]{1,0:T(8,128)(2,1)} fusion(bf16[1280,1024]{1,0:T(8,128)(2,1)S(1)} %get-tuple-element.73, bf16[1024,2048]{1,0:T(8,128)(2,1)S(1)} %bitcast.133), kind=kOutput, calls=%fused_computation.2 | convolution fusion | flops 5371330560 | bytes 12058624 | tf_op jit(solution)/shard_map/dot_general | solution.py:21
  368.2 1.0 copy-done.1
  369.2 1.0 broadcast_select_fusion.1.grad_out
  370.2 17.4 %convolution_convert_fusion = bf16[2048,2048]{1,0:T(8,128)(2,1)} fusion(bf16[1280,2048]{1,0:T(8,128)(2,1)} %bitcast.131, bf16[1280,1024]{1,0:T(8,128)(2,1)} %get-tuple-element.72, bf16[1280,1024]{1,0:T(8,128)(2,1)} %get-tuple-element.71), kind=kOutput, calls=%fused_computation | convolution fusion | flops 10752098304 | bytes 18874368 | tf_op jit(solution)/shard_map/dot_general | solution.py:25
  387.6 15.4 %convolution_convert_fusion.1 = bf16[1280,2048]{1,0:T(8,128)(2,1)} fusion(bf16[2048,2048]{1,0:T(8,128)(2,1)} %bitcast.129, bf16[1280,1024]{1,0:T(8,128)(2,1)S(1)} %copy-done.12, bf16[1280,1024]{1,0:T(8,128)(2,1)S(1)} %copy-done.11), kind=kOutput, calls=%fused_computation.1 | convolution fusion | flops 10750525440 | bytes 18874368 | tf_op jit(solution)/shard_map/dot_general | solution.py:29
  403.0 107.3 %shard_map.206 = (bf16[8,160,2048]{2,1,0:T(8,128)(2,1)}, f32[160,2048]{1,0:T(8,128)}, f32[1,2048]{1,0:T(1,128)}, bf16[8,64,2048]{2,1,0:T(8,128)(2,1)}) custom-call(bf16[8,160,2048]{2,1,0:T(8,128)(2,1)} %bitcast.100, f32[160,2048]{1,0:T(8,128)} %get-tuple-element.45.hidden, bf16[160,2048]{1,0:T(8,128)(2,1)} %broadcast_select_fusion.1.grad_out, ...), custom_call_target="tpu_custom_call" | custom-call | tf_op jit(solution)/shard_map/pallas_call | solution.py:990
  510.3 2.9 bitcast_select_fusion
  513.2 7.4 %convolution_convert_fusion.3 = bf16[1024,2048]{1,0:T(8,128)(2,1)} fusion(bf16[1280,1024]{1,0:T(8,128)(2,1)S(1)} %get-tuple-element.73, bf16[1280,2048]{1,0:T(8,128)(2,1)S(1)} %bitcast_select_fusion), kind=kOutput, calls=%fused_computation.11 | convolution fusion | flops 5370806272 | bytes 12058624 | tf_op jit(solution)/shard_map/dot_general | solution.py:25
  520.7 58.3 %shard_map.207 = (bf16[1280,2048]{1,0:T(8,128)(2,1)}, bf16[2048,768]{1,0:T(8,128)(2,1)}, bf16[256,2048]{1,0:T(8,128)(2,1)}, bf16[8,64,2048]{2,1,0:T(8,128)(2,1)}, f32[256,2048]{1,0:T(8,128)}) custom-call(bf16[1280,2048]{1,0:T(8,128)(2,1)} %bitcast.106, bf16[256,2048]{1,0:T(8,128)(2,1)} %bitcast.109, bf16[1280,256]{1,0:T(8,128)(2,1)} %get-tuple-element.51.queries, ...), custom_call_target="tpu_custom_call" | custom-call | tf_op jit(solution)/shard_map/pallas_call | solution.py:990
  579.0 89.6 %shard_map.208 = (bf16[160,2048]{1,0:T(8,128)(2,1)}, bf16[8,64,768]{2,1,0:T(8,128)(2,1)}, f32[64,2048]{1,0:T(8,128)}, f32[8,128]{1,0:T(8,128)}) custom-call(bf16[8,160,2048]{2,1,0:T(8,128)(2,1)} %bitcast.101, bf16[160,2048]{1,0:T(8,128)(2,1)} %tokens.5, f32[160,2048]{1,0:T(8,128)} %get-tuple-element.59.grad_hidden, f32[1,2048]{1,0:T(1,128)} %reshape.222.gain, ...), custom_call_target="tpu_custom_call" | custom-call | tf_op jit(solution)/shard_map/pallas_call | solution.py:990
  668.6 1.3 slice_convert_fusion.2
  669.9 0.5 reshape.229
  670.4 0.6 copy.46
  671.0 1.2 reshape.224
  672.2 0.5 reshape.230
  672.6 0.6 copy.47
  673.2 1.2 reshape.225
  674.4 0.5 reshape.231
  674.8 0.6 copy.48
  675.5 1.2 reshape.226
  676.6 3.3 slice_convert_fusion
  679.9 3.2 reshape.232
  683.1 2.8 copy.49
  685.9 2.5 copy.54
  688.4 2.2 reshape.233
  690.7 2.9 copy.50
  693.6 2.5 copy.55
  696.2 0.5 slice_bitcast_fusion
  696.7 2.1 add_convert_fusion
  698.8 2.0 copy.70
  700.8 1.9 copy.71
  702.6 1.3 copy.72
  (41 shorter events, 0.7 us)
Async XLA Ops:
  7.2 5.7 copy-start.6
  7.2 7.4 %copy-start.3 = (bf16[64,8192]{1,0:T(8,128)(2,1)S(1)}, bf16[64,8192]{1,0:T(8,128)(2,1)}, u32[]{:S(2)}) copy-start(bf16[64,8192]{1,0:T(8,128)(2,1)} %param.22) | copy-start | bytes 3145732
  7.2 689.5 %reduce-scatter.2.cloned.1.call-start = ((), (), s32[]{:S(2)}) async-start(), calls=%async_computation.1 | async-start | bytes 5898240 | tf_op jit(solution)/shard_map/reduce_scatter | solution.py:1131
  11.6 4.8 copy-start.4
  14.9 2.9 copy-start.8
  14.9 2.9 copy-start.9
  14.9 3.5 copy-start.5
  234.9 111.4 %slice-start = ((s8[5242880]{0:T(1024)(128)(4,1)}), s8[1048576]{0:T(1024)(128)(4,1)S(1)}, s32[]{:S(2)}) async-start(s8[5242880]{0:T(1024)(128)(4,1)} %bitcast.90), calls=%async_computation.2 | async-start | bytes 2097152
  328.7 17.5 %slice-start.1 = ((s8[5242880]{0:T(1024)(128)(4,1)}), s8[4194304]{0:T(1024)(128)(4,1)S(1)}, s32[]{:S(2)}) async-start(s8[5242880]{0:T(1024)(128)(4,1)} %bitcast.90), calls=%async_computation.3 | async-start | bytes 8388608
  346.3 2.2 copy-start.10
  368.1 1.1 copy-start.1
  370.2 17.4 %copy-start.11 = (bf16[1280,1024]{1,0:T(8,128)(2,1)S(1)}, bf16[1280,1024]{1,0:T(8,128)(2,1)}, u32[]{:S(2)}) copy-start(bf16[1280,1024]{1,0:T(8,128)(2,1)} %get-tuple-element.71) | copy-start | bytes 7864324
  370.2 17.4 %copy-start.12 = (bf16[1280,1024]{1,0:T(8,128)(2,1)S(1)}, bf16[1280,1024]{1,0:T(8,128)(2,1)}, u32[]{:S(2)}) copy-start(bf16[1280,1024]{1,0:T(8,128)(2,1)} %get-tuple-element.72) | copy-start | bytes 7864324
  690.6 5.5 copy-start.7
  690.7 6.1 copy-start
  693.6 9.1 %copy-start.2 = (f32[256,2048]{1,0:T(8,128)S(1)}, f32[256,2048]{1,0:T(8,128)}, u32[]{:S(2)}) copy-start(f32[256,2048]{1,0:T(8,128)} %get-tuple-element.107) | copy-start | bytes 6291460
Sparse Core Ops, SparseCore 0:
  368.3 68.3 reduce-scatter.1

commit v3 on v2

--- a/solution.py
+++ b/solution.py
@@ -2,6 +2,7 @@
 
 import jax
 import jax.numpy as jnp
+import numpy as np
 from jax import lax
 from jax.experimental import pallas as pl
 from jax.experimental.pallas import tpu as pltpu
@@ -50,16 +51,21 @@
     return values * cosine + jnp.where(lane % HEAD_DIM < half, ahead, behind) * sine
 
 
-def wide_tables(count, width):
+def wide_tables(count):
     half = HEAD_DIM // 2
-    inverse = THETA ** (-jnp.arange(half, dtype=F32) * 2.0 / HEAD_DIM)
-    angles = jnp.arange(count, dtype=jnp.int32).astype(F32)[:, None] * inverse[None, :]
-    cosine, sine = jnp.cos(angles), jnp.sin(angles)
-    repeats = width // HEAD_DIM
-    return (
-        jnp.tile(jnp.concatenate([cosine, cosine], -1), (1, repeats)),
-        jnp.tile(jnp.concatenate([-sine, sine], -1), (1, repeats)),
-    )
+    inverse = np.float32(THETA) ** (-np.arange(half, dtype=np.float32) * np.float32(2.0) / HEAD_DIM)
+    angles = np.arange(count, dtype=np.float32)[:, None] * inverse.astype(np.float32)[None, :]
+    cosine, sine = np.cos(angles).astype(np.float32), np.sin(angles).astype(np.float32)
+    return np.concatenate([cosine] * 4, -1), np.concatenate([-sine, sine] * 2, -1)
+
+
+def table_rows(table, block, width):
+    return jnp.concatenate([table[block, :]] * (width // 128), 1)
+
+
+def key_bias(j, length):
+    place = j * BLOCK + lax.broadcasted_iota(jnp.int32, (BLOCK, 1), 0)
+    return jnp.where(place < length, 0.0, -1000000000.0)
 
 
 def head_rows(values, head):
@@ -71,13 +77,13 @@
     return lax.broadcasted_iota(jnp.int32, shape, 0) > lax.broadcasted_iota(jnp.int32, shape, 1)
 
 
-def attend_block(i, rank_heads, queries, keys, values_t, bias, attended, log_totals):
+def attend_block(i, rank_heads, queries, keys, values_t, length, attended, log_totals):
     queries_t = queries.T
     masked = [(head_rows(queries_t, h) * SCALE).astype(BF16) for h in range(rank_heads)]
 
     def chunk(j, carry, last):
         part = pl.ds(pl.multiple_of(j * BLOCK, BLOCK), BLOCK)
-        key_part, bias_part = keys[part, :], bias[part, :]
+        key_part, bias_part = keys[part, :], key_bias(j, length)
         after = []
         for h in range(rank_heads):
             top, total, out = carry[h]
@@ -119,40 +125,34 @@
 
     def rows_of(part):
         rows = x[part, :].astype(F32)
-        normed[part, :] = (rows * inverse_rms(rows) * gain[...]).astype(BF16)
+        normed[part, :] = (rows * inverse_rms(rows) * gain[0:1, :]).astype(BF16)
 
     pl.loop(0, BLOCK // 16)(
         lambda t: rows_of(pl.ds(pl.multiple_of(start + t * 16, 16), 16))
     )
     block = pl.ds(pl.multiple_of(start, BLOCK), BLOCK)
     rows = normed[block, :]
-    cos, sin = cosine[block, :], sine[block, :]
-    rounded = turn_halves(dot(rows, qkv[:, :cols]), cos, sin).astype(BF16)
+
+    def weight(n):
+        return qkv[:, :, :, n * cols : (n + 1) * cols].reshape(x.shape[1], cols)
+
+    cos, sin = table_rows(cosine, block, cols), table_rows(sine, block, cols)
+    rounded = turn_halves(dot(rows, weight(0)), cos, sin).astype(BF16)
     queries[block, :] = rounded
-    keys[block, :] = turn_halves(dot(rows, qkv[:, cols : 2 * cols]), cos, sin).astype(BF16)
-    value = dot(rows, qkv[:, 2 * cols :])
+    keys[block, :] = turn_halves(dot(rows, weight(1)), cos, sin).astype(BF16)
+    value = dot(rows, weight(2))
     values[block, :] = value.astype(BF16)
     values_t[i] = value.T.astype(BF16)
     return rounded.astype(F32)
 
 
-def matmul_block(i, left, right, out, step=512):
-    block = pl.ds(pl.multiple_of(i * BLOCK, BLOCK), BLOCK)
-    rows = left[block, :]
-
-    @pl.loop(0, right.shape[1] // step)
-    def _(c):
-        part = pl.ds(pl.multiple_of(c * step, step), step)
-        out[block, part] = dot(rows, right[:, part]).astype(out.dtype)
-
-
 def lanes_of(values, head):
     lane = lax.broadcasted_iota(jnp.int32, values.shape, 1)
     return jnp.where((lane >= head * HEAD_DIM) & (lane < (head + 1) * HEAD_DIM), values, 0.0)
 
 
 def attend_back_block(
-    i, rank_heads, queries, keys, keys_t, values, attended, grad, bias, log_totals, grad_keys, grad_values
+    i, rank_heads, queries, keys, keys_t, values, attended, grad, length, log_totals, grad_keys, grad_values
 ):
     block = pl.ds(pl.multiple_of(i * BLOCK, BLOCK), BLOCK)
     query = queries[block, :].astype(F32) * SCALE
@@ -170,7 +170,7 @@
 
     def chunk(j, carry, last):
         part = pl.ds(pl.multiple_of(j * BLOCK, BLOCK), BLOCK)
-        key_part, value_part, bias_part = keys[part, :], values[part, :], bias[part, :]
+        key_part, value_part, bias_part = keys[part, :], values[part, :], key_bias(j, length)
         after, weights_all, grads_all = [], [], []
         for h in range(rank_heads):
             scores = dot(key_part, masked_q[h]) + bias_part
@@ -194,23 +194,25 @@
 
 
 def attend_back_rows(
-    i, rank_heads, grad_hidden, out_w, queries, keys, keys_t, values, attended, bias, log_totals,
+    i, rank_heads, grad_hidden, out_w, queries, keys, keys_t, values, attended, length, log_totals,
     cosine, sine, grad_keys, grad_values, grad_qkv,
 ):
     block = pl.ds(pl.multiple_of(i * BLOCK, BLOCK), BLOCK)
     cols = queries.shape[1]
     grad = cols_inner(grad_hidden[block, :], out_w[...]).astype(BF16).astype(F32)
     grad_q = attend_back_block(
-        i, rank_heads, queries, keys, keys_t, values, attended, grad, bias, log_totals, grad_keys, grad_values
+        i, rank_heads, queries, keys, keys_t, values, attended, grad, length, log_totals, grad_keys, grad_values
     )
-    grad_qkv[block, :cols] = turn_halves(grad_q, cosine[block, :], -sine[block, :]).astype(BF16)
+    grad_qkv[block, :cols] = turn_halves(
+        grad_q, table_rows(cosine, block, cols), -table_rows(sine, block, cols)
+    ).astype(BF16)
 
 
 def finish_back_rows(i, qkv, cosine, sine, grad_keys, grad_values, grad_qkv, parts):
     block = pl.ds(pl.multiple_of(i * BLOCK, BLOCK), BLOCK)
     cols = grad_keys.shape[1]
     grad_qkv[block, cols : 2 * cols] = turn_halves(
-        grad_keys[block, :], cosine[block, :], -sine[block, :]
+        grad_keys[block, :], table_rows(cosine, block, cols), -table_rows(sine, block, cols)
     ).astype(BF16)
     grad_qkv[block, 2 * cols :] = grad_values[block, :].astype(BF16)
     rows = grad_qkv[block, :]
@@ -345,6 +347,10 @@
                 k.sibling,
             )
 
+    def over(self, chip):
+        k = self.links
+        k.arrived(None, self.view(chip * 2 + 1 - k.c), self.recvs + 2 * k.chips + chip)
+
     def finish(self):
         k, chips = self.links, self.links.chips
         for chip in range(chips):
@@ -460,49 +466,44 @@
         k.pending.append(lambda: pl.when(k.f == rank)(lambda: here().wait()))
 
 
-def spread_bits(base, bits):
-    places = [base]
-    for b, own in bits:
-        places = places + [place + (1 - 2 * own) * (1 << b) for place in places]
-    return places
-
-
 class GroupGather:
-    def __init__(self, links, view):
-        self.links, self.view = links, view
+    def __init__(self, links, view, high):
+        self.links, self.view, self.high = links, view, high
         count = links.groups - 1
-        self.sends, self.recvs = links.take(2 * count, 2 * count)
-
-    def order(self, half):
-        bits = list(range(self.links.bits))
-        return bits if half == 0 else bits[::-1]
-
-    def base(self, half, stage):
-        return half * (self.links.groups - 1) + (1 << stage) - 1
-
-    def start(self, half, stage, source=None):
+        self.sends, self.recvs = links.take(count, count)
+
+    def flip(self, stage):
         k = self.links
-        order = self.order(half)
-        blocks = spread_bits(k.d, [(b, k.bit(b)) for b in order[:stage]])
-        for i, block in enumerate(blocks):
-            at = self.base(half, stage) + i
-            target = self.view(block, half)
+        low, up = 1 << stage, 1 << (k.bits - 1 - stage)
+        size = low + self.high * (up - low)
+        return (1 - 2 * lax.rem(lax.div(k.d, size), 2)) * size
+
+    def places(self, stage):
+        places = [self.links.d]
+        for past in range(stage):
+            places = places + [place + self.flip(past) for place in places]
+        return places
+
+    def start(self, stage, source=None):
+        k = self.links
+        for i, place in enumerate(self.places(stage)):
+            at = (1 << stage) - 1 + i
+            target = self.view(place)
             k.send(
                 None,
-                target if source is None else source(half),
+                target if source is None else source,
                 target,
                 self.sends + at,
                 self.recvs + at,
-                k.partner(order[stage]),
+                (k.d + self.flip(stage), k.f),
             )
 
-    def wait(self, half, stage):
-        k = self.links
-        order = self.order(half)
-        far = k.partner(order[stage])[0]
-        blocks = spread_bits(far, [(b, k.bit(b)) for b in order[:stage]])
-        for i, block in enumerate(blocks):
-            k.arrived(None, self.view(block, half), self.recvs + self.base(half, stage) + i)
+    def arrivals(self, stage):
+        return [place + self.flip(stage) for place in self.places(stage)]
+
+    def wait(self, stage):
+        for i, place in enumerate(self.arrivals(stage)):
+            self.links.arrived(None, self.view(place), self.recvs + (1 << stage) - 1 + i)
 
 
 class GroupScatter:
@@ -556,93 +557,86 @@
         action(pl.ds(pl.multiple_of(first + i * step, step), step))
 
 
-def halved(ref, count):
-    return lambda group, half: ref.at[group, pl.ds(half * count, count)]
-
-
-def first_kernel(
-    groups, ranks, tokens, qkv_out, gains, out_w, down_w,
-    x_all, qkv, gains_all, out_all, down_all, sends, recvs,
-):
-    k = Links(groups, ranks, sends, recvs)
-    x_line = LineGather(k, lambda rank: x_all.at[rank])
-    gains_ex, qkv_ex = Exchange(k), Exchange(k)
-    out_half, down_half = out_w.shape[0] // 2, down_w.shape[0] // 2
-    early = [
-        (GroupGather(k, halved(out_all, out_half)), lambda h: out_w.at[pl.ds(h * out_half, out_half)]),
-        (GroupGather(k, halved(down_all, down_half)), lambda h: down_w.at[pl.ds(h * down_half, down_half)]),
-    ]
-    late = [GroupGather(k, halved(qkv, ranks // 2)), GroupGather(k, halved(gains_all, ranks // 2))]
-    k.barrier()
-    gains_in = lambda rank: gains_all.at[k.d, rank]
-    qkv_in = lambda rank: qkv.at[k.d, rank]
-    gains_ex.start(lambda rank: gains, gains_in)
-    qkv_ex.start(lambda rank: qkv_out.at[rank], qkv_in)
-    for gather, source in early:
-        for half in range(2):
-            gather.start(half, 0, source)
-    own = [
-        k.move(tokens, x_all.at[k.f]),
-        k.move(out_w, out_all.at[k.d]),
-        k.move(down_w, down_all.at[k.d]),
-    ]
-    x_line.start(tokens)
-    gains_ex.finish(gains_in)
-    qkv_ex.finish(qkv_in)
-    for gather in late:
-        for half in range(2):
-            gather.start(half, 0)
-    for wait in own:
-        wait()
-    early = [gather for gather, _ in early]
-    x_line.step(1)
-    for gather in early:
-        for half in range(2):
-            gather.wait(half, 0)
-            gather.start(half, 1)
-    for reach in range(2, k.chips):
-        x_line.step(reach)
-        if reach == 2:
-            for gather in late:
-                for half in range(2):
-                    gather.wait(half, 0)
-                    gather.start(half, 1)
-    for stage in range(1, k.bits):
-        for gather in late + early:
-            for half in range(2):
-                gather.wait(half, stage)
-                if stage + 1 < k.bits:
-                    gather.start(half, stage + 1)
-    x_line.finish()
-    k.finish()
-
-
 def spaced(events, blocks):
     count = len(events)
     return [events[b * count // blocks : (b + 1) * count // blocks] for b in range(blocks)]
 
 
 def attend_kernel(
-    groups, ranks, rank_heads, x_all, cotangent, gate_up_out, qkv, gain, out_w, cosine, sine, bias,
-    parts, normed, queries, keys, values, attended, log_totals, cotangent_all, gate_up,
-    values_t, sends, recvs,
+    groups, ranks, rank_heads, slice_width,
+    lengths, tokens, qkv_out, gains, out_w, down_w, gate_up_out, cosine, sine,
+    x_all, qkv, gain_rows, normed, queries, keys, values, attended, log_totals,
+    attended_all, gate_up, out_all, down_all,
+    gains_all, values_t, sends, recvs,
 ):
     k = Links(groups, ranks, sends, recvs)
-    depth = gate_up_out.shape[1]
+    length = lengths[0]
+    cols, rows = queries.shape[1], tokens.shape[0]
+    depth, half = gate_up_out.shape[1], ranks // 2
     pieces = depth // 16
+    blocks = values_t.shape[0]
+    split = max(1, HEAD_DIM // out_w.shape[0])
+    down_half = down_w.shape[0] // 2
+
+    def unit(group, rank):
+        return (
+            (lax.div(rank, split) * split + lax.div(group, rank_heads)) * rank_heads
+            + lax.rem(group, rank_heads)
+        ) * split + lax.rem(rank, split)
+
+    def out_block(group, rank):
+        return out_all.at[unit(group, rank)]
+
+    def attended_block(i, rank):
+        return attended_all.at[
+            pl.ds(i * BLOCK, BLOCK), pl.ds(pl.multiple_of(rank * cols, cols), cols)
+        ]
+
+    x_line = LineGather(k, lambda rank: x_all.at[pl.ds(pl.multiple_of(rank * rows, 16), rows)])
+    out_line = LineGather(k, lambda rank: out_block(k.d, rank))
+    lines = [LineGather(k, lambda rank, i=i: attended_block(i, rank)) for i in range(blocks)]
+    gains_ex, qkv_ex = Exchange(k), Exchange(k)
     exchanges = [Exchange(k) for _ in range(pieces)]
+    downs = [
+        GroupGather(k, lambda group, h=h: down_all.at[group, pl.ds(h * down_half, down_half)], h)
+        for h in range(2)
+    ]
+    late = [
+        GroupGather(k, lambda group, h=h, ref=ref: ref.at[group, pl.ds(h * half, half)], h)
+        for ref in (qkv, gains_all)
+        for h in range(2)
+    ]
+    out_gathers = [
+        GroupGather(k, lambda group, r=r: out_block(group, k.c * half + r), k.c) for r in range(half)
+    ]
     gathers = [
-        GroupGather(
-            k,
-            lambda group, half, q=q: gate_up.at[
-                group, pl.ds(half * (ranks // 2), ranks // 2), pl.ds(q * 16, 16)
-            ],
-        )
+        [
+            GroupGather(
+                k,
+                lambda group, h=h, q=q: gate_up.at[group, pl.ds(h * half, half), pl.ds(q * 16, 16)],
+                h,
+            )
+            for h in range(2)
+        ]
         for q in range(pieces)
     ]
-    line = LineGather(k, lambda rank: cotangent_all.at[rank])
-    k.barrier()
-    own = k.move(cotangent, cotangent_all.at[k.f])
+    over_sends, over_recvs = k.take(half * groups, half * groups)
+
+    def onward(several, stage):
+        for gather in several:
+            gather.wait(stage)
+            if stage + 1 < k.bits:
+                gather.start(stage + 1)
+
+    def out_onward(stage):
+        for r, gather in enumerate(out_gathers):
+            gather.wait(stage)
+            if stage + 1 < k.bits:
+                gather.start(stage + 1)
+            for group in gather.arrivals(stage):
+                block = out_block(group, k.c * half + r)
+                at = r * groups + group
+                k.send(None, block, block, over_sends + at, over_recvs + at, k.sibling)
 
     def send_out(q):
         part = pl.ds(q * 16, 16)
@@ -652,124 +646,301 @@
 
     def came_in(q):
         exchanges[q].finish(lambda rank: gate_up.at[k.d, rank, pl.ds(q * 16, 16)])
-        for half in range(2):
-            gathers[q].start(half, 0)
-
-    def onward(q, stage):
-        for half in range(2):
-            gathers[q].wait(half, stage)
-            if stage + 1 < k.bits:
-                gathers[q].start(half, stage + 1)
+        for gather in gathers[q]:
+            gather.start(0)
+        if q + 2 < pieces:
+            send_out(q + 2)
+
+    gains_in = lambda rank: gains_all.at[k.d, rank]
+    qkv_in = lambda rank: qkv.at[k.d, rank]
+    k.barrier()
+    gains_ex.start(lambda rank: gains, gains_in)
+    qkv_ex.start(lambda rank: qkv_out.at[rank], qkv_in)
+    for h, gather in enumerate(downs):
+        gather.start(0, down_w.at[pl.ds(h * down_half, down_half)])
+    own_down = k.move(down_w, down_all.at[k.d])
+    gains_ex.finish(gains_in)
+    qkv_ex.finish(qkv_in)
+    out_line.start(out_w)
+    x_line.start(tokens)
+    own = [
+        k.move(out_w, out_block(k.d, k.f)),
+        k.move(tokens, x_all.at[pl.ds(pl.multiple_of(k.f * rows, 16), rows)]),
+    ]
+    for gather in late:
+        gather.start(0)
+    own_down()
+    onward(downs, 0)
+    for wait in own:
+        wait()
+    out_line.step(1)
+    x_line.step(1)
+    onward(late, 0)
+    for reach in range(2, k.chips):
+        out_line.step(reach)
+    out_line.finish()
+    for gather in out_gathers:
+        gather.start(0)
+    for q in range(min(2, pieces)):
+        x_line.step(2 + q)
+        send_out(q)
+    for reach in range(2 + min(2, pieces), k.chips):
+        x_line.step(reach)
+    for stage in range(1, k.bits):
+        onward(late, stage)
+    out_onward(0)
+    for stage in range(1, k.bits):
+        onward(downs, stage)
+    x_line.finish()
+    members = 128 // slice_width
+    for at in range(groups * ranks // members):
+        group, first = at * members // ranks, at * members % ranks
+        tile = gains_all[group, first].astype(F32)
+        for other in range(1, members):
+            tile = tile + gains_all[group, first + other].astype(F32)
+        gain_rows[:, at * 128 : (at + 1) * 128] = tile[:8]
 
     events = []
     for q in range(pieces):
-        events.append([lambda q=q: came_in(q)])
-        if q + 2 < pieces:
-            events[-1].append(lambda q=q: send_out(q + 2))
+        events.append(lambda q=q: came_in(q))
         if q > 0:
-            events[-1].append(lambda q=q: onward(q - 1, 0))
-        if q == pieces - 2 or pieces == 1:
-            events[-1].append(lambda: line.start(cotangent))
-    events.append([lambda: line.step(1), lambda: onward(pieces - 1, 0)])
-    for q in range(min(2, pieces)):
-        send_out(q)
-    blocks = values_t.shape[0]
-    plan = spaced(events, blocks)
+            events.append(lambda q=q: onward(gathers[q - 1], 0))
+    events.append(lambda: onward(gathers[pieces - 1], 0))
+    if k.bits == 2:
+        events.append(lambda: out_onward(1))
+    plan = spaced(events, 2 * blocks)
+    own = []
     for i in range(blocks):
         query = project_block(
-            i, x_all, gain, qkv, cosine, sine, normed, queries, keys, values, values_t
-        )
-        attend_block(i, rank_heads, query, keys, values_t, bias, attended, log_totals)
-        matmul_block(i, attended, out_w, parts)
-        for event in plan[i]:
-            for action in event:
-                action()
-    for reach in range(2, k.chips):
-        line.step(reach)
+            i, x_all, gain_rows, qkv, cosine, sine, normed, queries, keys, values, values_t
+        )
+        for event in plan[2 * i]:
+            event()
+        attend_block(i, rank_heads, query, keys, values_t, length, attended, log_totals)
+        mine = attended.at[pl.ds(i * BLOCK, BLOCK)]
+        lines[i].start(mine)
+        own.append(k.move(mine, attended_block(i, k.f)))
+        for reach in range(1, k.chips):
+            if i - reach >= 0:
+                lines[i - reach].step(reach)
+        for event in plan[2 * i + 1]:
+            event()
+    for i in range(blocks, blocks + k.chips - 1):
+        for reach in range(1, k.chips):
+            if 0 <= i - reach < blocks:
+                lines[i - reach].step(reach)
     for stage in range(1, k.bits):
-        for q in range(pieces):
-            onward(q, stage)
-    own()
-    line.finish()
-    k.finish()
-
-
-def sub_lines(k, subs, rows, parts, mine, held, landed, gathered):
-    scatters, gathers = [], []
-    for sub in range(subs):
-        part = pl.ds(sub * rows, rows)
-        scatters.append(
-            LineScatter(
-                k,
-                lambda rank, part=part: parts.at[rank, part],
-                lambda chip, part=part: mine.at[chip, part],
-                lambda chip, part=part: held.at[chip, part],
-                lambda side, chip, part=part: landed.at[side, chip, part],
-            )
-        )
-        gathers.append(LineGather(k, lambda rank, part=part: gathered.at[rank, part]))
-    return scatters, gathers
-
-
-def hidden_kernel(groups, ranks, subs, parts, tokens, gain, hidden, normed_all, mine, held, landed, normed, sends, recvs):
-    k = Links(groups, ranks, sends, recvs)
-    rows = tokens.shape[0] // subs
-    scatters, gathers = sub_lines(k, subs, rows, parts, mine, held, landed, normed_all)
-    k.barrier()
-    for scatter in scatters:
-        scatter.start()
-    own = []
-    for turn in range(subs + 1):
-        if turn < subs:
-            scatters[turn].pair()
-        for i in range(k.chips - 1):
-            if turn < subs:
-                scatters[turn].step(i)
-            if turn > 0:
-                gathers[turn - 1].step(i + 1)
-        if turn < subs:
-            scatters[turn].last()
-
-            def rows_of(part):
-                total = tokens[part].astype(F32) + held[k.z, part].astype(F32)
-                hidden[part] = total
-                scaled = total * inverse_rms(total)
-                normed[part] = (scaled * gain[...]).astype(BF16)
-
-            row_loop(rows, rows_of, first=turn * rows)
-            piece = pl.ds(turn * rows, rows)
-            gathers[turn].start(normed.at[piece])
-            own.append(k.move(normed.at[piece], normed_all.at[k.f, piece]))
-    for gather in gathers:
-        gather.finish()
+        if k.bits > 2:
+            out_onward(stage)
+        for several in gathers:
+            onward(several, stage)
+    for r in range(half):
+        for i in range(1, groups):
+            group = lax.rem(k.d + i, groups)
+            block = out_block(group, (1 - k.c) * half + r)
+            k.arrived(None, block, over_recvs + r * groups + group)
     for wait in own:
         wait()
+    for line in lines:
+        line.finish()
     k.finish()
 
 
-def middle_kernel(
-    groups, ranks, subs, parts, hidden, grad_out, gain, grad_gate_up,
-    grad_all, grad_hidden, sums, gate_up_sum,
-    mine, held, landed, rounded, gate_up_landed, sends, recvs,
+def feed_forward_kernel(
+    groups, ranks, attended_all, x_all, grad_out, out_w, gate_up, down_w, gain,
+    grad_out_all, hidden, normed, mixed, grad_gate_up, down_parts, parts,
+    attended_in, x_in, grad_in, hidden_b, normed_b, mixed_b, grad_b, down_b, parts_b, local, sends, recvs,
 ):
     k = Links(groups, ranks, sends, recvs)
-    rows = hidden.shape[0] // subs
-    scatters, gathers = sub_lines(k, subs, rows, parts, mine, held, landed, grad_all)
+    chips, rows = k.chips, hidden_b.shape[0]
+    width, units = out_w.shape[0], down_w.shape[0]
+    line = LineGather(k, lambda rank: grad_out_all.at[rank])
+    k.barrier()
+
+    def chip(t):
+        up = lax.rem(k.z + t, chips)
+        down = lax.rem(k.z + chips - t, chips)
+        return jnp.where(k.z < chips // 2, up, down)
+
+    def span(t):
+        return pl.ds(pl.multiple_of(chip(t) * rows, rows), rows)
+
+    def loads(t):
+        return [
+            pltpu.make_async_copy(ref.at[span(t)], buffer.at[t % 2], local.at[2 * n + t % 2])
+            for n, (ref, buffer) in enumerate(((attended_all, attended_in), (x_all, x_in)))
+        ]
+
+    results = ((hidden_b, hidden), (normed_b, normed), (mixed_b, mixed), (grad_b, grad_gate_up), (down_b, down_parts), (parts_b, parts))
+
+    def store(t, n):
+        buffer, ref = results[n]
+        return pltpu.make_async_copy(buffer, ref.at[span(t)], local.at[4 + n])
+
+    for load in loads(0):
+        load.start()
+    line.start(grad_out)
+    own = k.move(grad_out, grad_out_all.at[k.f])
+    own()
+    step = 512
+    for t in range(chips):
+        if t + 1 < chips:
+            for load in loads(t + 1):
+                load.start()
+        for load in loads(t):
+            load.wait()
+        if t > 0:
+            store(t - 1, 0).wait()
+
+        @pl.loop(0, width // step)
+        def _(c):
+            part = pl.ds(pl.multiple_of(c * step, step), step)
+            hidden_b[:, part] = x_in[t % 2, :, part].astype(F32) + dot(
+                attended_in[t % 2], out_w[:, part]
+            )
+
+        store(t, 0).start()
+        if t > 0:
+            store(t - 1, 1).wait()
+            line.step(t)
+
+        def normalise(part):
+            total = hidden_b[part, :]
+            normed_b[part, :] = (total * inverse_rms(total) * gain[...]).astype(BF16)
+
+        row_loop(rows, normalise)
+        store(t, 1).start()
+        line.over(chip(t))
+        place = chip(t) * 2
+        fetch = [
+            pltpu.make_async_copy(
+                grad_out_all.at[place + c], grad_in.at[pl.ds(c * (rows // 2), rows // 2)], local.at[10 + c]
+            )
+            for c in range(2)
+        ]
+        for copy in fetch:
+            copy.start()
+        for copy in fetch:
+            copy.wait()
+        if t > 0:
+            store(t - 1, 2).wait()
+            store(t - 1, 3).wait()
+
+        @pl.loop(0, units // BLOCK)
+        def _(u):
+            part = pl.ds(pl.multiple_of(u * BLOCK, BLOCK), BLOCK)
+            far = pl.ds(pl.multiple_of(units + u * BLOCK, BLOCK), BLOCK)
+            gate = dot(normed_b[...], gate_up[:, part])
+            up = dot(normed_b[...], gate_up[:, far])
+            grad_mixed = cols_inner(grad_in[...], down_w[part, :])
+            sigmoid = 1.0 / (1.0 + jnp.exp(-gate))
+            silu = gate * sigmoid
+            mixed_b[:, part] = (silu * up).astype(BF16)
+            grad_b[:, part] = (
+                grad_mixed * up * (sigmoid * (1.0 + gate * (1.0 - sigmoid)))
+            ).astype(BF16)
+            grad_b[:, far] = (grad_mixed * silu).astype(BF16)
+
+        store(t, 2).start()
+        store(t, 3).start()
+        if t > 0:
+            store(t - 1, 4).wait()
+            store(t - 1, 5).wait()
+
+        @pl.loop(0, width // step)
+        def _(c):
+            part = pl.ds(pl.multiple_of(c * step, step), step)
+            down_b[:, part] = dot(mixed_b[...], down_w[:, part]).astype(BF16)
+            parts_b[:, part] = cols_inner(grad_b[...], gate_up[part, :]).astype(BF16)
+
+        store(t, 4).start()
+        store(t, 5).start()
+    for n in range(len(results)):
+        store(chips - 1, n).wait()
+    k.finish()
+
+
+def middle_kernel(
+    groups, ranks, parts, down_parts, hidden_all, grad_out, gain, normed, grad_gate_up,
+    grad_all, grad_hidden, output, sums, gate_up_sum,
+    mine, held, landed, down_held, down_landed, rounded, hidden, tile, grad_w, gate_up_landed, local, sends, recvs,
+):
+    k = Links(groups, ranks, sends, recvs)
+    rows = hidden.shape[0]
+    depth = grad_w.shape[2]
+    scatter = LineScatter(
+        k,
+        lambda rank: parts.at[rank],
+        lambda chip: mine.at[chip],
+        lambda chip: held.at[chip],
+        lambda side, chip: landed.at[side, chip],
+    )
+    down_scatter = LineScatter(
+        k,
+        lambda rank: down_parts.at[rank],
+        lambda chip: mine.at[chip],
+        lambda chip: down_held.at[chip],
+        lambda side, chip: down_landed.at[side, chip],
+    )
+    gather = LineGather(k, lambda rank: grad_all.at[rank])
     gate_up_sums = [
         GroupScatter(
             k,
-            lambda group, n=n: grad_gate_up.at[group, n],
+            lambda group, n=n: grad_w.at[group, n],
             lambda i, n=n: gate_up_landed.at[n, i],
             n % 2 == 1,
         )
         for n in range(ranks)
     ]
+    per_group = ranks * depth // BLOCK
+    tiles = [(q, g) for q in range(per_group) for g in range(groups)]
+    per_tile = BLOCK // depth
+
+    def load(i):
+        q, g = tiles[i]
+        return pltpu.make_async_copy(
+            normed.at[:, pl.ds((g * per_group + q) * BLOCK, BLOCK)], tile.at[i % 2], local.at[i % 2]
+        )
+
+    own_hidden = pltpu.make_async_copy(
+        hidden_all.at[pl.ds(pl.multiple_of(k.f * rows, rows), rows)], hidden, local.at[2]
+    )
+    load(0).start()
+    own_hidden.start()
     k.barrier()
-    for scatter in scatters:
-        scatter.start()
-    for sums_of in gate_up_sums:
-        sums_of.start(0)
+    scatter.start()
+
+    def weight_tile(i):
+        q, g = tiles[i]
+        if i + 1 < len(tiles):
+            load(i + 1).start()
+        load(i).wait()
+        flipped = tile[i % 2].astype(F32).T.astype(BF16)
+        step = 512
+
+        @pl.loop(0, grad_gate_up.shape[1] // step)
+        def _(c):
+            part = pl.ds(pl.multiple_of(c * step, step), step)
+            total = dot(flipped, grad_gate_up[:, part]).astype(BF16)
+            for n in range(per_tile):
+                grad_w[g, q * per_tile + n, :, part] = total[n * depth : (n + 1) * depth]
+
+        if g == groups - 1:
+            for n in range(per_tile):
+                gate_up_sums[q * per_tile + n].start(0)
+
+    weight_tile(0)
+    scatter.pair()
+    scatter.step(0)
+    spots = spaced(list(range(1, len(tiles))), k.chips - 1)
+    for i in range(k.chips - 1):
+        for place in spots[i]:
+            weight_tile(place)
+        if i > 0:
+            scatter.step(i)
+    scatter.last()
     sums[...] = jnp.zeros_like(sums)
+    own_hidden.wait()
 
     def rows_of(part):
         total = hidden[part]
@@ -781,25 +952,24 @@
         grad_hidden[part] = grad_total
         rounded[part] = grad_total.astype(BF16)
 
-    own = []
-    for turn in range(subs + 1):
-        if turn < subs:
-            scatters[turn].pair()
-        for i in range(k.chips - 1):
-            if turn < subs:
-                scatters[turn].step(i)
-            if turn > 0:
-                gathers[turn - 1].step(i + 1)
-        if turn < subs:
-            scatters[turn].last()
-            row_loop(rows, rows_of, first=turn * rows)
-            piece = pl.ds(turn * rows, rows)
-            gathers[turn].start(rounded.at[piece])
-            own.append(k.move(rounded.at[piece], grad_all.at[k.f, piece]))
-        if turn == subs - 1:
+    row_loop(rows, rows_of)
+    gather.start(rounded)
+    down_scatter.start()
+    own = k.move(rounded, grad_all.at[k.f])
+    down_scatter.pair()
+    for i in range(k.chips - 1):
+        down_scatter.step(i)
+        gather.step(i + 1)
+        if i == 0:
             for sums_of in gate_up_sums:
                 sums_of.wait(0)
                 sums_of.start(1)
+    down_scatter.last()
+
+    def out_rows(part):
+        output[part] = (hidden[part] + down_held[k.z, part].astype(F32)).astype(BF16)
+
+    row_loop(rows, out_rows)
     for stage in range(1, k.bits):
         for n, sums_of in enumerate(gate_up_sums):
             if stage + 1 < k.bits:
@@ -807,18 +977,16 @@
                 sums_of.start(stage + 1)
             else:
                 sums_of.wait(stage, gate_up_sum.at[n])
-    for gather in gathers:
-        gather.finish()
-    for wait in own:
-        wait()
+    gather.finish()
+    own()
     k.finish()
 
 
 def attend_back_kernel(
-    groups, ranks, rank_heads, grad_hidden, out_w, queries, keys, values, attended, bias, log_totals,
+    groups, ranks, rank_heads, lengths, out_all, grad_hidden, queries, keys, values, attended, log_totals,
     cosine, sine, qkv, normed, gate_up_sum, grad_down,
     parts, grad_qkv_w, grad_out_w, gate_up_grad, down_grad,
-    grad_qkv, keys_t, grad_keys, grad_values, down_landed, sends, recvs,
+    out_w, grad_qkv, keys_t, grad_keys, grad_values, down_landed, sends, recvs,
 ):
     k = Links(groups, ranks, sends, recvs)
     pieces = down_landed.shape[0]
@@ -834,6 +1002,9 @@
     ]
     exchange = Exchange(k)
     gate_up_in = lambda rank: gate_up_grad.at[rank]
+    length = lengths[0]
+    cols = queries.shape[1]
+    fetch = k.move(out_all.at[pl.ds(pl.multiple_of(k.f * cols, cols), cols)], out_w)
     k.barrier()
     exchange.start(lambda rank: gate_up_sum.at[rank], gate_up_in)
     for sums_of in down_sums:
@@ -842,6 +1013,8 @@
     grad_keys[...] = jnp.zeros_like(grad_keys)
     grad_values[...] = jnp.zeros_like(grad_values)
 
+    fetch()
+
     @pl.loop(0, blocks)
     def _(i):
         block = pl.ds(pl.multiple_of(i * BLOCK, BLOCK), BLOCK)
@@ -850,7 +1023,7 @@
     @pl.loop(0, blocks)
     def _(i):
         attend_back_rows(
-            i, rank_heads, grad_hidden, out_w, queries, keys, keys_t, values, attended, bias, log_totals,
+            i, rank_heads, grad_hidden, out_w, queries, keys, keys_t, values, attended, length, log_totals,
             cosine, sine, grad_keys, grad_values, grad_qkv,
         )
 
@@ -984,15 +1157,17 @@
 
 VMEM = pl.BlockSpec(memory_space=pltpu.VMEM)
 ANY = pl.BlockSpec(memory_space=pl.ANY)
-
-
-def call(kernel, identity, ins, outs, scratch, semaphores, args):
+SMEM = pl.BlockSpec(memory_space=pltpu.SMEM)
+
+
+def call(kernel, identity, ins, outs, scratch, semaphores, args, local=0):
     return pl.pallas_call(
         kernel,
         out_shape=[jax.ShapeDtypeStruct(shape, kind) for shape, kind, _ in outs],
         in_specs=ins,
         out_specs=[place for _, _, place in outs],
         scratch_shapes=[pltpu.VMEM(shape, kind) for shape, kind in scratch]
+        + [pltpu.SemaphoreType.DMA((local,))] * (local > 0)
         + [pltpu.SemaphoreType.DMA((semaphores,))] * 2,
         compiler_params=pltpu.CompilerParams(
             collective_id=identity, has_side_effects=True, vmem_limit_bytes=60 * 1024 * 1024
@@ -1031,16 +1206,6 @@
 
         span = [[base * split + i for i in range(split)] for base in range(ranks // split)]
 
-        def widen(weight):
-            if split > 1:
-                weight = lax.all_gather(weight, "fsdp", axis=0, tiled=True, axis_index_groups=span)
-            return weight
-
-        def narrow(whole):
-            if split > 1:
-                whole = whole.reshape(split, -1, width)[lax.rem(rank, split)]
-            return whole
-
         def place_output(grad):
             if split > 1:
                 place = lax.rem(rank, split)
@@ -1055,126 +1220,116 @@
         slice_width = norm_attn.shape[0]
         qkv_out = jnp.concatenate([heads_out(w) for w in (w_query, w_key, w_value)], -1)
         gate_up_out = jnp.concatenate([units_out(w) for w in (w_gate, w_up)], -1)
-        gains = jnp.pad(
-            jnp.stack([norm_attn, norm_mlp]), ((0, 14), (0, 128 - slice_width))
-        )
-        out_own = widen(w_output)
-        x_all, qkv, gains_all, out_w, down_w = call(
-            functools.partial(first_kernel, groups, ranks),
-            1,
-            [VMEM] * 5,
-            [
-                ((ranks, rows, width), BF16, ANY),
-                ((groups,) + qkv_out.shape, BF16, ANY),
-                ((groups, ranks, 16, 128), BF16, ANY),
-                ((groups,) + out_own.shape, BF16, ANY),
-                ((groups,) + w_down.shape, BF16, ANY),
-            ],
-            [],
-            160,
-            (tokens, qkv_out, gains, out_own, w_down),
-        )
-        qkv = qkv.reshape(width, -1)
-        gain_one, gain_two = (
-            gains_all[:, :, i, :slice_width].astype(F32).reshape(1, width) for i in range(2)
-        )
-        out_w = narrow(out_w.reshape(-1, width))
-        down_w = down_w.reshape(-1, width)
-
-        places = jnp.arange(count, dtype=jnp.int32)
-        bias = jnp.where(places < lengths[0], 0.0, -1000000000.0).astype(F32)[:, None]
-        cosine, sine = wide_tables(count, head_cols)
+        place = (lax.axis_index("dp") * ranks + rank) * slice_width % 128
+        gains = lax.dynamic_update_slice(
+            jnp.zeros((16, 128), BF16), jnp.stack([norm_attn, norm_mlp]), (0, place)
+        )
+        cosine, sine = (jnp.asarray(table) for table in wide_tables(count))
         blocks = count // BLOCK
         heads_shape = ((count, head_cols), BF16, VMEM)
-        parts, normed_one, queries, keys, values, attended, log_totals, cotangent_all, gate_up = call(
-            functools.partial(attend_kernel, groups, ranks, rank_heads),
+        (
+            x_all, qkv, gain_rows, normed_one, queries, keys, values, attended, log_totals,
+            attended_all, gate_up, out_all, down_w,
+        ) = call(
+            functools.partial(attend_kernel, groups, ranks, rank_heads, slice_width),
             5,
-            [VMEM] * 9,
-            [((count, width), BF16, VMEM)] * 2
+            [SMEM] + [VMEM] * 8,
+            [
+                ((count, width), BF16, VMEM),
+                ((groups,) + qkv_out.shape, BF16, VMEM),
+                ((8, width), F32, VMEM),
+                ((count, width), BF16, VMEM),
+            ]
             + [heads_shape] * 4
             + [
                 ((blocks, rank_heads, BLOCK), F32, VMEM),
-                ((ranks, rows, width), BF16, ANY),
+                ((count, width), BF16, ANY),
                 ((groups,) + gate_up_out.shape, BF16, ANY),
+                ((groups * ranks, out_rows, width), BF16, ANY),
+                ((groups,) + w_down.shape, BF16, ANY),
             ],
-            [((blocks, head_cols, BLOCK), BF16)],
-            192,
-            (
-                x_all.reshape(count, width),
-                cotangent,
-                gate_up_out,
-                qkv,
-                gain_one,
-                out_w,
-                cosine,
-                sine,
-                bias,
-            ),
-        )
+            [
+                ((groups, ranks, 16, 128), BF16),
+                ((blocks, head_cols, BLOCK), BF16),
+            ],
+            448,
+            (lengths, tokens, qkv_out, gains, w_output, w_down, gate_up_out, cosine, sine),
+        )
+        qkv = qkv.reshape(width, -1)
+        gain_one, gain_two = gain_rows[0:1], gain_rows[1:2]
         gate_up = gate_up.reshape(width, -1)
-        line_scratch = [((chips, rows, width), BF16)] * 2 + [((2, chips, rows, width), BF16)]
-        hidden, normed_two = call(
-            functools.partial(hidden_kernel, groups, ranks, 2),
-            2,
-            [ANY] + [VMEM] * 2,
-            [((rows, width), F32, VMEM), ((ranks, rows, width), BF16, ANY)],
-            line_scratch + [((rows, width), BF16)],
-            160,
-            (parts.reshape(ranks, rows, width), tokens, gain_two),
-        )
-        normed_two = normed_two.reshape(count, width)
-        gate_up_lin = dot(normed_two, gate_up)
-        gate, up = gate_up_lin[:, :unit_cols], gate_up_lin[:, unit_cols:]
-        sigmoid = 1.0 / (1.0 + jnp.exp(-gate))
-        silu = gate * sigmoid
-        mixed = (silu * up).astype(BF16)
-        down_sum = lax.psum_scatter(
-            dot(mixed, down_w).astype(BF16), "fsdp", scatter_dimension=0, tiled=True
-        )
-        output = (hidden + down_sum.astype(F32)).astype(BF16)
-
-        live = places[:, None] < lengths[0]
-        grad_out_all = jnp.where(
-            live, cotangent_all.reshape(count, width), jnp.zeros((), BF16)
-        )
+        out_all = out_all.reshape(width, width)
+        down_w = down_w.reshape(-1, width)
         own_places = rank * rows + jnp.arange(rows, dtype=jnp.int32)
         grad_out = jnp.where(own_places[:, None] < lengths[0], cotangent, jnp.zeros((), BF16))
-        grad_mixed = cols_inner(grad_out_all, down_w)
-        grad_down = rows_inner(mixed, grad_out_all).astype(BF16).reshape(groups, hidden_part, width)
-        grad_gate = grad_mixed * up * (sigmoid * (1.0 + gate * (1.0 - sigmoid)))
-        grad_up = grad_mixed * silu
-        grad_gate_up = jnp.concatenate([grad_gate.astype(BF16), grad_up.astype(BF16)], -1)
-        parts = cols_inner(grad_gate_up, gate_up).astype(BF16).reshape(ranks, rows, width)
-        grad_gate_up_w = rows_inner(normed_two, grad_gate_up).astype(BF16)
-        grad_hidden_all, grad_hidden, sums_two, gate_up_sum = call(
-            functools.partial(middle_kernel, groups, ranks, 2),
+        pair = 2 * rows
+        grad_out_all, hidden, normed_two, mixed, grad_gate_up, down_parts, parts = call(
+            functools.partial(feed_forward_kernel, groups, ranks),
+            2,
+            [ANY] * 2 + [VMEM] * 5,
+            [
+                ((ranks, rows, width), BF16, ANY),
+                ((count, width), F32, ANY),
+                ((count, width), BF16, ANY),
+                ((count, unit_cols), BF16, ANY),
+                ((count, 2 * unit_cols), BF16, ANY),
+                ((count, width), BF16, ANY),
+                ((count, width), BF16, ANY),
+            ],
+            [
+                ((2, pair, width), BF16),
+                ((2, pair, width), BF16),
+                ((pair, width), BF16),
+                ((pair, width), F32),
+                ((pair, width), BF16),
+                ((pair, unit_cols), BF16),
+                ((pair, 2 * unit_cols), BF16),
+                ((pair, width), BF16),
+                ((pair, width), BF16),
+            ],
+            64,
+            (attended_all, x_all, grad_out, out_all, gate_up, down_w, gain_two),
+            local=12,
+        )
+        grad_down = rows_inner(mixed, grad_out_all.reshape(count, width)).astype(BF16)
+        line_scratch = [((chips, rows, width), BF16), ((2, chips, rows, width), BF16)]
+        grad_hidden_all, grad_hidden, output, sums_two, gate_up_sum = call(
+            functools.partial(middle_kernel, groups, ranks),
             3,
-            [ANY] + [VMEM] * 4,
+            [ANY] * 3 + [VMEM] * 2 + [ANY, VMEM],
             [
                 ((ranks, rows, width), BF16, ANY),
                 ((rows, width), F32, VMEM),
+                ((rows, width), BF16, VMEM),
                 ((1, width), F32, VMEM),
                 ((ranks, depth, 2 * unit_cols), BF16, VMEM),
             ],
-            line_scratch
+            [((chips, rows, width), BF16)]
+            + line_scratch * 2
             + [
                 ((rows, width), BF16),
+                ((rows, width), F32),
+                ((2, count, BLOCK), BF16),
+                ((groups, ranks, depth, 2 * unit_cols), BF16),
                 ((ranks, groups - 1, depth, 2 * unit_cols), BF16),
             ],
             160,
             (
-                parts,
+                parts.reshape(ranks, rows, width),
+                down_parts.reshape(ranks, rows, width),
                 hidden,
                 grad_out,
                 gain_two,
-                grad_gate_up_w.reshape(groups, ranks, depth, 2 * unit_cols),
+                normed_two,
+                grad_gate_up,
             ),
+            local=3,
         )
         pieces = 4
         parts, grad_qkv_w, grad_out_w, grad_gate_up_w, grad_w_down = call(
             functools.partial(attend_back_kernel, groups, ranks, rank_heads),
             6,
-            [VMEM] * 14,
+            [SMEM, ANY] + [VMEM] * 12,
             [
                 ((count, width), BF16, VMEM),
                 ((width, 3 * head_cols), BF16, VMEM),
@@ -1183,6 +1338,7 @@
                 ((hidden_part, width), F32, VMEM),
             ],
             [
+                ((head_cols, width), BF16),
                 ((count, 3 * head_cols), BF16),
                 ((blocks, head_cols, BLOCK), BF16),
                 ((count, head_cols), F32),
@@ -1191,20 +1347,20 @@
             ],
             160,
             (
+                lengths,
+                out_all,
                 grad_hidden_all.reshape(count, width),
-                out_w,
                 queries,
                 keys,
                 values,
                 attended,
-                bias,
                 log_totals,
                 cosine,
                 sine,
                 qkv,
                 normed_one,
                 gate_up_sum,
-                grad_down,
+                grad_down.reshape(groups, hidden_part, width),
             ),
         )
         grad_out_w = place_output(grad_out_w)
@@ -1224,7 +1380,8 @@
                 ((out_rows, width), F32, VMEM),
                 (tile, F32, VMEM),
             ],
-            line_scratch
+            [((chips, rows, width), BF16)]
+            + line_scratch
             + [
                 ((1, width), F32),
                 ((ranks, groups - 1, depth, 3 * head_cols), BF16),

time: 715 us -> 625 us (0.87)
  matrix products: 77.4 us -> 9.83 us
  between operations: 15.6 us -> 2.13 us
  local copies, waits for them, and re-layouts: 47.2 us -> 36.6 us
  other arithmetic: 18.4 us -> 8.69 us
    dot_general x4 -> x0, matrix products: 52.6 us -> none  [the longest x2 27.7 us: cols_inner(): lax.dot_general(left, right, (((1,), (1,)), ((), ())), preferred_element_...]
    dot_general x2 -> x1, matrix products: 24.9 us -> 9.83 us  [rows_inner(): lax.dot_general(left, right, (((0,), (0,)), ((), ())), preferred_element_...]
    pallas_call x6 -> x5, Pallas kernels: 553 us -> 559 us  [call(): pl.pallas_call(kernel, out_shape=[jax.ShapeDtypeStruct(shape, kind) for s...]
  transfers between devices with their start and end apart: 1 -> 0, of which waited for: 0 -> 0; matrix products, arithmetic and copies ran while one was open for 10% -> 0% of each run, Pallas kernels for 36% -> 0%
where the time goes in v3:
time: 625 us; the launch traced here: 617 us
  Pallas kernels  559 us (89%)
  local copies, waits for them, and re-layouts  36.6 us (6%)
  matrix products  9.83 us (2%)
  other arithmetic  8.69 us (1%)
    pallas_call x5, Pallas kernels, call(): pl.pallas_call(kernel, out_shape=[jax.ShapeDtypeStruct(shape, kind) for s...  559 us

profile of v3, /device:TPU:0, one launch (start us, length us, event | category | flops | bytes accessed | tf_op | source)
XLA Modules:
  0.0 616.6 jit_solution(14852971989543300964)
XLA Ops:
  0.6 0.0 copy-start.7
  1.4 0.7 pad_maximum_fusion.2
  2.1 0.3 dynamic_update_slice.3.gains
  2.4 0.0 copy-start.9
  2.4 0.0 copy-start.8
  2.4 1.5 reshape.124
  3.9 0.2 copy.48
  4.1 0.3 reshape.125
  4.5 0.0 copy-done.7
  4.5 0.5 reshape.126
  5.0 0.2 copy.47
  5.2 0.0 copy-start.3
  5.2 0.3 reshape.127
  5.6 0.0 copy-done.9
  5.6 0.0 copy-done.8
  5.6 0.0 copy-start.1
  5.6 0.5 reshape.128
  6.1 0.2 copy.46
  6.3 0.3 reshape.129
  6.7 0.9 pad_maximum_fusion.1.qkv_out
  7.6 0.0 copy-done.3
  7.6 1.0 broadcast_select_fusion.grad_out
  8.6 0.3 copy.35
  8.8 0.0 copy-start.2
  8.8 0.4 copy.45
  9.2 0.8 reshape.131
  10.0 0.0 copy-done.2
  10.0 0.3 copy.36
  10.3 0.4 copy.44
  10.7 0.8 reshape.133
  11.5 1.5 pad_maximum_fusion.gate_up_out
  13.0 204.5 %shard_map.221 = (bf16[1280,2048]{1,0:T(8,128)(2,1)}, bf16[4,8,64,768]{3,2,1,0:T(8,128)(2,1)}, f32[8,2048]{1,0:T(8,128)}, bf16[1280,2048]{1,0:T(8,128)(2,1)}, bf...) custom-call(s32[1]{0:T(128)} %copy.54.lengths, ...), custom_call_target="tpu_custom_call" | custom-call | tf_op jit(solution)/shard_map/pallas_call | solution.py:1164
  217.5 1.5 fusion
  219.1 83.9 %shard_map.222 = (bf16[8,160,2048]{2,1,0:T(8,128)(2,1)}, f32[1280,2048]{1,0:T(8,128)}, bf16[1280,2048]{1,0:T(8,128)(2,1)}, bf16[1280,1024]{1,0:T(8,128)(2,1)}, b...) custom-call(bf16[1280,2048]{1,0:T(8,128)(2,1)} %get-tuple-element.45.attended_all, ...), custom_call_target="tpu_custom_call" | custom-call | tf_op jit(solution)/shard_map/pallas_call | solution.py:1164
  303.0 123.3 %shard_map.223 = (bf16[8,160,2048]{2,1,0:T(8,128)(2,1)}, f32[160,2048]{1,0:T(8,128)}, bf16[160,2048]{1,0:T(8,128)(2,1)}, f32[1,2048]{1,0:T(1,128)}, bf16[8,64,2048]{2,1,0:T(8,128)(2,1)}) custom-call(bf16[8,160,2048]{2,1,0:T(8,128)(2,1)} %bitcast.81, bf16[8,160,2048]{2,1,0:T(8,128)(2,1)} %bitcast.80, f32[1280,2048]{1,0:T(8,128)} %get-tuple-element.53.hidden_all, ...), custom_call_target="tpu_custom_call" | custom-call | tf_op jit(solution)/shard_map/pallas_call | solution.py:1164
  426.3 0.0 copy-done.10
  426.3 9.8 %convolution_convert_fusion = bf16[1024,2048]{1,0:T(8,128)(2,1)} fusion(bf16[1280,1024]{1,0:T(8,128)(2,1)S(1)} %copy-done.10, bf16[1280,2048]{1,0:T(8,128)(2,1)} %bitcast.102), kind=kOutput, calls=%fused_computation | convolution fusion | flops 5370806272 | bytes 12058624 | tf_op jit(solution)/shard_map/dot_general | solution.py:26
  436.2 59.0 %shard_map.224 = (bf16[1280,2048]{1,0:T(8,128)(2,1)}, bf16[2048,768]{1,0:T(8,128)(2,1)}, bf16[256,2048]{1,0:T(8,128)(2,1)}, bf16[8,64,2048]{2,1,0:T(8,128)(2,1)}, f32[256,2048]{1,0:T(8,128)}) custom-call(s32[1]{0:T(128)} %copy.54.lengths, bf16[2048,2048]{1,0:T(8,128)(2,1)} %bitcast.73, bf16[1280,2048]{1,0:T(8,128)(2,1)} %bitcast.79, ...), custom_call_target="tpu_custom_call" | custom-call | tf_op jit(solution)/shard_map/pallas_call | solution.py:1164
  495.2 88.6 %shard_map.225 = (bf16[160,2048]{1,0:T(8,128)(2,1)}, bf16[8,64,768]{2,1,0:T(8,128)(2,1)}, f32[64,2048]{1,0:T(8,128)}, f32[8,128]{1,0:T(8,128)}) custom-call(bf16[8,160,2048]{2,1,0:T(8,128)(2,1)} %bitcast.82, bf16[160,2048]{1,0:T(8,128)(2,1)} %tokens.3, f32[160,2048]{1,0:T(8,128)} %get-tuple-element.69.grad_hidden, f32[1,2048]{1,0:T(1,128)} %get-tuple-element.84.gain, ...), custom_call_target="tpu_custom_call" | custom-call | tf_op jit(solution)/shard_map/pallas_call | solution.py:1164
  583.8 0.8 constant_dynamic-slice_fusion
  584.5 0.5 slice_bitcast_fusion
  585.0 1.3 slice_convert_fusion.2
  586.3 0.5 reshape.153
  586.8 0.6 copy.32
  587.4 1.2 reshape.148
  588.6 0.5 reshape.152
  589.0 0.6 copy.31
  589.6 1.2 reshape.147
  590.8 0.5 reshape.151
  591.2 0.6 copy.30
  591.8 1.2 reshape.146
  593.0 3.3 slice_convert_fusion
  596.3 3.2 reshape.155
  599.5 2.8 copy.34
  602.3 2.5 copy.38
  604.8 2.2 reshape.154
  607.0 2.8 copy.33
  609.8 2.5 copy.37
  612.4 0.0 copy-done.4
  612.4 0.8 copy.55
  613.2 0.8 copy.56
  614.0 0.8 copy.57
  614.8 0.0 copy-done
  614.8 1.3 copy.58
  (10 shorter events, 0.0 us)
Async XLA Ops:
  0.6 3.8 copy-start.7
  2.4 3.2 copy-start.9
  2.4 3.2 copy-start.8
  5.2 2.4 copy-start.3
  5.6 3.0 copy-start.1
  8.8 1.2 copy-start.2
  303.0 123.3 %copy-start.10 = (bf16[1280,1024]{1,0:T(8,128)(2,1)S(1)}, bf16[1280,1024]{1,0:T(8,128)(2,1)}, u32[]{:S(2)}) copy-start(bf16[1280,1024]{1,0:T(8,128)(2,1)} %get-tuple-element.66) | copy-start | bytes 7864324
  609.8 2.5 copy-start.4
  609.8 3.4 copy-start.5
  609.8 4.2 copy-start.6
  612.4 2.5 copy-start

commit v4 on v3

--- a/solution.py
+++ b/solution.py
@@ -208,20 +208,14 @@
     ).astype(BF16)
 
 
-def finish_back_rows(i, qkv, cosine, sine, grad_keys, grad_values, grad_qkv, parts):
+def finish_back_rows(i, cosine, sine, grad_keys, grad_values, grad_qkv):
     block = pl.ds(pl.multiple_of(i * BLOCK, BLOCK), BLOCK)
     cols = grad_keys.shape[1]
     grad_qkv[block, cols : 2 * cols] = turn_halves(
         grad_keys[block, :], table_rows(cosine, block, cols), -table_rows(sine, block, cols)
     ).astype(BF16)
     grad_qkv[block, 2 * cols :] = grad_values[block, :].astype(BF16)
-    rows = grad_qkv[block, :]
-    step = 512
-
-    @pl.loop(0, qkv.shape[0] // step)
-    def _(c):
-        part = pl.ds(pl.multiple_of(c * step, step), step)
-        parts[block, part] = cols_inner(rows, qkv[part, :]).astype(BF16)
+
 
 MESH = pl.DeviceIdType.MESH
 
@@ -370,68 +364,78 @@
 
 
 class LineScatter:
-    def __init__(self, links, parts, mine, held, landed):
-        self.links, self.parts, self.mine = links, parts, mine
-        self.held, self.landed = held, landed
+    def __init__(self, links, mine, held, landed):
+        self.links, self.mine, self.held, self.landed = links, mine, held, landed
         chips = links.chips
         self.sends, self.recvs = links.take(2 * chips, 3 * chips)
         self.gone = [lambda: None] * 2
-
-    def start(self):
-        k, chips = self.links, self.links.chips
-        for chip in range(chips):
-            k.send(
-                None,
-                self.parts(chip * 2 + 1 - k.c),
-                self.held(chip),
-                self.sends + chip,
-                self.recvs + chip,
-                k.sibling,
-            )
-        self.own = [k.move(self.parts(chip * 2 + k.c), self.mine(chip)) for chip in range(chips)]
-
-    def pair(self):
+        self.own = {}
+
+    def give(self, chip, other, later=True):
+        k = self.links
+        return k.send(
+            None, other, self.held(chip), self.sends + chip, self.recvs + chip, k.sibling, later=later
+        )
+
+    def start(self, parts):
         k = self.links
         for chip in range(k.chips):
+            self.give(chip, parts(chip * 2 + 1 - k.c))
+            self.own[chip] = k.move(parts(chip * 2 + k.c), self.mine(chip))
+
+    def pair(self, chip, mine=None):
+        k = self.links
+        k.arrived(None, self.held(chip), self.recvs + chip)
+        add_rows(self.held(chip), self.held(chip), self.mine(chip) if mine is None else mine)
+
+    def pairs(self):
+        for chip in range(self.links.chips):
             self.own[chip]()
-            k.arrived(None, self.held(chip), self.recvs + chip)
-            add_rows(self.held(chip), self.held(chip), self.mine(chip))
+            self.pair(chip)
+
+    def place(self, side, chip, at):
+        return self.landed(chip if side == 0 else jnp.where(chip == at, self.links.chips, chip))
+
+    def onward(self, side, way, chip, before):
+        k, chips = self.links, self.links.chips
+        inner = before & (k.z > 0 if way > 0 else k.z < chips - 1)
+        arrival = self.recvs + (1 + side) * chips + chip
+
+        def add():
+            k.arrived(None, self.place(side, chip, k.z), arrival)
+            add_rows(self.held(chip), self.held(chip), self.place(side, chip, k.z))
+
+        pl.when(inner)(add)
+        return k.send(
+            before,
+            self.held(chip),
+            self.place(side, chip, k.z + way),
+            self.sends + chips + chip,
+            arrival,
+            k.beside(way),
+        )
 
     def step(self, i):
         k, chips = self.links, self.links.chips
         for side, way in enumerate((1, -1)):
             chip = k.z + way * (chips - 1 - i)
-            before = (chip >= 0) & (chip < chips)
-            inner = before & (k.z > 0 if way > 0 else k.z < chips - 1)
-            mine = self.recvs + (1 + side) * chips + chip
-
-            def add():
-                k.arrived(None, self.landed(side, chip), mine)
-                add_rows(self.held(chip), self.held(chip), self.landed(side, chip))
-
-            pl.when(inner)(add)
-            self.gone[side]()
-            self.gone[side] = k.send(
-                before,
-                self.held(chip),
-                self.landed(side, chip),
-                self.sends + chips + chip,
-                mine,
-                k.beside(way),
-                later=False,
-            )
+            self.onward(side, way, chip, (chip >= 0) & (chip < chips))
+
+    def toward(self, chip):
+        k = self.links
+        for side, way in enumerate((1, -1)):
+            self.onward(side, way, chip, chip > k.z if way > 0 else chip < k.z)
 
     def last(self):
         k, chips = self.links, self.links.chips
         for side, inner in enumerate((k.z > 0, k.z < chips - 1)):
 
             def add():
-                k.arrived(None, self.landed(side, k.z), self.recvs + (1 + side) * chips + k.z)
-                add_rows(self.held(k.z), self.held(k.z), self.landed(side, k.z))
+                block = self.place(side, k.z, k.z)
+                k.arrived(None, block, self.recvs + (1 + side) * chips + k.z)
+                add_rows(self.held(k.z), self.held(k.z), block)
 
             pl.when(inner)(add)
-        for gone in self.gone:
-            gone()
 
 
 class Exchange:
@@ -746,51 +750,70 @@
     k.finish()
 
 
+def far_first(k, t):
+    total = 0
+    for z in range(k.chips):
+        order = sorted(range(k.chips), key=lambda chip: -abs(chip - z))
+        total = total + jnp.where(k.z == z, order[t], 0)
+    return total
+
+
 def feed_forward_kernel(
-    groups, ranks, attended_all, x_all, grad_out, out_w, gate_up, down_w, gain,
-    grad_out_all, hidden, normed, mixed, grad_gate_up, down_parts, parts,
-    attended_in, x_in, grad_in, hidden_b, normed_b, mixed_b, grad_b, down_b, parts_b, local, sends, recvs,
+    groups, ranks, attended_all, x_all, out_all, gate_up_all, down_all, grad_out, gain,
+    grad_out_all, hidden, output, normed, mixed, grad_gate_up, parts,
+    out_w, gate_up, down_w, attended_in, x_in, grad_in, hidden_b, normed_b, gates, mixed_b, grad_b, down_b, parts_b,
+    held, landed, local, sends, recvs,
 ):
     k = Links(groups, ranks, sends, recvs)
-    chips, rows = k.chips, hidden_b.shape[0]
+    chips, pair = k.chips, hidden_b.shape[0]
+    rows = pair // 2
     width, units = out_w.shape[0], down_w.shape[0]
+    step = 512
     line = LineGather(k, lambda rank: grad_out_all.at[rank])
-    k.barrier()
-
-    def chip(t):
-        up = lax.rem(k.z + t, chips)
-        down = lax.rem(k.z + chips - t, chips)
-        return jnp.where(k.z < chips // 2, up, down)
+    scatter = LineScatter(
+        k, None, lambda chip: held.at[chip], lambda slot: landed.at[slot]
+    )
+    weights = [
+        pltpu.make_async_copy(ref, buffer, local.at[n])
+        for n, (ref, buffer) in enumerate(((out_all, out_w), (gate_up_all, gate_up), (down_all, down_w)))
+    ]
+    order = [far_first(k, t) for t in range(chips)]
 
     def span(t):
-        return pl.ds(pl.multiple_of(chip(t) * rows, rows), rows)
+        return pl.ds(pl.multiple_of(order[t] * pair, 16), pair)
 
     def loads(t):
         return [
-            pltpu.make_async_copy(ref.at[span(t)], buffer.at[t % 2], local.at[2 * n + t % 2])
+            pltpu.make_async_copy(ref.at[span(t)], buffer.at[t % 2], local.at[3 + 2 * n + t % 2])
             for n, (ref, buffer) in enumerate(((attended_all, attended_in), (x_all, x_in)))
         ]
 
-    results = ((hidden_b, hidden), (normed_b, normed), (mixed_b, mixed), (grad_b, grad_gate_up), (down_b, down_parts), (parts_b, parts))
-
-    def store(t, n):
-        buffer, ref = results[n]
-        return pltpu.make_async_copy(buffer, ref.at[span(t)], local.at[4 + n])
-
-    for load in loads(0):
+    def fetches(t):
+        return [
+            pltpu.make_async_copy(
+                grad_out_all.at[order[t] * 2 + c],
+                grad_in.at[t % 2, pl.ds(c * rows, rows)],
+                local.at[7 + 2 * (t % 2) + c],
+            )
+            for c in range(2)
+        ]
+
+    def store(n, buffer, ref, t):
+        return pltpu.make_async_copy(buffer, ref.at[span(t)], local.at[11 + n])
+
+    for load in loads(0) + weights:
         load.start()
+    k.barrier()
     line.start(grad_out)
     own = k.move(grad_out, grad_out_all.at[k.f])
-    own()
-    step = 512
+    weights[0].wait()
+    gone = None
     for t in range(chips):
         if t + 1 < chips:
             for load in loads(t + 1):
                 load.start()
         for load in loads(t):
             load.wait()
-        if t > 0:
-            store(t - 1, 0).wait()
 
         @pl.loop(0, width // step)
         def _(c):
@@ -799,32 +822,28 @@
                 attended_in[t % 2], out_w[:, part]
             )
 
-        store(t, 0).start()
         if t > 0:
-            store(t - 1, 1).wait()
-            line.step(t)
+            store(0, normed_b, normed, t - 1).wait()
 
         def normalise(part):
             total = hidden_b[part, :]
             normed_b[part, :] = (total * inverse_rms(total) * gain[...]).astype(BF16)
 
-        row_loop(rows, normalise)
-        store(t, 1).start()
-        line.over(chip(t))
-        place = chip(t) * 2
-        fetch = [
-            pltpu.make_async_copy(
-                grad_out_all.at[place + c], grad_in.at[pl.ds(c * (rows // 2), rows // 2)], local.at[10 + c]
-            )
-            for c in range(2)
-        ]
-        for copy in fetch:
-            copy.start()
-        for copy in fetch:
-            copy.wait()
+        row_loop(pair, normalise)
+        store(0, normed_b, normed, t).start()
+        if t == 0:
+            weights[1].wait()
+        if t == chips - 1:
+
+            @pl.loop(0, rows // 16)
+            def _(i):
+                source = pl.ds(pl.multiple_of(k.c * rows + i * 16, 16), 16)
+                hidden[pl.ds(pl.multiple_of(i * 16, 16), 16), :] = hidden_b[source, :]
+
         if t > 0:
-            store(t - 1, 2).wait()
-            store(t - 1, 3).wait()
+            store(1, mixed_b, mixed, t - 1).wait()
+            line.step(t)
+        here = span(t)
 
         @pl.loop(0, units // BLOCK)
         def _(u):
@@ -832,57 +851,102 @@
             far = pl.ds(pl.multiple_of(units + u * BLOCK, BLOCK), BLOCK)
             gate = dot(normed_b[...], gate_up[:, part])
             up = dot(normed_b[...], gate_up[:, far])
-            grad_mixed = cols_inner(grad_in[...], down_w[part, :])
-            sigmoid = 1.0 / (1.0 + jnp.exp(-gate))
-            silu = gate * sigmoid
-            mixed_b[:, part] = (silu * up).astype(BF16)
-            grad_b[:, part] = (
-                grad_mixed * up * (sigmoid * (1.0 + gate * (1.0 - sigmoid)))
-            ).astype(BF16)
-            grad_b[:, far] = (grad_mixed * silu).astype(BF16)
-
-        store(t, 2).start()
-        store(t, 3).start()
-        if t > 0:
-            store(t - 1, 4).wait()
-            store(t - 1, 5).wait()
+            gates[here, part] = gate
+            gates[here, far] = up
+            mixed_b[:, part] = (gate / (1.0 + jnp.exp(-gate)) * up).astype(BF16)
+
+        store(1, mixed_b, mixed, t).start()
+        if t == 0:
+            weights[2].wait()
+        else:
+            gone()
 
         @pl.loop(0, width // step)
         def _(c):
             part = pl.ds(pl.multiple_of(c * step, step), step)
             down_b[:, part] = dot(mixed_b[...], down_w[:, part]).astype(BF16)
+
+        def core_rows(core):
+            return down_b.at[pl.ds(pl.multiple_of(core * rows, 16), rows)]
+
+        gone = scatter.give(order[t], core_rows(1 - k.c), later=False)
+        scatter.pair(order[t], core_rows(k.c))
+        if t % 2 == 1:
+            scatter.step(t // 2)
+    store(0, normed_b, normed, chips - 1).wait()
+    store(1, mixed_b, mixed, chips - 1).wait()
+    gone()
+    own()
+    for chip in range(chips):
+        line.over(chip)
+    for fetch in fetches(0):
+        fetch.start()
+    for t in range(chips):
+        if t + 1 < chips:
+            for fetch in fetches(t + 1):
+                fetch.start()
+        for fetch in fetches(t):
+            fetch.wait()
+        if t > 0:
+            store(2, grad_b, grad_gate_up, t - 1).wait()
+        here = span(t)
+
+        @pl.loop(0, units // BLOCK)
+        def _(u):
+            part = pl.ds(pl.multiple_of(u * BLOCK, BLOCK), BLOCK)
+            far = pl.ds(pl.multiple_of(units + u * BLOCK, BLOCK), BLOCK)
+            gate, up = gates[here, part], gates[here, far]
+            grad_mixed = cols_inner(grad_in[t % 2], down_w[part, :])
+            sigmoid = 1.0 / (1.0 + jnp.exp(-gate))
+            grad_b[:, part] = (
+                grad_mixed * up * (sigmoid * (1.0 + gate * (1.0 - sigmoid)))
+            ).astype(BF16)
+            grad_b[:, far] = (grad_mixed * (gate * sigmoid)).astype(BF16)
+
+        store(2, grad_b, grad_gate_up, t).start()
+        if t > 0:
+            store(3, parts_b, parts, t - 1).wait()
+        if (chips + t) % 2 == 1 and (chips + t) // 2 < chips - 1:
+            scatter.step((chips + t) // 2)
+
+        @pl.loop(0, width // step)
+        def _(c):
+            part = pl.ds(pl.multiple_of(c * step, step), step)
             parts_b[:, part] = cols_inner(grad_b[...], gate_up[part, :]).astype(BF16)
 
-        store(t, 4).start()
-        store(t, 5).start()
-    for n in range(len(results)):
-        store(chips - 1, n).wait()
+        store(3, parts_b, parts, t).start()
+    scatter.last()
+
+    def out_rows(part):
+        output[part] = (hidden[part] + held[k.z, part].astype(F32)).astype(BF16)
+
+    row_loop(rows, out_rows)
+    store(2, grad_b, grad_gate_up, chips - 1).wait()
+    store(3, parts_b, parts, chips - 1).wait()
     k.finish()
 
 
 def middle_kernel(
-    groups, ranks, parts, down_parts, hidden_all, grad_out, gain, normed, grad_gate_up,
-    grad_all, grad_hidden, output, sums, gate_up_sum,
-    mine, held, landed, down_held, down_landed, rounded, hidden, tile, grad_w, gate_up_landed, local, sends, recvs,
+    groups, ranks, subs, parts, hidden, grad_out, gain, normed, grad_gate_up_all,
+    grad_all, grad_hidden, sums, gate_up_sum,
+    grad_gate_up, mine, held, landed, rounded, tile, grad_w, gate_up_landed, local, sends, recvs,
 ):
     k = Links(groups, ranks, sends, recvs)
-    rows = hidden.shape[0]
+    rows = hidden.shape[0] // subs
     depth = grad_w.shape[2]
-    scatter = LineScatter(
-        k,
-        lambda rank: parts.at[rank],
-        lambda chip: mine.at[chip],
-        lambda chip: held.at[chip],
-        lambda side, chip: landed.at[side, chip],
-    )
-    down_scatter = LineScatter(
-        k,
-        lambda rank: down_parts.at[rank],
-        lambda chip: mine.at[chip],
-        lambda chip: down_held.at[chip],
-        lambda side, chip: down_landed.at[side, chip],
-    )
-    gather = LineGather(k, lambda rank: grad_all.at[rank])
+    step = 512
+    scatters, gathers = [], []
+    for sub in range(subs):
+        piece = pl.ds(sub * rows, rows)
+        scatters.append(
+            LineScatter(
+                k,
+                lambda chip, piece=piece: mine.at[chip, piece],
+                lambda chip, piece=piece: held.at[chip, piece],
+                lambda slot, piece=piece: landed.at[slot, piece],
+            )
+        )
+        gathers.append(LineGather(k, lambda rank, piece=piece: grad_all.at[rank, piece]))
     gate_up_sums = [
         GroupScatter(
             k,
@@ -893,8 +957,8 @@
         for n in range(ranks)
     ]
     per_group = ranks * depth // BLOCK
+    per_tile = BLOCK // depth
     tiles = [(q, g) for q in range(per_group) for g in range(groups)]
-    per_tile = BLOCK // depth
 
     def load(i):
         q, g = tiles[i]
@@ -902,21 +966,14 @@
             normed.at[:, pl.ds((g * per_group + q) * BLOCK, BLOCK)], tile.at[i % 2], local.at[i % 2]
         )
 
-    own_hidden = pltpu.make_async_copy(
-        hidden_all.at[pl.ds(pl.multiple_of(k.f * rows, rows), rows)], hidden, local.at[2]
-    )
-    load(0).start()
-    own_hidden.start()
-    k.barrier()
-    scatter.start()
-
-    def weight_tile(i):
+    whole = pltpu.make_async_copy(grad_gate_up_all, grad_gate_up, local.at[2])
+
+    def work(i):
         q, g = tiles[i]
         if i + 1 < len(tiles):
             load(i + 1).start()
         load(i).wait()
         flipped = tile[i % 2].astype(F32).T.astype(BF16)
-        step = 512
 
         @pl.loop(0, grad_gate_up.shape[1] // step)
         def _(c):
@@ -929,18 +986,12 @@
             for n in range(per_tile):
                 gate_up_sums[q * per_tile + n].start(0)
 
-    weight_tile(0)
-    scatter.pair()
-    scatter.step(0)
-    spots = spaced(list(range(1, len(tiles))), k.chips - 1)
-    for i in range(k.chips - 1):
-        for place in spots[i]:
-            weight_tile(place)
-        if i > 0:
-            scatter.step(i)
-    scatter.last()
+    load(0).start()
+    whole.start()
+    k.barrier()
+    for sub, scatter in enumerate(scatters):
+        scatter.start(lambda rank, sub=sub: parts.at[rank, pl.ds(sub * rows, rows)])
     sums[...] = jnp.zeros_like(sums)
-    own_hidden.wait()
 
     def rows_of(part):
         total = hidden[part]
@@ -952,24 +1003,37 @@
         grad_hidden[part] = grad_total
         rounded[part] = grad_total.astype(BF16)
 
-    row_loop(rows, rows_of)
-    gather.start(rounded)
-    down_scatter.start()
-    own = k.move(rounded, grad_all.at[k.f])
-    down_scatter.pair()
-    for i in range(k.chips - 1):
-        down_scatter.step(i)
-        gather.step(i + 1)
-        if i == 0:
-            for sums_of in gate_up_sums:
+    own = []
+    hops = k.chips - 1
+    early = len(tiles) // 4
+    plan = spaced(list(range(early, len(tiles))), hops - 1) + [[]] * (subs * hops + 1)
+    whole.wait()
+    for place in range(early):
+        work(place)
+    for turn in range(subs + 1):
+        if turn < subs:
+            scatters[turn].pairs()
+        for i in range(hops):
+            if turn < subs:
+                scatters[turn].step(i)
+            if turn > 0:
+                gathers[turn - 1].step(i + 1)
+            for place in plan[turn * hops + i]:
+                work(place)
+            if turn == 1 and i == 0:
+                for sums_of in gate_up_sums[: ranks // 2]:
+                    sums_of.wait(0)
+                    sums_of.start(1)
+        if turn < subs:
+            scatters[turn].last()
+            row_loop(rows, rows_of, first=turn * rows)
+            piece = pl.ds(turn * rows, rows)
+            gathers[turn].start(rounded.at[piece])
+            own.append(k.move(rounded.at[piece], grad_all.at[k.f, piece]))
+        if turn == 1:
+            for sums_of in gate_up_sums[ranks // 2 :]:
                 sums_of.wait(0)
                 sums_of.start(1)
-    down_scatter.last()
-
-    def out_rows(part):
-        output[part] = (hidden[part] + down_held[k.z, part].astype(F32)).astype(BF16)
-
-    row_loop(rows, out_rows)
     for stage in range(1, k.bits):
         for n, sums_of in enumerate(gate_up_sums):
             if stage + 1 < k.bits:
@@ -977,127 +1041,171 @@
                 sums_of.start(stage + 1)
             else:
                 sums_of.wait(stage, gate_up_sum.at[n])
-    gather.finish()
-    own()
+    for gather in gathers:
+        gather.finish()
+    for wait in own:
+        wait()
     k.finish()
 
 
 def attend_back_kernel(
-    groups, ranks, rank_heads, lengths, out_all, grad_hidden, queries, keys, values, attended, log_totals,
-    cosine, sine, qkv, normed, gate_up_sum, grad_down,
-    parts, grad_qkv_w, grad_out_w, gate_up_grad, down_grad,
-    out_w, grad_qkv, keys_t, grad_keys, grad_values, down_landed, sends, recvs,
+    groups, ranks, rank_heads, slice_width,
+    lengths, out_all, normed, grad_rows, queries, keys, values, attended, log_totals,
+    cosine, sine, qkv, gate_up_sum, grad_down, tokens, grad_hidden, gain_rows, sums_two,
+    gate_up_grad, down_grad, qkv_grad, out_grad, grad_tokens, gain_grads,
+    out_w, grad_qkv, keys_t, grad_keys, grad_values, down_landed, held, landed, parts_b, tile,
+    grad_qkv_w, qkv_landed, grad_out_w, out_landed, sums, tiles, tiles_landed, tiles_sum, group_tiles,
+    local, sends, recvs,
 ):
     k = Links(groups, ranks, sends, recvs)
-    pieces = down_landed.shape[0]
-    down_rows = down_grad.shape[0] // pieces
-    down_sums = [
+    length = lengths[0]
+    cols, width = queries.shape[1], grad_rows.shape[1]
+    rows = tokens.shape[0]
+    pair = 2 * rows
+    blocks = keys_t.shape[0]
+    depth = qkv_grad.shape[1]
+    step = 512
+
+    def group_sums(ref, landing, count):
+        size = ref.shape[1] // count
+        return [
+            GroupScatter(
+                k,
+                lambda group, n=n: ref.at[group, pl.ds(n * size, size)],
+                lambda i, n=n: landing.at[n, i],
+                n % 2 == 1,
+            )
+            for n in range(count)
+        ], size
+
+    down_sums, down_size = group_sums(grad_down, down_landed, down_landed.shape[0])
+    out_sums, out_size = group_sums(grad_out_w, out_landed, out_landed.shape[0])
+    qkv_sums = [
         GroupScatter(
             k,
-            lambda group, n=n: grad_down.at[group, pl.ds(n * down_rows, down_rows)],
-            lambda i, n=n: down_landed.at[n, i],
+            lambda group, n=n: grad_qkv_w.at[group, n],
+            lambda i, n=n: qkv_landed.at[n, i],
             n % 2 == 1,
         )
-        for n in range(pieces)
+        for n in range(ranks)
     ]
-    exchange = Exchange(k)
+    scatter = LineScatter(
+        k, None, lambda chip: held.at[chip], lambda slot: landed.at[slot]
+    )
+    gate_up_ex, exchange, tile_exchange = Exchange(k), Exchange(k), Exchange(k)
+    tile_sends, tile_recvs = k.take(groups, groups)
     gate_up_in = lambda rank: gate_up_grad.at[rank]
-    length = lengths[0]
-    cols = queries.shape[1]
+    qkv_in = lambda rank: qkv_grad.at[rank]
+
+    def onward(several, stage):
+        for sums_of in several:
+            sums_of.wait(stage)
+            sums_of.start(stage + 1)
+
+    per_group = ranks * depth // BLOCK
+    per_tile = BLOCK // depth
+    work = [(q, g) for q in range(per_group) for g in range(groups)]
+
+    def load(i):
+        q, g = work[i]
+        return pltpu.make_async_copy(
+            normed.at[:, pl.ds((g * per_group + q) * BLOCK, BLOCK)], tile.at[i % 2], local.at[i % 2]
+        )
+
+    def weight_tile(i):
+        q, g = work[i]
+        if i + 1 < len(work):
+            load(i + 1).start()
+        load(i).wait()
+        flipped = tile[i % 2].astype(F32).T.astype(BF16)
+        for c in range(3):
+            part = slice(c * cols, (c + 1) * cols)
+            total = dot(flipped, grad_qkv[:, part]).astype(BF16)
+            for n in range(per_tile):
+                grad_qkv_w[g, q * per_tile + n, :, part] = total[n * depth : (n + 1) * depth]
+        if g == groups - 1:
+            for n in range(per_tile):
+                qkv_sums[q * per_tile + n].start(0)
+
+    before = []
+
+    def parts_of(t):
+        chip = far_first(k, t)
+        here = pl.ds(pl.multiple_of(chip * pair, 16), pair)
+        if t > 1:
+            before[t - 2]()
+            before[t - 2] = lambda: None
+
+        @pl.loop(0, width // step)
+        def _(c):
+            part = pl.ds(pl.multiple_of(c * step, step), step)
+            parts_b[t % 2, :, part] = cols_inner(grad_qkv[here, :], qkv[part, :]).astype(BF16)
+
+        def core_rows(core):
+            return parts_b.at[t % 2, pl.ds(pl.multiple_of(core * rows, 16), rows)]
+
+        before.append(scatter.give(chip, core_rows(1 - k.c), later=False))
+        return chip, core_rows(k.c)
+
+    def onto(t, chip, mine):
+        scatter.pair(chip, mine)
+        if t + 1 < k.chips:
+            scatter.toward(chip)
+
+    load(0).start()
     fetch = k.move(out_all.at[pl.ds(pl.multiple_of(k.f * cols, cols), cols)], out_w)
     k.barrier()
-    exchange.start(lambda rank: gate_up_sum.at[rank], gate_up_in)
     for sums_of in down_sums:
         sums_of.start(0)
-    blocks = keys_t.shape[0]
+    gate_up_ex.start(lambda rank: gate_up_sum.at[rank], gate_up_in)
     grad_keys[...] = jnp.zeros_like(grad_keys)
     grad_values[...] = jnp.zeros_like(grad_values)
-
-    fetch()
 
     @pl.loop(0, blocks)
     def _(i):
         block = pl.ds(pl.multiple_of(i * BLOCK, BLOCK), BLOCK)
         keys_t[i] = keys[block, :].astype(F32).T.astype(BF16)
 
-    @pl.loop(0, blocks)
-    def _(i):
+    fetch()
+
+    def back_rows(i):
         attend_back_rows(
-            i, rank_heads, grad_hidden, out_w, queries, keys, keys_t, values, attended, length, log_totals,
+            i, rank_heads, grad_rows, out_w, queries, keys, keys_t, values, attended, length, log_totals,
             cosine, sine, grad_keys, grad_values, grad_qkv,
         )
 
+    pl.loop(0, blocks - 1)(back_rows)
     for stage in range(k.bits - 1):
-        for sums_of in down_sums:
-            sums_of.wait(stage)
-            sums_of.start(stage + 1)
-
-    @pl.loop(0, blocks)
-    def _(i):
-        finish_back_rows(i, qkv, cosine, sine, grad_keys, grad_values, grad_qkv, parts)
-
-    @pl.loop(0, normed.shape[1] // BLOCK)
+        onward(down_sums, stage)
+    back_rows(blocks - 1)
+    pl.loop(0, blocks)(
+        lambda i: finish_back_rows(i, cosine, sine, grad_keys, grad_values, grad_qkv)
+    )
+    shares = spaced(list(range(len(work))), k.chips)
+    for t in range(k.chips):
+        chip, mine = parts_of(t)
+        for i in shares[t]:
+            weight_tile(i)
+        onto(t, chip, mine)
+
+    out_rows = grad_out_w.shape[1]
+    split = groups * out_rows // cols
+    out_base = lax.rem(k.f, split) * (cols // out_rows)
+    if split > 1:
+        grad_out_w[...] = jnp.zeros_like(grad_out_w)
+
+    @pl.loop(0, width // BLOCK)
     def _(t):
         part = pl.ds(pl.multiple_of(t * BLOCK, BLOCK), BLOCK)
-        grad_qkv_w[part, :] = rows_inner(normed[:, part], grad_qkv[...]).astype(BF16)
-        grad_out_w[:, part] = rows_inner(attended[...], grad_hidden[:, part]).astype(BF16)
-
-    for n, sums_of in enumerate(down_sums):
-        sums_of.wait(k.bits - 1, down_grad.at[pl.ds(n * down_rows, down_rows)])
-    exchange.finish(gate_up_in)
-    k.finish()
-
-
-def last_kernel(
-    groups, ranks, slice_width, parts, tokens, grad_hidden, gain, sums_two, grad_qkv, grad_out_w,
-    grad_tokens, qkv_grad, out_grad, gain_grads,
-    mine, held, landed, sums, qkv_landed, out_landed, tiles, tiles_landed, tiles_sum, group_tiles, sends, recvs,
-):
-    k = Links(groups, ranks, sends, recvs)
-    rows = tokens.shape[0]
-    scatter = LineScatter(
-        k, lambda rank: parts.at[rank], lambda chip: mine.at[chip], lambda chip: held.at[chip], lambda side, chip: landed.at[side, chip]
-    )
-    qkv_sums = [
-        GroupScatter(
-            k,
-            lambda group, n=n: grad_qkv.at[group, n],
-            lambda i, n=n: qkv_landed.at[n, i],
-            n % 2 == 1,
-        )
-        for n in range(ranks)
-    ]
-    pieces = out_landed.shape[0]
-    piece_rows = out_grad.shape[0] // pieces
-    out_sums = [
-        GroupScatter(
-            k,
-            lambda group, n=n: grad_out_w.at[group, pl.ds(n * piece_rows, piece_rows)],
-            lambda i, n=n: out_landed.at[n, i],
-            n % 2 == 1,
-        )
-        for n in range(pieces)
-    ]
-    exchange, tile_exchange = Exchange(k), Exchange(k)
-    tile_sends, tile_recvs = k.take(groups, groups)
-    qkv_in = lambda rank: qkv_grad.at[rank]
-    k.barrier()
-    scatter.start()
-    for sums_of in qkv_sums:
-        sums_of.start(0)
+        total = rows_inner(attended[...], grad_rows[:, part]).astype(BF16)
+        for n in range(cols // out_rows):
+            grad_out_w[out_base + n, :, part] = total[n * out_rows : (n + 1) * out_rows]
+
     for sums_of in out_sums:
         sums_of.start(0)
-    scatter.pair()
-    for i in range(k.chips - 1):
-        scatter.step(i)
-        if i == 0:
-            for sums_of in qkv_sums:
-                sums_of.wait(0)
-                sums_of.start(1)
-    for stage in range(1, k.bits - 1):
-        for sums_of in qkv_sums:
-            sums_of.wait(stage)
-            sums_of.start(stage + 1)
+    for stage in range(k.bits - 1):
+        onward(qkv_sums, stage)
+        onward(out_sums, stage)
     for n, sums_of in enumerate(qkv_sums):
         exchange.start_piece(n, sums_of.wait(k.bits - 1), qkv_in)
     scatter.last()
@@ -1110,7 +1218,7 @@
         grad = held[k.z, part].astype(F32)
         sums[...] += jnp.sum(grad * scaled, 0, keepdims=True)
         grad_tokens[part] = (
-            grad_hidden[part] + norm_back(grad * gain[...], scaled, scale)
+            grad_hidden[part] + norm_back(grad * gain_rows[0:1, :], scaled, scale)
         ).astype(BF16)
 
     row_loop(rows, rows_of)
@@ -1122,12 +1230,10 @@
             tiles[rank, group, 1:2] = sums_two[:, at : at + 128]
     tile_in = lambda rank: tiles_landed.at[rank]
     tile_exchange.start(lambda rank: tiles.at[rank], tile_in)
-    for stage in range(k.bits - 1):
-        for sums_of in out_sums:
-            sums_of.wait(stage)
-            sums_of.start(stage + 1)
     for n, sums_of in enumerate(out_sums):
-        sums_of.wait(k.bits - 1, out_grad.at[pl.ds(n * piece_rows, piece_rows)])
+        sums_of.wait(k.bits - 1, out_grad.at[pl.ds(n * out_size, out_size)])
+    for n, sums_of in enumerate(down_sums):
+        sums_of.wait(k.bits - 1, down_grad.at[pl.ds(n * down_size, down_size)])
     tile_exchange.finish(tile_in)
     total = tiles_landed[0]
     for rank in range(1, ranks):
@@ -1151,8 +1257,41 @@
     for group in range(1, groups):
         total = total + group_tiles[group]
     gain_grads[...] = total
+    for wait in before:
+        wait()
+    gate_up_ex.finish(gate_up_in)
     exchange.finish(qkv_in, own=False)
     k.finish()
+
+
+def head_places(ranks, rank_heads, split):
+    places = {}
+    for rank in range(ranks):
+        for b in range(rank_heads):
+            head = (rank % split * rank_heads + b) * (ranks // split) + rank // split
+            places[head] = (rank, b)
+    return [places[head] for head in range(HEADS)]
+
+
+def finish_kernel(
+    groups, places, gate_up_grad, qkv_grad, grad_w_gate, grad_w_up, grad_w_query, grad_w_key, grad_w_value
+):
+    ranks, cols, units = qkv_grad.shape[0], qkv_grad.shape[2] // 3, gate_up_grad.shape[2] // 2
+    part = units // groups
+    for rank in range(ranks):
+        for group in range(groups):
+            at = (group * ranks + rank) * part
+            for n, out in enumerate((grad_w_gate, grad_w_up)):
+                start = n * units + group * part
+                out[:, at : at + part] = gate_up_grad[rank, :, start : start + part].astype(F32)
+    for n, out in enumerate((grad_w_query, grad_w_key, grad_w_value)):
+        for head in range(0, HEADS, 2):
+            halves = []
+            for rank, b in places[head : head + 2]:
+                start = n * cols + b * HEAD_DIM
+                halves.append(qkv_grad[rank, :, start : start + HEAD_DIM].astype(F32))
+            at = head * HEAD_DIM
+            out[:, at : at + 2 * HEAD_DIM] = jnp.concatenate(halves, 1)
 
 
 VMEM = pl.BlockSpec(memory_space=pltpu.VMEM)
@@ -1170,7 +1309,7 @@
         + [pltpu.SemaphoreType.DMA((local,))] * (local > 0)
         + [pltpu.SemaphoreType.DMA((semaphores,))] * 2,
         compiler_params=pltpu.CompilerParams(
-            collective_id=identity, has_side_effects=True, vmem_limit_bytes=60 * 1024 * 1024
+            collective_id=identity, has_side_effects=True, vmem_limit_bytes=61 * 1024 * 1024
         ),
     )(*args)
 
@@ -1205,14 +1344,6 @@
             return shaped.transpose(1, 2, 0, 3).reshape(depth, groups * ranks * hidden_part)
 
         span = [[base * split + i for i in range(split)] for base in range(ranks // split)]
-
-        def place_output(grad):
-            if split > 1:
-                place = lax.rem(rank, split)
-                grad = jnp.where(
-                    (jnp.arange(split) == place)[:, None, None], grad[None], jnp.zeros((), BF16)
-                )
-            return grad.reshape(groups, -1, width)
 
         head_cols = rank_heads * HEAD_DIM
         unit_cols = groups * hidden_part
@@ -1263,79 +1394,81 @@
         own_places = rank * rows + jnp.arange(rows, dtype=jnp.int32)
         grad_out = jnp.where(own_places[:, None] < lengths[0], cotangent, jnp.zeros((), BF16))
         pair = 2 * rows
-        grad_out_all, hidden, normed_two, mixed, grad_gate_up, down_parts, parts = call(
+        line_scratch = [
+            ((chips, rows, width), BF16),
+            ((chips, rows, width), BF16),
+            ((chips + 1, rows, width), BF16),
+        ]
+        grad_out_all, hidden, output, normed_two, mixed, grad_gate_up, parts = call(
             functools.partial(feed_forward_kernel, groups, ranks),
             2,
-            [ANY] * 2 + [VMEM] * 5,
+            [ANY] * 5 + [VMEM] * 2,
             [
                 ((ranks, rows, width), BF16, ANY),
-                ((count, width), F32, ANY),
+                ((rows, width), F32, VMEM),
+                ((rows, width), BF16, VMEM),
                 ((count, width), BF16, ANY),
                 ((count, unit_cols), BF16, ANY),
                 ((count, 2 * unit_cols), BF16, ANY),
                 ((count, width), BF16, ANY),
-                ((count, width), BF16, ANY),
             ],
             [
+                ((width, width), BF16),
+                ((width, 2 * unit_cols), BF16),
+                ((unit_cols, width), BF16),
                 ((2, pair, width), BF16),
                 ((2, pair, width), BF16),
-                ((pair, width), BF16),
+                ((2, pair, width), BF16),
                 ((pair, width), F32),
                 ((pair, width), BF16),
+                ((count, 2 * unit_cols), F32),
                 ((pair, unit_cols), BF16),
                 ((pair, 2 * unit_cols), BF16),
                 ((pair, width), BF16),
                 ((pair, width), BF16),
-            ],
-            64,
-            (attended_all, x_all, grad_out, out_all, gate_up, down_w, gain_two),
-            local=12,
+            ]
+            + line_scratch[1:],
+            128,
+            (attended_all, x_all, out_all, gate_up, down_w, grad_out, gain_two),
+            local=15,
         )
         grad_down = rows_inner(mixed, grad_out_all.reshape(count, width)).astype(BF16)
-        line_scratch = [((chips, rows, width), BF16), ((2, chips, rows, width), BF16)]
-        grad_hidden_all, grad_hidden, output, sums_two, gate_up_sum = call(
-            functools.partial(middle_kernel, groups, ranks),
+        grad_hidden_all, grad_hidden, sums_two, gate_up_sum = call(
+            functools.partial(middle_kernel, groups, ranks, 2),
             3,
-            [ANY] * 3 + [VMEM] * 2 + [ANY, VMEM],
+            [ANY] + [VMEM] * 3 + [ANY] * 2,
             [
                 ((ranks, rows, width), BF16, ANY),
                 ((rows, width), F32, VMEM),
-                ((rows, width), BF16, VMEM),
                 ((1, width), F32, VMEM),
                 ((ranks, depth, 2 * unit_cols), BF16, VMEM),
             ],
-            [((chips, rows, width), BF16)]
-            + line_scratch * 2
+            [((count, 2 * unit_cols), BF16)]
+            + line_scratch
             + [
                 ((rows, width), BF16),
-                ((rows, width), F32),
                 ((2, count, BLOCK), BF16),
                 ((groups, ranks, depth, 2 * unit_cols), BF16),
                 ((ranks, groups - 1, depth, 2 * unit_cols), BF16),
             ],
             160,
-            (
-                parts.reshape(ranks, rows, width),
-                down_parts.reshape(ranks, rows, width),
-                hidden,
-                grad_out,
-                gain_two,
-                normed_two,
-                grad_gate_up,
-            ),
+            (parts.reshape(ranks, rows, width), hidden, grad_out, gain_two, normed_two, grad_gate_up),
             local=3,
         )
-        pieces = 4
-        parts, grad_qkv_w, grad_out_w, grad_gate_up_w, grad_w_down = call(
-            functools.partial(attend_back_kernel, groups, ranks, rank_heads),
+        down_pieces, out_pieces = 4, 2
+        out_place = out_rows * split
+        tile = (8, 128)
+        grad_gate_up_w, grad_w_down, grad_qkv_w, grad_w_output, grad_tokens, sums = call(
+            functools.partial(attend_back_kernel, groups, ranks, rank_heads, slice_width),
             6,
-            [SMEM, ANY] + [VMEM] * 12,
+            [SMEM, ANY, ANY] + [VMEM] * 15,
             [
-                ((count, width), BF16, VMEM),
-                ((width, 3 * head_cols), BF16, VMEM),
-                ((head_cols, width), BF16, VMEM),
                 ((ranks, depth, 2 * unit_cols), BF16, ANY),
                 ((hidden_part, width), F32, VMEM),
+                ((ranks, depth, 3 * head_cols), BF16, ANY),
+                ((out_place, width), F32, VMEM),
+                ((rows, width), BF16, VMEM),
+                (tile, F32, VMEM),
             ],
             [
                 ((head_cols, width), BF16),
@@ -1343,12 +1476,27 @@
                 ((blocks, head_cols, BLOCK), BF16),
                 ((count, head_cols), F32),
                 ((count, head_cols), F32),
-                ((pieces, groups - 1, hidden_part // pieces, width), BF16),
+                ((down_pieces, groups - 1, hidden_part // down_pieces, width), BF16),
+            ]
+            + line_scratch[1:]
+            + [
+                ((2, pair, width), BF16),
+                ((2, count, BLOCK), BF16),
+                ((groups, ranks, depth, 3 * head_cols), BF16),
+                ((ranks, groups - 1, depth, 3 * head_cols), BF16),
+                ((groups, out_place, width), BF16),
+                ((out_pieces, groups - 1, out_place // out_pieces, width), BF16),
+                ((1, width), F32),
+                ((ranks, groups) + tile, F32),
+                ((ranks, groups) + tile, F32),
+                ((groups,) + tile, F32),
+                ((groups,) + tile, F32),
             ],
-            160,
+            192,
             (
                 lengths,
                 out_all,
+                normed_one,
                 grad_hidden_all.reshape(count, width),
                 queries,
                 keys,
@@ -1358,57 +1506,37 @@
                 cosine,
                 sine,
                 qkv,
-                normed_one,
                 gate_up_sum,
                 grad_down.reshape(groups, hidden_part, width),
-            ),
-        )
-        grad_out_w = place_output(grad_out_w)
-        grad_w_gate = units_in(grad_gate_up_w[..., :unit_cols]).astype(F32)
-        grad_w_up = units_in(grad_gate_up_w[..., unit_cols:]).astype(F32)
-        parts = parts.reshape(ranks, rows, width)
-        pieces = 2
-        out_rows = grad_out_w.shape[1]
-        tile = (8, 128)
-        grad_tokens, grad_qkv_w, grad_w_output, sums = call(
-            functools.partial(last_kernel, groups, ranks, slice_width),
-            4,
-            [ANY] + [VMEM] * 6,
-            [
-                ((rows, width), BF16, VMEM),
-                ((ranks, depth, 3 * head_cols), BF16, ANY),
-                ((out_rows, width), F32, VMEM),
-                (tile, F32, VMEM),
-            ],
-            [((chips, rows, width), BF16)]
-            + line_scratch
-            + [
-                ((1, width), F32),
-                ((ranks, groups - 1, depth, 3 * head_cols), BF16),
-                ((pieces, groups - 1, out_rows // pieces, width), BF16),
-                ((ranks, groups) + tile, F32),
-                ((ranks, groups) + tile, F32),
-                ((groups,) + tile, F32),
-                ((groups,) + tile, F32),
-            ],
-            160,
-            (
-                parts,
                 tokens,
                 grad_hidden,
-                gain_one,
+                gain_rows,
                 sums_two,
-                grad_qkv_w.reshape(groups, ranks, depth, 3 * head_cols),
-                grad_out_w,
             ),
+            local=2,
         )
         if split > 1:
             grad_w_output = lax.psum_scatter(
                 grad_w_output, "fsdp", scatter_dimension=0, tiled=True, axis_index_groups=span
             )
-        grad_w_query, grad_w_key, grad_w_value = (
-            heads_in(grad_qkv_w[..., i * head_cols : (i + 1) * head_cols]).astype(F32) for i in range(3)
-        )
+        if hidden_part % 128 == 0:
+            wide, narrow = (
+                jax.ShapeDtypeStruct((depth, size), F32) for size in (w_gate.shape[1], width)
+            )
+            grad_w_gate, grad_w_up, grad_w_query, grad_w_key, grad_w_value = pl.pallas_call(
+                functools.partial(finish_kernel, groups, head_places(ranks, rank_heads, split)),
+                out_shape=[wide, wide, narrow, narrow, narrow],
+                in_specs=[VMEM] * 2,
+                out_specs=[VMEM] * 5,
+                compiler_params=pltpu.CompilerParams(vmem_limit_bytes=32 * 1024 * 1024),
+            )(grad_gate_up_w, grad_qkv_w)
+        else:
+            grad_w_gate = units_in(grad_gate_up_w[..., :unit_cols]).astype(F32)
+            grad_w_up = units_in(grad_gate_up_w[..., unit_cols:]).astype(F32)
+            grad_w_query, grad_w_key, grad_w_value = (
+                heads_in(grad_qkv_w[..., i * head_cols : (i + 1) * head_cols]).astype(F32)
+                for i in range(3)
+            )
         place = (lax.axis_index("dp") * ranks + rank) * slice_width % 128
         sums = lax.dynamic_slice_in_dim(sums, place, slice_width, 1)
         return (

time: 625 us -> 570 us (0.912)
  Pallas kernels: 559 us -> 527 us
  local copies, waits for them, and re-layouts: 36.6 us -> 17.5 us
    pallas_call x5 -> x4, Pallas kernels: 559 us -> 524 us  [call(): pl.pallas_call(kernel, out_shape=[jax.ShapeDtypeStruct(shape, kind) for s...]
    convert_element_type x13 -> x0, local copies, waits for them, and re-layouts: 17.6 us -> none  [the longest x9 6.64 us: body(): heads_in(grad_qkv_w[..., i * head_cols:(i + 1) * head_cols]).astype(F32)]
where the time goes in v4:
time: 570 us; the launch traced here: 561 us
  Pallas kernels  527 us (92%)
  local copies, waits for them, and re-layouts  17.5 us (3%)
  matrix products  9.82 us (2%)
    pallas_call x4, Pallas kernels, call(): pl.pallas_call(kernel, out_shape=[jax.ShapeDtypeStruct(shape, kind) for s...  524 us

profile of v4, /device:TPU:0, one launch (start us, length us, event | category | flops | bytes accessed | tf_op | source)
XLA Modules:
  0.0 560.6 jit_solution(3090040261018291589)
XLA Ops:
  0.6 0.0 copy-start.9
  1.4 0.7 pad_maximum_fusion.2
  2.1 0.3 dynamic_update_slice.3.gains
  2.4 0.0 copy-start.10
  2.4 1.5 reshape.82
  3.8 0.2 copy.41
  4.1 0.3 reshape.83
  4.4 1.5 reshape.84
  5.9 0.0 copy-start.5
  5.9 0.2 copy.40
  6.1 0.0 copy-start.3
  6.1 0.3 reshape.85
  6.5 0.0 copy-done.9
  6.5 0.5 reshape.86
  7.0 0.2 copy.39
  7.2 0.0 copy-done.10
  7.2 0.3 reshape.87
  7.6 0.9 pad_maximum_fusion.1.qkv_out
  8.5 0.0 copy-done.5
  8.5 1.0 broadcast_select_fusion.grad_out
  9.5 0.0 copy-done.3
  9.5 0.0 copy-start.4
  9.5 0.3 copy.30
  9.7 0.4 copy.38
  10.1 0.8 reshape.89
  10.9 0.0 copy-done.4
  10.9 0.3 copy.31
  11.2 0.4 copy.37
  11.6 0.8 reshape.91
  12.4 1.5 pad_maximum_fusion.gate_up_out
  13.9 204.3 %shard_map.221 = (bf16[1280,2048]{1,0:T(8,128)(2,1)}, bf16[4,8,64,768]{3,2,1,0:T(8,128)(2,1)}, f32[8,2048]{1,0:T(8,128)}, bf16[1280,2048]{1,0:T(8,128)(2,1)}, bf...) custom-call(s32[1]{0:T(128)} %copy.47.lengths, ...), custom_call_target="tpu_custom_call" | custom-call | tf_op jit(solution)/shard_map/pallas_call | solution.py:1303
  218.2 1.4 slice.9.gain
  219.7 98.2 %shard_map.222 = (bf16[8,160,2048]{2,1,0:T(8,128)(2,1)}, f32[160,2048]{1,0:T(8,128)}, bf16[160,2048]{1,0:T(8,128)(2,1)}, bf16[1280,2048]{1,0:T(8,128)(2,1)}, bf1...) custom-call(bf16[1280,2048]{1,0:T(8,128)(2,1)} %get-tuple-element.46.attended_all, ...), custom_call_target="tpu_custom_call" | custom-call | tf_op jit(solution)/shard_map/pallas_call | solution.py:1303
  317.9 0.0 copy-start.11
  317.9 95.9 %shard_map.223 = (bf16[8,160,2048]{2,1,0:T(8,128)(2,1)}, f32[160,2048]{1,0:T(8,128)}, f32[1,2048]{1,0:T(1,128)}, bf16[8,64,2048]{2,1,0:T(8,128)(2,1)}) custom-call(bf16[8,160,2048]{2,1,0:T(8,128)(2,1)} %bitcast.49, f32[160,2048]{1,0:T(8,128)} %get-tuple-element.55.hidden, bf16[160,2048]{1,0:T(8,128)(2,1)} %broadcast_select_fusion.grad_out, ...), custom_call_target="tpu_custom_call" | custom-call | tf_op jit(solution)/shard_map/pallas_call | solution.py:1303
  413.8 0.0 copy-done.11
  413.8 9.8 %convolution_convert_fusion = bf16[1024,2048]{1,0:T(8,128)(2,1)} fusion(bf16[1280,1024]{1,0:T(8,128)(2,1)S(1)} %copy-done.11, bf16[1280,2048]{1,0:T(8,128)(2,1)} %bitcast.62), kind=kOutput, calls=%fused_computation | convolution fusion | flops 5370806272 | bytes 12058624 | tf_op jit(solution)/shard_map/dot_general | solution.py:26
  423.6 0.0 copy-start.6
  423.6 125.9 %shard_map.224 = (bf16[8,64,2048]{2,1,0:T(8,128)(2,1)}, f32[256,2048]{1,0:T(8,128)}, bf16[8,64,768]{2,1,0:T(8,128)(2,1)}, f32[64,2048]{1,0:T(8,128)}, bf16[160,2048]{1,0:T(8,128)(2,1)}, /*index=5*/f32[8,128]{1,0:T(8,128)}) custom-call(s32[1]{0:T(128)} %copy.47.lengths, bf16[2048,2048]{1,0:T(8,128)(2,1)} %bitcast.46, ...), custom_call_target="tpu_custom_call" | custom-call | tf_op jit(solution)/shard_map/pallas_call | solution.py:1303
  549.6 0.8 constant_dynamic-slice_fusion
  550.3 0.5 slice_bitcast_fusion
  550.8 0.0 copy-start
  550.8 1.6 copy-done
  552.4 0.0 copy-start.1
  552.4 1.1 copy-done.1
  553.6 0.0 copy-start.7
  553.6 0.0 copy-start.8
  553.6 0.0 copy-start.2
  553.6 3.0 shard_map.225
  556.6 0.0 copy-done.6
  556.6 0.8 copy.48
  557.4 0.0 copy-done.7
  557.5 0.8 copy.49
  558.3 0.0 copy-done.8
  558.3 0.8 copy.50
  559.1 0.0 copy-done.2
  559.1 1.3 copy.51
  (2 shorter events, 0.0 us)
Async XLA Ops:
  0.6 5.8 %copy-start.9 = (bf16[64,2048]{1,0:T(8,128)(2,1)S(1)}, bf16[64,2048]{1,0:T(8,128)(2,1)}, u32[]{:S(2)}) copy-start(bf16[64,2048]{1,0:T(8,128)(2,1)} %param.20) | copy-start | bytes 786436
  2.4 4.8 copy-start.10
  5.9 2.6 copy-start.5
  6.1 3.4 copy-start.3
  9.5 1.5 copy-start.4
  317.9 95.9 %copy-start.11 = (bf16[1280,1024]{1,0:T(8,128)(2,1)S(1)}, bf16[1280,1024]{1,0:T(8,128)(2,1)}, u32[]{:S(2)}) copy-start(bf16[1280,1024]{1,0:T(8,128)(2,1)} %get-tuple-element.66) | copy-start | bytes 7864324
  423.6 133.0 %copy-start.6 = (bf16[160,2048]{1,0:T(8,128)(2,1)S(1)}, bf16[160,2048]{1,0:T(8,128)(2,1)}, u32[]{:S(2)}) copy-start(bf16[160,2048]{1,0:T(8,128)(2,1)} %get-tuple-element.94) | copy-start | bytes 1966084
  550.8 1.6 copy-start
  552.4 1.1 copy-start.1
  553.6 3.9 copy-start.7
  553.6 4.7 copy-start.8
  553.6 5.5 copy-start.2

commit v5 on v4

--- a/solution.py
+++ b/solution.py
@@ -566,14 +566,34 @@
     return [events[b * count // blocks : (b + 1) * count // blocks] for b in range(blocks)]
 
 
+def head_places(ranks, rank_heads, split):
+    places = {}
+    for rank in range(ranks):
+        for b in range(rank_heads):
+            head = (rank % split * rank_heads + b) * (ranks // split) + rank // split
+            places[head] = (rank, b)
+    return [places[head] for head in range(HEADS)]
+
+
 def attend_kernel(
-    groups, ranks, rank_heads, slice_width,
-    lengths, tokens, qkv_out, gains, out_w, down_w, gate_up_out, cosine, sine,
+    groups, ranks, rank_heads, slice_width, packed, traffic,
+    lengths, tokens, w_query, w_key, w_value, gains, out_w, down_w, w_gate, w_up, cosine, sine,
     x_all, qkv, gain_rows, normed, queries, keys, values, attended, log_totals,
     attended_all, gate_up, out_all, down_all,
-    gains_all, values_t, sends, recvs,
+    gains_all, values_t, qkv_out, gate_up_out, sends, recvs,
 ):
     k = Links(groups, ranks, sends, recvs)
+    places = head_places(ranks, rank_heads, max(1, HEAD_DIM // out_w.shape[0]))
+    for rank in range(ranks):
+        mine = [[h for h in range(HEADS) if places[h] == (rank, b)][0] for b in range(rank_heads)]
+        for n, ref in enumerate((w_query, w_key, w_value)):
+            for b in range(0, rank_heads, 2):
+                halves = [
+                    ref[:, head * HEAD_DIM : (head + 1) * HEAD_DIM].astype(F32)
+                    for head in mine[b : b + 2]
+                ]
+                at = (n * rank_heads + b) * HEAD_DIM
+                qkv_out[rank, :, at : at + 2 * HEAD_DIM] = jnp.concatenate(halves, 1).astype(BF16)
     length = lengths[0]
     cols, rows = queries.shape[1], tokens.shape[0]
     depth, half = gate_up_out.shape[1], ranks // 2
@@ -642,10 +662,12 @@
                 at = r * groups + group
                 k.send(None, block, block, over_sends + at, over_recvs + at, k.sibling)
 
+    units_from = w_gate if packed else gate_up_out
+
     def send_out(q):
         part = pl.ds(q * 16, 16)
         exchanges[q].start(
-            lambda rank: gate_up_out.at[rank, part], lambda rank: gate_up.at[k.d, rank, part]
+            lambda rank: units_from.at[rank, part], lambda rank: gate_up.at[k.d, rank, part]
         )
 
     def came_in(q):
@@ -663,6 +685,15 @@
     for h, gather in enumerate(downs):
         gather.start(0, down_w.at[pl.ds(h * down_half, down_half)])
     own_down = k.move(down_w, down_all.at[k.d])
+    if not packed:
+        units = gate_up_out.shape[2] // 2
+        share = units // groups
+        for rank in range(ranks):
+            for group in range(groups):
+                at = (group * ranks + rank) * share
+                for n, ref in enumerate((w_gate, w_up)):
+                    start = n * units + group * share
+                    gate_up_out[rank, :, start : start + share] = ref[:, at : at + share]
     gains_ex.finish(gains_in)
     qkv_ex.finish(qkv_in)
     out_line.start(out_w)
@@ -696,6 +727,7 @@
     for stage in range(1, k.bits):
         onward(downs, stage)
     x_line.finish()
+    traffic.put(0, 1)
     members = 128 // slice_width
     for at in range(groups * ranks // members):
         group, first = at * members // ranks, at * members % ranks
@@ -733,6 +765,7 @@
         for reach in range(1, k.chips):
             if 0 <= i - reach < blocks:
                 lines[i - reach].step(reach)
+    traffic.put()
     for stage in range(1, k.bits):
         if k.bits > 2:
             out_onward(stage)
@@ -759,7 +792,7 @@
 
 
 def feed_forward_kernel(
-    groups, ranks, attended_all, x_all, out_all, gate_up_all, down_all, grad_out, gain,
+    groups, ranks, traffic, attended_all, x_all, out_all, gate_up_all, down_all, grad_out, gain_rows,
     grad_out_all, hidden, output, normed, mixed, grad_gate_up, parts,
     out_w, gate_up, down_w, attended_in, x_in, grad_in, hidden_b, normed_b, gates, mixed_b, grad_b, down_b, parts_b,
     held, landed, local, sends, recvs,
@@ -791,7 +824,7 @@
     def fetches(t):
         return [
             pltpu.make_async_copy(
-                grad_out_all.at[order[t] * 2 + c],
+                grad_out_all.at[order[chips - 1 - t] * 2 + c],
                 grad_in.at[t % 2, pl.ds(c * rows, rows)],
                 local.at[7 + 2 * (t % 2) + c],
             )
@@ -807,7 +840,7 @@
     line.start(grad_out)
     own = k.move(grad_out, grad_out_all.at[k.f])
     weights[0].wait()
-    gone = None
+    gone = []
     for t in range(chips):
         if t + 1 < chips:
             for load in loads(t + 1):
@@ -827,7 +860,7 @@
 
         def normalise(part):
             total = hidden_b[part, :]
-            normed_b[part, :] = (total * inverse_rms(total) * gain[...]).astype(BF16)
+            normed_b[part, :] = (total * inverse_rms(total) * gain_rows[1:2, :]).astype(BF16)
 
         row_loop(pair, normalise)
         store(0, normed_b, normed, t).start()
@@ -842,7 +875,8 @@
 
         if t > 0:
             store(1, mixed_b, mixed, t - 1).wait()
-            line.step(t)
+        if t > 2:
+            line.step(t - 1)
         here = span(t)
 
         @pl.loop(0, units // BLOCK)
@@ -858,38 +892,45 @@
         store(1, mixed_b, mixed, t).start()
         if t == 0:
             weights[2].wait()
-        else:
-            gone()
+        elif t > 1:
+            gone[t - 2]()
 
         @pl.loop(0, width // step)
         def _(c):
             part = pl.ds(pl.multiple_of(c * step, step), step)
-            down_b[:, part] = dot(mixed_b[...], down_w[:, part]).astype(BF16)
-
-        def core_rows(core):
-            return down_b.at[pl.ds(pl.multiple_of(core * rows, 16), rows)]
-
-        gone = scatter.give(order[t], core_rows(1 - k.c), later=False)
-        scatter.pair(order[t], core_rows(k.c))
+            down_b[t % 2, :, part] = dot(mixed_b[...], down_w[:, part]).astype(BF16)
+
+        def core_rows(t, core):
+            return down_b.at[t % 2, pl.ds(pl.multiple_of(core * rows, 16), rows)]
+
+        gone.append(scatter.give(order[t], core_rows(t, 1 - k.c), later=False))
+        if t > 0:
+            scatter.pair(order[t - 1], core_rows(t - 1, k.c))
+        if t == 1:
+            line.step(1)
         if t % 2 == 1:
             scatter.step(t // 2)
     store(0, normed_b, normed, chips - 1).wait()
     store(1, mixed_b, mixed, chips - 1).wait()
-    gone()
+    for wait in gone[-2:]:
+        wait()
     own()
-    for chip in range(chips):
-        line.over(chip)
+    line.over(order[chips - 1])
     for fetch in fetches(0):
         fetch.start()
     for t in range(chips):
+        if t == 1:
+            line.step(chips - 1)
         if t + 1 < chips:
+            line.over(order[chips - 2 - t])
             for fetch in fetches(t + 1):
                 fetch.start()
         for fetch in fetches(t):
             fetch.wait()
+        near = chips - 1 - t
         if t > 0:
-            store(2, grad_b, grad_gate_up, t - 1).wait()
-        here = span(t)
+            store(2, grad_b, grad_gate_up, near + 1).wait()
+        here = span(near)
 
         @pl.loop(0, units // BLOCK)
         def _(u):
@@ -903,9 +944,11 @@
             ).astype(BF16)
             grad_b[:, far] = (grad_mixed * (gate * sigmoid)).astype(BF16)
 
-        store(2, grad_b, grad_gate_up, t).start()
+        store(2, grad_b, grad_gate_up, near).start()
         if t > 0:
-            store(3, parts_b, parts, t - 1).wait()
+            store(3, parts_b, parts, near + 1).wait()
+        if t == 0:
+            scatter.pair(order[chips - 1], down_b.at[(chips - 1) % 2, pl.ds(pl.multiple_of(k.c * rows, 16), rows)])
         if (chips + t) % 2 == 1 and (chips + t) // 2 < chips - 1:
             scatter.step((chips + t) // 2)
 
@@ -914,22 +957,22 @@
             part = pl.ds(pl.multiple_of(c * step, step), step)
             parts_b[:, part] = cols_inner(grad_b[...], gate_up[part, :]).astype(BF16)
 
-        store(3, parts_b, parts, t).start()
+        store(3, parts_b, parts, near).start()
     scatter.last()
 
     def out_rows(part):
         output[part] = (hidden[part] + held[k.z, part].astype(F32)).astype(BF16)
 
     row_loop(rows, out_rows)
-    store(2, grad_b, grad_gate_up, chips - 1).wait()
-    store(3, parts_b, parts, chips - 1).wait()
+    store(2, grad_b, grad_gate_up, 0).wait()
+    store(3, parts_b, parts, 0).wait()
     k.finish()
 
 
 def middle_kernel(
-    groups, ranks, subs, parts, hidden, grad_out, gain, normed, grad_gate_up_all,
-    grad_all, grad_hidden, sums, gate_up_sum,
-    grad_gate_up, mine, held, landed, rounded, tile, grad_w, gate_up_landed, local, sends, recvs,
+    groups, ranks, subs, traffic, parts, hidden, grad_out, gain_rows, normed, grad_gate_up, mixed, grad_out_all,
+    grad_all, grad_hidden, sums, gate_up_sum, grad_down,
+    mine, held, landed, rounded, tile, grad_w, gate_up_landed, local, sends, recvs,
 ):
     k = Links(groups, ranks, sends, recvs)
     rows = hidden.shape[0] // subs
@@ -960,19 +1003,31 @@
     per_tile = BLOCK // depth
     tiles = [(q, g) for q in range(per_group) for g in range(groups)]
 
+    downs = mixed.shape[1] // BLOCK
+
     def load(i):
-        q, g = tiles[i]
+        ref, at = mixed, i - len(tiles)
+        if i < len(tiles):
+            ref, at = normed, tiles[i][1] * per_group + tiles[i][0]
         return pltpu.make_async_copy(
-            normed.at[:, pl.ds((g * per_group + q) * BLOCK, BLOCK)], tile.at[i % 2], local.at[i % 2]
-        )
-
-    whole = pltpu.make_async_copy(grad_gate_up_all, grad_gate_up, local.at[2])
+            ref.at[:, pl.ds(at * BLOCK, BLOCK)], tile.at[i % 2], local.at[i % 2]
+        )
 
     def work(i):
-        q, g = tiles[i]
-        if i + 1 < len(tiles):
+        if i + 1 < len(tiles) + downs:
             load(i + 1).start()
         load(i).wait()
+        if i >= len(tiles):
+            flipped = tile[i % 2].astype(F32).T.astype(BF16)
+            at = (i - len(tiles)) * BLOCK
+
+            @pl.loop(0, grad_down.shape[1] // step)
+            def _(c):
+                part = pl.ds(pl.multiple_of(c * step, step), step)
+                grad_down[at : at + BLOCK, part] = dot(flipped, grad_out_all[:, part]).astype(BF16)
+
+            return
+        q, g = tiles[i]
         flipped = tile[i % 2].astype(F32).T.astype(BF16)
 
         @pl.loop(0, grad_gate_up.shape[1] // step)
@@ -987,7 +1042,6 @@
                 gate_up_sums[q * per_tile + n].start(0)
 
     load(0).start()
-    whole.start()
     k.barrier()
     for sub, scatter in enumerate(scatters):
         scatter.start(lambda rank, sub=sub: parts.at[rank, pl.ds(sub * rows, rows)])
@@ -999,15 +1053,16 @@
         scaled = total * scale
         grad = held[k.z, part].astype(F32)
         sums[...] += jnp.sum(grad * scaled, 0, keepdims=True)
-        grad_total = grad_out[part].astype(F32) + norm_back(grad * gain[...], scaled, scale)
+        grad_total = grad_out[part].astype(F32) + norm_back(grad * gain_rows[1:2, :], scaled, scale)
         grad_hidden[part] = grad_total
         rounded[part] = grad_total.astype(BF16)
 
     own = []
     hops = k.chips - 1
     early = len(tiles) // 4
-    plan = spaced(list(range(early, len(tiles))), hops - 1) + [[]] * (subs * hops + 1)
-    whole.wait()
+    plan = spaced(list(range(early, len(tiles))), hops - 1) + [[]]
+    plan = plan + spaced(list(range(len(tiles), len(tiles) + downs)), subs * hops)
+    traffic.ready(5)
     for place in range(early):
         work(place)
     for turn in range(subs + 1):
@@ -1019,6 +1074,8 @@
             if turn > 0:
                 gathers[turn - 1].step(i + 1)
             for place in plan[turn * hops + i]:
+                if place == len(tiles):
+                    traffic.ready(7)
                 work(place)
             if turn == 1 and i == 0:
                 for sums_of in gate_up_sums[: ranks // 2]:
@@ -1049,7 +1106,7 @@
 
 
 def attend_back_kernel(
-    groups, ranks, rank_heads, slice_width,
+    groups, ranks, rank_heads, slice_width, traffic,
     lengths, out_all, normed, grad_rows, queries, keys, values, attended, log_totals,
     cosine, sine, qkv, gate_up_sum, grad_down, tokens, grad_hidden, gain_rows, sums_two,
     gate_up_grad, down_grad, qkv_grad, out_grad, grad_tokens, gain_grads,
@@ -1147,26 +1204,25 @@
         before.append(scatter.give(chip, core_rows(1 - k.c), later=False))
         return chip, core_rows(k.c)
 
-    def onto(t, chip, mine):
-        scatter.pair(chip, mine)
-        if t + 1 < k.chips:
-            scatter.toward(chip)
-
     load(0).start()
     fetch = k.move(out_all.at[pl.ds(pl.multiple_of(k.f * cols, cols), cols)], out_w)
     k.barrier()
+    traffic.ready(13)
     for sums_of in down_sums:
         sums_of.start(0)
     gate_up_ex.start(lambda rank: gate_up_sum.at[rank], gate_up_in)
     grad_keys[...] = jnp.zeros_like(grad_keys)
     grad_values[...] = jnp.zeros_like(grad_values)
 
+    traffic.ready(5)
+
     @pl.loop(0, blocks)
     def _(i):
         block = pl.ds(pl.multiple_of(i * BLOCK, BLOCK), BLOCK)
         keys_t[i] = keys[block, :].astype(F32).T.astype(BF16)
 
     fetch()
+    traffic.ready()
 
     def back_rows(i):
         attend_back_rows(
@@ -1181,12 +1237,18 @@
     pl.loop(0, blocks)(
         lambda i: finish_back_rows(i, cosine, sine, grad_keys, grad_values, grad_qkv)
     )
-    shares = spaced(list(range(len(work))), k.chips)
+    shares = spaced(list(range(len(work))), 2) + [[]] * k.chips
+    given = None
     for t in range(k.chips):
-        chip, mine = parts_of(t)
+        now = parts_of(t)
+        if given is not None:
+            scatter.pair(*given)
+        given = now
         for i in shares[t]:
             weight_tile(i)
-        onto(t, chip, mine)
+        if t == 1:
+            scatter.step(0)
+    scatter.pair(*given)
 
     out_rows = grad_out_w.shape[1]
     split = groups * out_rows // cols
@@ -1205,9 +1267,15 @@
         sums_of.start(0)
     for stage in range(k.bits - 1):
         onward(qkv_sums, stage)
-        onward(out_sums, stage)
+        if stage == 0:
+            scatter.step(1)
     for n, sums_of in enumerate(qkv_sums):
         exchange.start_piece(n, sums_of.wait(k.bits - 1), qkv_in)
+        if n == ranks // 2 - 1:
+            for i in range(2, k.chips - 1):
+                scatter.step(i)
+    for stage in range(k.bits - 1):
+        onward(out_sums, stage)
     scatter.last()
     sums[...] = jnp.zeros_like(sums)
 
@@ -1264,15 +1332,6 @@
     k.finish()
 
 
-def head_places(ranks, rank_heads, split):
-    places = {}
-    for rank in range(ranks):
-        for b in range(rank_heads):
-            head = (rank % split * rank_heads + b) * (ranks // split) + rank // split
-            places[head] = (rank, b)
-    return [places[head] for head in range(HEADS)]
-
-
 def finish_kernel(
     groups, places, gate_up_grad, qkv_grad, grad_w_gate, grad_w_up, grad_w_query, grad_w_key, grad_w_value
 ):
@@ -1297,16 +1356,62 @@
 VMEM = pl.BlockSpec(memory_space=pltpu.VMEM)
 ANY = pl.BlockSpec(memory_space=pl.ANY)
 SMEM = pl.BlockSpec(memory_space=pltpu.SMEM)
+LOAD, STORE = "load", "store"
+
+
+class Traffic:
+    def __init__(self, ins, outs):
+        self.ins, self.outs, self.begun = ins, outs, []
+        for load in ins.values():
+            load.start()
+
+    def ready(self, *places):
+        for place in places or tuple(self.ins):
+            self.ins.pop(place).wait()
+
+    def put(self, *places):
+        for place in places or tuple(self.outs):
+            store = self.outs.pop(place)
+            store.start()
+            self.begun.append(store)
+
+    def close(self):
+        self.ready()
+        self.put()
+        for store in self.begun:
+            store.wait()
 
 
 def call(kernel, identity, ins, outs, scratch, semaphores, args, local=0):
+    loads = [i for i, place in enumerate(ins) if place == LOAD]
+    stores = [i for i, (_, _, place) in enumerate(outs) if place == STORE]
+
+    def body(*refs):
+        inputs, results = list(refs[: len(ins)]), list(refs[len(ins) : len(ins) + len(outs)])
+        rest = refs[len(ins) + len(outs) :]
+        own = len(scratch) + (local > 0)
+        buffers, moves = rest[own : own + len(loads) + len(stores)], rest[-3]
+        coming, going = {}, {}
+        for n, i in enumerate(loads):
+            coming[i] = pltpu.make_async_copy(inputs[i], buffers[n], moves.at[n])
+            inputs[i] = buffers[n]
+        for n, i in enumerate(stores, len(loads)):
+            going[i] = pltpu.make_async_copy(buffers[n], results[i], moves.at[n])
+            results[i] = buffers[n]
+        traffic = Traffic(coming, going)
+        kernel(traffic, *inputs, *results, *rest[:own], *rest[-2:])
+        traffic.close()
+
     return pl.pallas_call(
-        kernel,
+        body,
         out_shape=[jax.ShapeDtypeStruct(shape, kind) for shape, kind, _ in outs],
-        in_specs=ins,
-        out_specs=[place for _, _, place in outs],
+        in_specs=[ANY if place == LOAD else place for place in ins],
+        out_specs=[ANY if place == STORE else place for _, _, place in outs],
         scratch_shapes=[pltpu.VMEM(shape, kind) for shape, kind in scratch]
         + [pltpu.SemaphoreType.DMA((local,))] * (local > 0)
+        + [pltpu.VMEM(args[i].shape, args[i].dtype) for i in loads]
+        + [pltpu.VMEM(outs[i][0], outs[i][1]) for i in stores]
+        + [pltpu.SemaphoreType.DMA((max(1, len(loads) + len(stores)),))]
         + [pltpu.SemaphoreType.DMA((semaphores,))] * 2,
         compiler_params=pltpu.CompilerParams(
             collective_id=identity, has_side_effects=True, vmem_limit_bytes=61 * 1024 * 1024
@@ -1349,45 +1454,50 @@
         unit_cols = groups * hidden_part
         chips = ranks // 2
         slice_width = norm_attn.shape[0]
-        qkv_out = jnp.concatenate([heads_out(w) for w in (w_query, w_key, w_value)], -1)
-        gate_up_out = jnp.concatenate([units_out(w) for w in (w_gate, w_up)], -1)
+        packed = hidden_part % 128 != 0
+        gate_up_shape = (ranks, depth, 2 * unit_cols)
+        if packed:
+            feeds = (jnp.concatenate([units_out(w) for w in (w_gate, w_up)], -1), w_up)
+        else:
+            feeds = (w_gate, w_up)
         place = (lax.axis_index("dp") * ranks + rank) * slice_width % 128
         gains = lax.dynamic_update_slice(
             jnp.zeros((16, 128), BF16), jnp.stack([norm_attn, norm_mlp]), (0, place)
         )
         cosine, sine = (jnp.asarray(table) for table in wide_tables(count))
         blocks = count // BLOCK
-        heads_shape = ((count, head_cols), BF16, VMEM)
+        heads_shape = ((count, head_cols), BF16, STORE)
         (
             x_all, qkv, gain_rows, normed_one, queries, keys, values, attended, log_totals,
             attended_all, gate_up, out_all, down_w,
         ) = call(
-            functools.partial(attend_kernel, groups, ranks, rank_heads, slice_width),
+            functools.partial(attend_kernel, groups, ranks, rank_heads, slice_width, packed),
             5,
-            [SMEM] + [VMEM] * 8,
+            [SMEM] + [VMEM] * 11,
             [
-                ((count, width), BF16, VMEM),
-                ((groups,) + qkv_out.shape, BF16, VMEM),
+                ((count, width), BF16, STORE),
+                ((groups, ranks, depth, 3 * head_cols), BF16, STORE),
                 ((8, width), F32, VMEM),
-                ((count, width), BF16, VMEM),
+                ((count, width), BF16, STORE),
             ]
             + [heads_shape] * 4
             + [
-                ((blocks, rank_heads, BLOCK), F32, VMEM),
+                ((blocks, rank_heads, BLOCK), F32, STORE),
                 ((count, width), BF16, ANY),
-                ((groups,) + gate_up_out.shape, BF16, ANY),
+                ((groups,) + gate_up_shape, BF16, ANY),
                 ((groups * ranks, out_rows, width), BF16, ANY),
                 ((groups,) + w_down.shape, BF16, ANY),
             ],
             [
                 ((groups, ranks, 16, 128), BF16),
                 ((blocks, head_cols, BLOCK), BF16),
+                ((ranks, depth, 3 * head_cols), BF16),
+                (gate_up_shape, BF16),
             ],
             448,
-            (lengths, tokens, qkv_out, gains, w_output, w_down, gate_up_out, cosine, sine),
+            (lengths, tokens, w_query, w_key, w_value, gains, w_output, w_down) + feeds + (cosine, sine),
         )
         qkv = qkv.reshape(width, -1)
-        gain_one, gain_two = gain_rows[0:1], gain_rows[1:2]
         gate_up = gate_up.reshape(width, -1)
         out_all = out_all.reshape(width, width)
         down_w = down_w.reshape(-1, width)
@@ -1424,27 +1534,26 @@
                 ((count, 2 * unit_cols), F32),
                 ((pair, unit_cols), BF16),
                 ((pair, 2 * unit_cols), BF16),
-                ((pair, width), BF16),
+                ((2, pair, width), BF16),
                 ((pair, width), BF16),
             ]
             + line_scratch[1:],
             128,
-            (attended_all, x_all, out_all, gate_up, down_w, grad_out, gain_two),
+            (attended_all, x_all, out_all, gate_up, down_w, grad_out, gain_rows),
             local=15,
         )
-        grad_down = rows_inner(mixed, grad_out_all.reshape(count, width)).astype(BF16)
-        grad_hidden_all, grad_hidden, sums_two, gate_up_sum = call(
+        grad_hidden_all, grad_hidden, sums_two, gate_up_sum, grad_down = call(
             functools.partial(middle_kernel, groups, ranks, 2),
             3,
-            [ANY] + [VMEM] * 3 + [ANY] * 2,
+            [ANY] + [VMEM] * 3 + [ANY, LOAD, ANY, LOAD],
             [
                 ((ranks, rows, width), BF16, ANY),
                 ((rows, width), F32, VMEM),
                 ((1, width), F32, VMEM),
                 ((ranks, depth, 2 * unit_cols), BF16, VMEM),
+                ((unit_cols, width), BF16, STORE),
             ],
-            [((count, 2 * unit_cols), BF16)]
-            + line_scratch
+            line_scratch
             + [
                 ((rows, width), BF16),
                 ((2, count, BLOCK), BF16),
@@ -1452,8 +1561,17 @@
                 ((ranks, groups - 1, depth, 2 * unit_cols), BF16),
             ],
             160,
-            (parts.reshape(ranks, rows, width), hidden, grad_out, gain_two, normed_two, grad_gate_up),
-            local=3,
+            (
+                parts.reshape(ranks, rows, width),
+                hidden,
+                grad_out,
+                gain_rows,
+                normed_two,
+                grad_gate_up,
+                mixed,
+                grad_out_all.reshape(count, width),
+            ),
+            local=2,
         )
         down_pieces, out_pieces = 4, 2
         out_place = out_rows * split
@@ -1461,7 +1579,7 @@
         grad_gate_up_w, grad_w_down, grad_qkv_w, grad_w_output, grad_tokens, sums = call(
             functools.partial(attend_back_kernel, groups, ranks, rank_heads, slice_width),
             6,
-            [SMEM, ANY, ANY] + [VMEM] * 15,
+            [SMEM, ANY, ANY] + [LOAD] * 9 + [ANY, LOAD] + [VMEM] * 4,
             [
                 ((ranks, depth, 2 * unit_cols), BF16, ANY),
                 ((hidden_part, width), F32, VMEM),

time: 570 us -> 543 us (0.953)
  matrix products: 9.82 us -> 0 us
  local copies, waits for them, and re-layouts: 17.5 us -> 8.11 us
    dot_general x1 -> x0, matrix products: 9.82 us -> none  [rows_inner(): lax.dot_general(left, right, (((0,), (0,)), ((), ())), preferred_element_...]
    reshape x13 -> x0, local copies, waits for them, and re-layouts: 7.42 us -> none  [the longest x6 4.06 us: heads_out(): shaped = weight.reshape(depth, split, rank_heads, ranks // split, HEAD_DIM)]
    pallas_call x4, Pallas kernels: 524 us -> 519 us  [call(): pl.pallas_call(body, out_shape=[jax.ShapeDtypeStruct(shape, kind) for sha...]
where the time goes in v5:
time: 543 us; the launch traced here: 534 us
  Pallas kernels  522 us (96%)
  local copies, waits for them, and re-layouts  8.11 us (1%)
    pallas_call x4, Pallas kernels, call(): pl.pallas_call(body, out_shape=[jax.ShapeDtypeStruct(shape, kind) for sha...  519 us

profile of v5, /device:TPU:0, one launch (start us, length us, event | category | flops | bytes accessed | tf_op | source)
XLA Modules:
  0.0 534.3 jit_solution(1044056947584808216)
XLA Ops:
  1.3 0.7 pad_maximum_fusion
  2.0 0.3 dynamic_update_slice.3.refs_5_
  2.3 0.0 copy-start.6
  2.3 2.0 broadcast_select_fusion.refs_5_.refs_2_
  4.4 0.0 copy-done.6
  4.4 199.7 %shard_map.221 = (bf16[1280,2048]{1,0:T(8,128)(2,1)}, bf16[4,8,64,768]{3,2,1,0:T(8,128)(2,1)}, f32[8,2048]{1,0:T(8,128)}, bf16[1280,2048]{1,0:T(8,128)(2,1)}, bf...) custom-call(s32[1]{0:T(128)} %copy.30.refs_0_, ...), custom_call_target="tpu_custom_call" | custom-call | tf_op jit(solution)/shard_map/pallas_call | solution.py:1405
  204.1 86.8 %shard_map.222 = (bf16[8,160,2048]{2,1,0:T(8,128)(2,1)}, f32[160,2048]{1,0:T(8,128)}, bf16[160,2048]{1,0:T(8,128)(2,1)}, bf16[1280,2048]{1,0:T(8,128)(2,1)}, bf1...) custom-call(bf16[1280,2048]{1,0:T(8,128)(2,1)} %get-tuple-element.47.refs_0_, ...), custom_call_target="tpu_custom_call" | custom-call | tf_op jit(solution)/shard_map/pallas_call | solution.py:1405
  290.9 105.4 %shard_map.223 = (bf16[8,160,2048]{2,1,0:T(8,128)(2,1)}, f32[160,2048]{1,0:T(8,128)}, f32[1,2048]{1,0:T(1,128)}, bf16[8,64,2048]{2,1,0:T(8,128)(2,1)}, bf16[1024,2048]{1,0:T(8,128)(2,1)}) custom-call(bf16[8,160,2048]{2,1,0:T(8,128)(2,1)} %bitcast.21, f32[160,2048]{1,0:T(8,128)} %get-tuple-element.56.refs_1_, ...), custom_call_target="tpu_custom_call" | custom-call | tf_op jit(solution)/shard_map/pallas_call | solution.py:1405
  396.3 0.0 copy-start.3
  396.4 126.6 %shard_map.224 = (bf16[8,64,2048]{2,1,0:T(8,128)(2,1)}, f32[256,2048]{1,0:T(8,128)}, bf16[8,64,768]{2,1,0:T(8,128)(2,1)}, f32[64,2048]{1,0:T(8,128)}, bf16[160,2048]{1,0:T(8,128)(2,1)}, /*index=5*/f32[8,128]{1,0:T(8,128)}) custom-call(s32[1]{0:T(128)} %copy.30.refs_0_, bf16[2048,2048]{1,0:T(8,128)(2,1)} %bitcast.17, ...), custom_call_target="tpu_custom_call" | custom-call | tf_op jit(solution)/shard_map/pallas_call | solution.py:1405
  523.0 0.8 constant_dynamic-slice_fusion
  523.7 0.5 slice_bitcast_fusion
  524.3 0.0 copy-start
  524.3 1.6 copy-done
  525.8 0.0 copy-start.1
  525.9 1.1 copy-done.1
  527.0 0.0 copy-start.4
  527.0 0.0 copy-start.5
  527.0 0.0 copy-start.2
  527.0 3.0 shard_map.225
  530.0 0.0 copy-done.3
  530.0 0.8 copy.31
  530.9 0.0 copy-done.4
  530.9 0.8 copy.32
  531.7 0.0 copy-done.5
  531.7 0.8 copy.33
  532.5 0.0 copy-done.2
  532.5 1.3 copy.34
  (2 shorter events, 0.0 us)
Async XLA Ops:
  2.3 2.1 copy-start.6
  396.3 133.7 %copy-start.3 = (bf16[160,2048]{1,0:T(8,128)(2,1)S(1)}, bf16[160,2048]{1,0:T(8,128)(2,1)}, u32[]{:S(2)}) copy-start(bf16[160,2048]{1,0:T(8,128)(2,1)} %get-tuple-element.96) | copy-start | bytes 1966084
  524.3 1.6 copy-start
  525.8 1.1 copy-start.1
  527.0 3.9 copy-start.4
  527.0 4.7 copy-start.5
  527.0 5.5 %copy-start.2 = (f32[256,2048]{1,0:T(8,128)S(1)}, f32[256,2048]{1,0:T(8,128)}, u32[]{:S(2)}) copy-start(f32[256,2048]{1,0:T(8,128)} %get-tuple-element.106) | copy-start | bytes 6291460

commit v6 on v5

--- a/solution.py
+++ b/solution.py
@@ -801,7 +801,8 @@
     chips, pair = k.chips, hidden_b.shape[0]
     rows = pair // 2
     width, units = out_w.shape[0], down_w.shape[0]
-    step = 512
+    step = 1024
+    chunk = 512
     line = LineGather(k, lambda rank: grad_out_all.at[rank])
     scatter = LineScatter(
         k, None, lambda chip: held.at[chip], lambda slot: landed.at[slot]
@@ -879,10 +880,10 @@
             line.step(t - 1)
         here = span(t)
 
-        @pl.loop(0, units // BLOCK)
+        @pl.loop(0, units // chunk)
         def _(u):
-            part = pl.ds(pl.multiple_of(u * BLOCK, BLOCK), BLOCK)
-            far = pl.ds(pl.multiple_of(units + u * BLOCK, BLOCK), BLOCK)
+            part = pl.ds(pl.multiple_of(u * chunk, chunk), chunk)
+            far = pl.ds(pl.multiple_of(units + u * chunk, chunk), chunk)
             gate = dot(normed_b[...], gate_up[:, part])
             up = dot(normed_b[...], gate_up[:, far])
             gates[here, part] = gate
@@ -932,10 +933,10 @@
             store(2, grad_b, grad_gate_up, near + 1).wait()
         here = span(near)
 
-        @pl.loop(0, units // BLOCK)
+        @pl.loop(0, units // chunk)
         def _(u):
-            part = pl.ds(pl.multiple_of(u * BLOCK, BLOCK), BLOCK)
-            far = pl.ds(pl.multiple_of(units + u * BLOCK, BLOCK), BLOCK)
+            part = pl.ds(pl.multiple_of(u * chunk, chunk), chunk)
+            far = pl.ds(pl.multiple_of(units + u * chunk, chunk), chunk)
             gate, up = gates[here, part], gates[here, far]
             grad_mixed = cols_inner(grad_in[t % 2], down_w[part, :])
             sigmoid = 1.0 / (1.0 + jnp.exp(-gate))
@@ -977,7 +978,7 @@
     k = Links(groups, ranks, sends, recvs)
     rows = hidden.shape[0] // subs
     depth = grad_w.shape[2]
-    step = 512
+    step = 1024
     scatters, gathers = [], []
     for sub in range(subs):
         piece = pl.ds(sub * rows, rows)

time: 543 us -> 537 us (0.989)
  Pallas kernels: 522 us -> 515 us
    pallas_call x4, Pallas kernels: 519 us -> 512 us  [call(): pl.pallas_call(body, out_shape=[jax.ShapeDtypeStruct(shape, kind) for sha...]
where the time goes in v6:
time: 537 us; the launch traced here: 528 us
  Pallas kernels  515 us (96%)
  local copies, waits for them, and re-layouts  8.11 us (2%)
    pallas_call x4, Pallas kernels, call(): pl.pallas_call(body, out_shape=[jax.ShapeDtypeStruct(shape, kind) for sha...  512 us

profile of v6, /device:TPU:0, one launch (start us, length us, event | category | flops | bytes accessed | tf_op | source)
XLA Modules:
  0.0 528.1 jit_solution(4669873607689202040)
XLA Ops:
  1.3 0.7 pad_maximum_fusion
  2.0 0.3 dynamic_update_slice.3.refs_5_
  2.3 0.0 copy-start.6
  2.3 2.0 broadcast_select_fusion.refs_5_.refs_2_
  4.4 0.0 copy-done.6
  4.4 199.7 %shard_map.221 = (bf16[1280,2048]{1,0:T(8,128)(2,1)}, bf16[4,8,64,768]{3,2,1,0:T(8,128)(2,1)}, f32[8,2048]{1,0:T(8,128)}, bf16[1280,2048]{1,0:T(8,128)(2,1)}, bf...) custom-call(s32[1]{0:T(128)} %copy.30.refs_0_, ...), custom_call_target="tpu_custom_call" | custom-call | tf_op jit(solution)/shard_map/pallas_call | solution.py:1406
  204.1 82.1 %shard_map.222 = (bf16[8,160,2048]{2,1,0:T(8,128)(2,1)}, f32[160,2048]{1,0:T(8,128)}, bf16[160,2048]{1,0:T(8,128)(2,1)}, bf16[1280,2048]{1,0:T(8,128)(2,1)}, bf1...) custom-call(bf16[1280,2048]{1,0:T(8,128)(2,1)} %get-tuple-element.47.refs_0_, ...), custom_call_target="tpu_custom_call" | custom-call | tf_op jit(solution)/shard_map/pallas_call | solution.py:1406
  286.2 100.8 %shard_map.223 = (bf16[8,160,2048]{2,1,0:T(8,128)(2,1)}, f32[160,2048]{1,0:T(8,128)}, f32[1,2048]{1,0:T(1,128)}, bf16[8,64,2048]{2,1,0:T(8,128)(2,1)}, bf16[1024,2048]{1,0:T(8,128)(2,1)}) custom-call(bf16[8,160,2048]{2,1,0:T(8,128)(2,1)} %bitcast.21, f32[160,2048]{1,0:T(8,128)} %get-tuple-element.56.refs_1_, ...), custom_call_target="tpu_custom_call" | custom-call | tf_op jit(solution)/shard_map/pallas_call | solution.py:1406
  387.0 0.0 copy-start.3
  387.0 129.8 %shard_map.224 = (bf16[8,64,2048]{2,1,0:T(8,128)(2,1)}, f32[256,2048]{1,0:T(8,128)}, bf16[8,64,768]{2,1,0:T(8,128)(2,1)}, f32[64,2048]{1,0:T(8,128)}, bf16[160,2048]{1,0:T(8,128)(2,1)}, /*index=5*/f32[8,128]{1,0:T(8,128)}) custom-call(s32[1]{0:T(128)} %copy.30.refs_0_, bf16[2048,2048]{1,0:T(8,128)(2,1)} %bitcast.17, ...), custom_call_target="tpu_custom_call" | custom-call | tf_op jit(solution)/shard_map/pallas_call | solution.py:1406
  516.8 0.8 constant_dynamic-slice_fusion
  517.5 0.5 slice_bitcast_fusion
  518.1 0.0 copy-start
  518.1 1.6 copy-done
  519.6 0.0 copy-start.1
  519.6 1.1 copy-done.1
  520.8 0.0 copy-start.4
  520.8 0.0 copy-start.5
  520.8 0.0 copy-start.2
  520.8 3.0 shard_map.225
  523.8 0.0 copy-done.3
  523.8 0.8 copy.31
  524.7 0.0 copy-done.4
  524.7 0.8 copy.32
  525.5 0.0 copy-done.5
  525.5 0.8 copy.33
  526.3 0.0 copy-done.2
  526.3 1.3 copy.34
  (2 shorter events, 0.0 us)
Async XLA Ops:
  2.3 2.1 copy-start.6
  387.0 136.8 %copy-start.3 = (bf16[160,2048]{1,0:T(8,128)(2,1)S(1)}, bf16[160,2048]{1,0:T(8,128)(2,1)}, u32[]{:S(2)}) copy-start(bf16[160,2048]{1,0:T(8,128)(2,1)} %get-tuple-element.96) | copy-start | bytes 1966084
  518.1 1.6 copy-start
  519.6 1.1 copy-start.1
  520.8 3.9 copy-start.4
  520.8 4.7 copy-start.5
  520.8 5.5 %copy-start.2 = (f32[256,2048]{1,0:T(8,128)S(1)}, f32[256,2048]{1,0:T(8,128)}, u32[]{:S(2)}) copy-start(f32[256,2048]{1,0:T(8,128)} %get-tuple-element.106) | copy-start | bytes 6291460

commit v7 on v6

--- a/solution.py
+++ b/solution.py
@@ -694,9 +694,9 @@
                 for n, ref in enumerate((w_gate, w_up)):
                     start = n * units + group * share
                     gate_up_out[rank, :, start : start + share] = ref[:, at : at + share]
+    out_line.start(out_w)
     gains_ex.finish(gains_in)
     qkv_ex.finish(qkv_in)
-    out_line.start(out_w)
     x_line.start(tokens)
     own = [
         k.move(out_w, out_block(k.d, k.f)),
@@ -716,10 +716,10 @@
     out_line.finish()
     for gather in out_gathers:
         gather.start(0)
+    x_line.step(2)
     for q in range(min(2, pieces)):
-        x_line.step(2 + q)
         send_out(q)
-    for reach in range(2 + min(2, pieces), k.chips):
+    for reach in range(3, k.chips):
         x_line.step(reach)
     for stage in range(1, k.bits):
         onward(late, stage)

time: 537 us -> 530 us (0.987)
  Pallas kernels: 515 us -> 508 us
    pallas_call x4, Pallas kernels: 512 us -> 505 us  [call(): pl.pallas_call(body, out_shape=[jax.ShapeDtypeStruct(shape, kind) for sha...]
where the time goes in v7:
time: 530 us; the launch traced here: 521 us
  Pallas kernels  508 us (96%)
  local copies, waits for them, and re-layouts  8.11 us (2%)
    pallas_call x4, Pallas kernels, call(): pl.pallas_call(body, out_shape=[jax.ShapeDtypeStruct(shape, kind) for sha...  505 us

profile of v7, /device:TPU:0, one launch (start us, length us, event | category | flops | bytes accessed | tf_op | source)
XLA Modules:
  0.0 521.1 jit_solution(2919385598216400660)
XLA Ops:
  1.3 0.7 pad_maximum_fusion
  2.0 0.3 dynamic_update_slice.3.refs_5_
  2.3 0.0 copy-start.6
  2.3 2.0 broadcast_select_fusion.refs_5_.refs_2_
  4.4 0.0 copy-done.6
  4.4 198.6 %shard_map.221 = (bf16[1280,2048]{1,0:T(8,128)(2,1)}, bf16[4,8,64,768]{3,2,1,0:T(8,128)(2,1)}, f32[8,2048]{1,0:T(8,128)}, bf16[1280,2048]{1,0:T(8,128)(2,1)}, bf...) custom-call(s32[1]{0:T(128)} %copy.30.refs_0_, ...), custom_call_target="tpu_custom_call" | custom-call | tf_op jit(solution)/shard_map/pallas_call | solution.py:1406
  203.0 80.5 %shard_map.222 = (bf16[8,160,2048]{2,1,0:T(8,128)(2,1)}, f32[160,2048]{1,0:T(8,128)}, bf16[160,2048]{1,0:T(8,128)(2,1)}, bf16[1280,2048]{1,0:T(8,128)(2,1)}, bf1...) custom-call(bf16[1280,2048]{1,0:T(8,128)(2,1)} %get-tuple-element.47.refs_0_, ...), custom_call_target="tpu_custom_call" | custom-call | tf_op jit(solution)/shard_map/pallas_call | solution.py:1406
  283.5 101.4 %shard_map.223 = (bf16[8,160,2048]{2,1,0:T(8,128)(2,1)}, f32[160,2048]{1,0:T(8,128)}, f32[1,2048]{1,0:T(1,128)}, bf16[8,64,2048]{2,1,0:T(8,128)(2,1)}, bf16[1024,2048]{1,0:T(8,128)(2,1)}) custom-call(bf16[8,160,2048]{2,1,0:T(8,128)(2,1)} %bitcast.21, f32[160,2048]{1,0:T(8,128)} %get-tuple-element.56.refs_1_, ...), custom_call_target="tpu_custom_call" | custom-call | tf_op jit(solution)/shard_map/pallas_call | solution.py:1406
  384.9 0.0 copy-start.3
  384.9 124.8 %shard_map.224 = (bf16[8,64,2048]{2,1,0:T(8,128)(2,1)}, f32[256,2048]{1,0:T(8,128)}, bf16[8,64,768]{2,1,0:T(8,128)(2,1)}, f32[64,2048]{1,0:T(8,128)}, bf16[160,2048]{1,0:T(8,128)(2,1)}, /*index=5*/f32[8,128]{1,0:T(8,128)}) custom-call(s32[1]{0:T(128)} %copy.30.refs_0_, bf16[2048,2048]{1,0:T(8,128)(2,1)} %bitcast.17, ...), custom_call_target="tpu_custom_call" | custom-call | tf_op jit(solution)/shard_map/pallas_call | solution.py:1406
  509.8 0.8 constant_dynamic-slice_fusion
  510.5 0.5 slice_bitcast_fusion
  511.1 0.0 copy-start
  511.1 1.6 copy-done
  512.6 0.0 copy-start.1
  512.6 1.1 copy-done.1
  513.8 0.0 copy-start.4
  513.8 0.0 copy-start.5
  513.8 0.0 copy-start.2
  513.8 3.0 shard_map.225
  516.8 0.0 copy-done.3
  516.8 0.8 copy.31
  517.7 0.0 copy-done.4
  517.7 0.8 copy.32
  518.5 0.0 copy-done.5
  518.5 0.8 copy.33
  519.3 0.0 copy-done.2
  519.3 1.3 copy.34
  (2 shorter events, 0.0 us)
Async XLA Ops:
  2.3 2.1 copy-start.6
  384.9 131.9 %copy-start.3 = (bf16[160,2048]{1,0:T(8,128)(2,1)S(1)}, bf16[160,2048]{1,0:T(8,128)(2,1)}, u32[]{:S(2)}) copy-start(bf16[160,2048]{1,0:T(8,128)(2,1)} %get-tuple-element.96) | copy-start | bytes 1966084
  511.1 1.6 copy-start
  512.6 1.1 copy-start.1
  513.8 3.9 copy-start.4
  513.8 4.7 copy-start.5
  513.8 5.5 %copy-start.2 = (f32[256,2048]{1,0:T(8,128)S(1)}, f32[256,2048]{1,0:T(8,128)}, u32[]{:S(2)}) copy-start(f32[256,2048]{1,0:T(8,128)} %get-tuple-element.106) | copy-start | bytes 6291460
